TPU v7x, 32 devices: a whole 2x2x4 slice. The times are simulated.
32 devices in a mesh: ctx: 8 (over y, x, core), ch: 4 (over z).
Axes of the slice: x: 2, y: 2, z: 4, core: 2. Of those that a mesh axis runs over, the one named last changes fastest.
Arguments:
- query_proj: bfloat16 [16384, 4096], P('ctx', 'ch'), may hold values from -6 to 6
- key_proj: bfloat16 [16384, 4096], P('ctx', 'ch'), may hold values from -6 to 6
- value_proj: bfloat16 [16384, 4096], P('ctx', 'ch'), may hold values from -6 to 6
- out_grad: bfloat16 [16384, 4096], P('ctx', 'ch'), may hold values from -6 to 6
- long_filter: bfloat16 [4096, 16384], P(None, ('ch', 'ctx')), as said below
- skip_gain: float32 [4096], P('ch'), may hold values from -4 to 4
Outputs:
- output: bfloat16 [16384, 4096], P('ctx', 'ch')
- query_grad: bfloat16 [16384, 4096], P('ctx', 'ch')
- key_grad: bfloat16 [16384, 4096], P('ctx', 'ch')
- value_grad: bfloat16 [16384, 4096], P('ctx', 'ch')
Inputs may be any that keep to these rules, and one draw needn't show every extreme that they name: `long_filter`: each channel's filter is a rough sequence of taps under an envelope that falls with the tap index.
All inputs are finite; a program needn't handle non-finite values.
Results may differ from a plain program's by a relative error of at most 0.007.
Values may be sent and summed in bfloat16 or wider, within the bound.
No kernel may reach another device: no remote copies, remote signals or barrier semaphores. Data moves between devices by JAX's collectives and lax.ppermute only.
A program may use at most 384 MiB of HBM per device.

v0:
```python
import math

import jax
import jax.numpy as jnp
from jax import lax
from jax.sharding import PartitionSpec as P

FA = 32
FB = 32
FC = 32


highest = lax.Precision.HIGHEST


def angles(rows, cols, period):
    row_index = lax.broadcasted_iota(jnp.int32, (rows, cols), 0)
    col_index = lax.broadcasted_iota(jnp.int32, (rows, cols), 1)
    return 2.0 * math.pi / period * (row_index * col_index % period).astype(jnp.float32)


def angle_pair(phase):
    return (jnp.cos(phase), jnp.sin(phase))


def lead_product(matrix, signal):
    return jnp.einsum("ka,abr->kbr", matrix, signal, precision=highest)


def middle_product(matrix, signal):
    return jnp.einsum("jb,abr->ajr", matrix, signal, precision=highest)


def pointwise(matrix, signal):
    return matrix * signal


def kron_product(matrix, signal):
    return jnp.einsum("abr,rs->abs", signal, matrix, precision=highest)


def split_product(matrix, signal):
    shaped = signal.reshape(signal.shape[0], signal.shape[1], FC, signal.shape[2] // FC)
    return jnp.einsum("abmc,mk->abkc", shaped, matrix, precision=highest).reshape(signal.shape)


def make_toolkit(local_ch):
    points = FA * FB * FC
    trail_width = FC * local_ch
    lead_fwd = angle_pair(angles(FA, FA // 2, FA))
    lead_inv = angle_pair(angles(FA // 2, FA, FA))
    middle = angle_pair(angles(FB, FB, FB))
    outer_k = lax.broadcasted_iota(jnp.int32, (FA, FB, trail_width), 0)
    outer_b = lax.broadcasted_iota(jnp.int32, (FA, FB, trail_width), 1)
    outer_m = lax.broadcasted_iota(jnp.int32, (FA, FB, trail_width), 2) // local_ch
    outer = angle_pair(
        2.0 * math.pi / points * ((outer_b * FC + outer_m) * outer_k % points).astype(jnp.float32)
    )
    inner_k = lax.broadcasted_iota(jnp.int32, (FB, trail_width), 0)
    inner_m = lax.broadcasted_iota(jnp.int32, (FB, trail_width), 1) // local_ch
    inner = angle_pair(
        2.0 * math.pi / (FB * FC) * (inner_m * inner_k % (FB * FC)).astype(jnp.float32)
    )
    if trail_width <= 512:
        row_index = lax.broadcasted_iota(jnp.int32, (trail_width, trail_width), 0)
        col_index = lax.broadcasted_iota(jnp.int32, (trail_width, trail_width), 1)
        same_channel = (row_index % local_ch == col_index % local_ch).astype(jnp.float32)
        phase = (
            2.0
            * math.pi
            / FC
            * (row_index // local_ch * (col_index // local_ch) % FC).astype(jnp.float32)
        )
        trail = (jnp.cos(phase) * same_channel, jnp.sin(phase) * same_channel)
        trail_op = kron_product
    else:
        trail = angle_pair(angles(FC, FC, FC))
        trail_op = split_product
    return (lead_fwd, lead_inv, middle, outer, inner, trail, trail_op)


def rotate(real_part, imag_part, pair, orient, product):
    cosine, sine = pair
    if imag_part is None:
        return (product(cosine, real_part), orient * product(sine, real_part))
    new_real = product(cosine, real_part) - orient * product(sine, imag_part)
    new_imag = product(cosine, imag_part) + orient * product(sine, real_part)
    return (new_real, new_imag)


def transform(toolkit, real_part, imag_part):
    lead_fwd, lead_inv, middle, outer, inner, trail, trail_op = toolkit
    real_part, imag_part = rotate(real_part, imag_part, lead_fwd, -1.0, lead_product)
    real_part, imag_part = rotate(real_part, imag_part, outer, -1.0, pointwise)
    real_part, imag_part = rotate(real_part, imag_part, middle, -1.0, middle_product)
    real_part, imag_part = rotate(real_part, imag_part, inner, -1.0, pointwise)
    return rotate(real_part, imag_part, trail, -1.0, trail_op)


def inverse(toolkit, real_part, imag_part):
    lead_fwd, lead_inv, middle, outer, inner, trail, trail_op = toolkit
    real_part, imag_part = rotate(real_part, imag_part, trail, 1.0, trail_op)
    real_part, imag_part = rotate(real_part, imag_part, inner, 1.0, pointwise)
    real_part, imag_part = rotate(real_part, imag_part, middle, 1.0, middle_product)
    real_part, imag_part = rotate(real_part, imag_part, outer, 1.0, pointwise)
    real_part, imag_part = rotate(real_part, imag_part, lead_inv, 1.0, lead_product)
    factor = 1.0 / (FA * FB * FC)
    return (real_part * factor, imag_part * factor)


def convolve_pair(toolkit, filter_spec, gated_ch, grad_ch):
    tokens, local_ch = gated_ch.shape
    grid_shape = (FA // 2, FB, FC * local_ch)
    signal_real = gated_ch.astype(jnp.float32).reshape(grid_shape)
    signal_imag = jnp.flip(grad_ch, 0).astype(jnp.float32).reshape(grid_shape)
    spec_real, spec_imag = transform(toolkit, signal_real, signal_imag)
    filt_real, filt_imag = filter_spec
    prod_real = spec_real * filt_real - spec_imag * filt_imag
    prod_imag = spec_real * filt_imag + spec_imag * filt_real
    back_real, back_imag = inverse(toolkit, prod_real, prod_imag)
    convolved = back_real.reshape(tokens, local_ch).astype(jnp.bfloat16)
    reflected = jnp.flip(back_imag.reshape(tokens, local_ch), 0).astype(jnp.bfloat16)
    return (convolved, reflected)


def finish_tokens(
    query_proj, key_proj, value_proj, out_grad, skip_gain, gated_kv, grad_gate, convolved, reflected
):
    summed = convolved.astype(jnp.float32) + skip_gain[None, :] * gated_kv.astype(jnp.float32)
    output = (query_proj.astype(jnp.float32) * summed).astype(jnp.bfloat16)
    query_grad = (out_grad.astype(jnp.float32) * summed).astype(jnp.bfloat16)
    grad_sum = reflected.astype(jnp.float32) + skip_gain[None, :] * grad_gate.astype(jnp.float32)
    key_grad = (grad_sum * value_proj.astype(jnp.float32)).astype(jnp.bfloat16)
    value_grad = (grad_sum * key_proj.astype(jnp.float32)).astype(jnp.bfloat16)
    return (output, query_grad, key_grad, value_grad)


def shards(query_proj, key_proj, value_proj, out_grad, long_filter, skip_gain):
    groups = lax.axis_size("ctx")
    tensor_groups = lax.axis_size("ch")
    channels, tap_cols = long_filter.shape
    local_ch = channels // (groups * tensor_groups)
    reordered = (
        long_filter.reshape(tensor_groups, groups, local_ch, tap_cols)
        .transpose(1, 0, 2, 3)
        .reshape(channels, tap_cols)
    )
    filter_rows = lax.all_to_all(
        lax.all_to_all(reordered, "ctx", split_axis=0, concat_axis=1, tiled=True),
        "ch",
        split_axis=0,
        concat_axis=1,
        tiled=True,
    )
    toolkit = make_toolkit(local_ch)
    filter_grid = filter_rows.T.astype(jnp.float32).reshape(FA // 2, FB, FC * local_ch)
    filter_spec = transform(toolkit, filter_grid, None)
    gated_kv = (key_proj.astype(jnp.float32) * value_proj.astype(jnp.float32)).astype(jnp.bfloat16)
    grad_gate = (out_grad.astype(jnp.float32) * query_proj.astype(jnp.float32)).astype(jnp.bfloat16)
    gated_ch = lax.all_to_all(gated_kv, "ctx", split_axis=1, concat_axis=0, tiled=True)
    grad_ch = lax.all_to_all(grad_gate, "ctx", split_axis=1, concat_axis=0, tiled=True)
    conv_ch, refl_ch = convolve_pair(toolkit, filter_spec, gated_ch, grad_ch)
    convolved = lax.all_to_all(conv_ch, "ctx", split_axis=0, concat_axis=1, tiled=True)
    reflected = lax.all_to_all(refl_ch, "ctx", split_axis=0, concat_axis=1, tiled=True)
    return finish_tokens(
        query_proj,
        key_proj,
        value_proj,
        out_grad,
        skip_gain,
        gated_kv,
        grad_gate,
        convolved,
        reflected,
    )


def solution(mesh):
    placed = (
        P("ctx", "ch"),
        P("ctx", "ch"),
        P("ctx", "ch"),
        P("ctx", "ch"),
        P(None, ("ch", "ctx")),
        P("ch"),
    )
    return jax.shard_map(
        shards,
        mesh=mesh,
        in_specs=placed,
        out_specs=(P("ctx", "ch"), P("ctx", "ch"), P("ctx", "ch"), P("ctx", "ch")),
        check_vma=False,
    )
```

profile of v0, /device:TPU:0, one launch (start us, length us, event | category | flops | bytes accessed | tf_op | source)
XLA Modules:
  0.0 1755.0 jit_solution(13154514714627541441)
XLA Ops:
  70.6 42.7 %all-to-all-done.1 = bf16[2048,8,128]{0,2,1:T(8,128)(2,1)} async-done(((bf16[2048,8,128]{0,2,1:T(8,128)(2,1)}), bf16[2048,8,128]{0,2,1:T(8,128)(2,1)}, u32[]{:S(2)}, u32[]{:S(2)}) %all-to-all-start.1) | async-done | bytes 4194336 | tf_op jit(solution)/shard_map/all_to_all | solution.py:161
  131.8 35.2 %all-to-all-done = bf16[2048,8,128]{2,0,1:T(8,128)(2,1)} async-done(((bf16[2048,8,128]{2,0,1:T(8,128)(2,1)}), bf16[2048,8,128]{2,0,1:T(8,128)(2,1)}, u32[]{:S(2)}, u32[]{:S(2)}) %all-to-all-start) | async-done | bytes 4194336 | tf_op jit(solution)/shard_map/all_to_all | solution.py:160
  182.4 59.4 %rev.8 = bf16[16384,128]{1,0:T(8,128)(2,1)} reverse(bf16[16384,128]{1,0:T(8,128)(2,1)} %bitcast.243), dimensions={0} | reverse | bytes 8388608 | tf_op jit(solution)/shard_map/jit(_flip)/rev | solution.py:115
  334.3 89.4 %multiply_subtract_fusion.3 = (f32[32,32,4096]{2,0,1:T(8,128)}, f32[32,32,4096]{2,0,1:T(8,128)}, f32[32,32,4096]{2,0,1:T(8,128)}, f32[32,32,4096]{2,0,1:T(8,128)}) fusion(f32[32,32,4096]{2,0,1:T(8,128)S(1)} %fusion.81, s32[4096]{0:T(1024)S(1)} %get-tuple-element.34, s32[4096]{0:T(1024)S(1)} %get-tuple-element.35, pred[4096]{0:T(1024)(128)(4,1)S(1)} %fusion.128, ...), kind=kOutput, calls=%fused_computation.56 | convolution fusion | flops 943725568 | bytes 121671808 | tf_op jit(solution)/shard_map/ka,abr->kbr/dot_general | solution.py:27
  423.7 41.9 %fusion.41 = f32[32,4096,32]{1,2,0:T(8,128)} fusion(f32[32,32,4096]{2,0,1:T(8,128)} %get-tuple-element.18), kind=kOutput, calls=%fused_computation.82 | convolution fusion | flops 1610627072 | bytes 33554432 | tf_op jit(solution)/shard_map/jb,abr->ajr/dot_general | solution.py:31
  465.6 41.4 %fusion.43 = f32[32,4096,32]{1,2,0:T(8,128)} fusion(f32[32,32,4096]{2,0,1:T(8,128)} %get-tuple-element.18), kind=kOutput, calls=%fused_computation.84 | convolution fusion | flops 1610627072 | bytes 33554432 | tf_op jit(solution)/shard_map/jb,abr->ajr/dot_general | solution.py:31
  507.0 41.5 %fusion.37 = f32[32,4096,32]{1,2,0:T(8,128)} fusion(f32[32,32,4096]{2,0,1:T(8,128)} %get-tuple-element.19), kind=kOutput, calls=%fused_computation.78 | convolution fusion | flops 1610627072 | bytes 33554432 | tf_op jit(solution)/shard_map/jb,abr->ajr/dot_general | solution.py:31
  548.5 41.9 %fusion.39 = f32[32,4096,32]{1,2,0:T(8,128)} fusion(f32[32,32,4096]{2,0,1:T(8,128)} %get-tuple-element.19), kind=kOutput, calls=%fused_computation.80 | convolution fusion | flops 1610627072 | bytes 33554432 | tf_op jit(solution)/shard_map/jb,abr->ajr/dot_general | solution.py:31
  590.4 41.4 %fusion.53 = f32[32,4096,32]{1,2,0:T(8,128)} fusion(f32[32,32,4096]{2,0,1:T(8,128)} %get-tuple-element.28), kind=kOutput, calls=%fused_computation.94 | convolution fusion | flops 1610627072 | bytes 33554432 | tf_op jit(solution)/shard_map/jb,abr->ajr/dot_general | solution.py:31
  631.8 41.7 %fusion.55 = f32[32,4096,32]{1,2,0:T(8,128)} fusion(f32[32,32,4096]{2,0,1:T(8,128)} %get-tuple-element.28), kind=kOutput, calls=%fused_computation.96 | convolution fusion | flops 1610627072 | bytes 33554432 | tf_op jit(solution)/shard_map/jb,abr->ajr/dot_general | solution.py:31
  673.4 41.9 %fusion.57 = f32[32,4096,32]{1,2,0:T(8,128)} fusion(f32[32,32,4096]{2,0,1:T(8,128)} %get-tuple-element.29), kind=kOutput, calls=%fused_computation.98 | convolution fusion | flops 1610627072 | bytes 33554432 | tf_op jit(solution)/shard_map/jb,abr->ajr/dot_general | solution.py:31
  715.3 41.4 %fusion.59 = f32[32,4096,32]{1,2,0:T(8,128)} fusion(f32[32,32,4096]{2,0,1:T(8,128)} %get-tuple-element.29), kind=kOutput, calls=%fused_computation.100 | convolution fusion | flops 1610627072 | bytes 33554432 | tf_op jit(solution)/shard_map/jb,abr->ajr/dot_general | solution.py:31
  756.8 132.5 %fusion.14 = (f32[32,32,4096]{2,0,1:T(8,128)}, f32[32,32,4096]{2,0,1:T(8,128)}, f32[32,32,4096]{2,0,1:T(8,128)}, f32[32,32,4096]{2,0,1:T(8,128)}) fusion(f32[32,4096]{1,0:T(8,128)S(1)} %copy-done.6, f32[32,4096]{1,0:T(8,128)S(1)} %copy-done.4, f32[32,4096,32]{1,2,0:T(8,128)} %fusion.39, f32[32,4096,32]{1,2,0:T(8,128)} %fusion.43, ...), kind=kLoop, calls=%fused_computation.23 | loop fusion | flops 100663296 | bytes 202375168 | tf_op jit(solution)/shard_map/sub | solution.py:86
  981.0 20.1 %multiply_subtract_fusion.2 = f32[32,32,32,128]{3,0,2,1:T(8,128)} fusion(f32[32,32,32,128]{3,0,2,1:T(8,128)} %fusion.31, f32[32,32,32,128]{3,2,0,1:T(8,128)S(1)} %bitcast.227), kind=kOutput, calls=%fused_computation.54 | convolution fusion | flops 1619015680 | bytes 50331648 | tf_op jit(solution)/shard_map/abmc,mk->abkc/dot_general | solution.py:44
  1001.1 19.9 %multiply_add_fusion.2 = f32[32,32,32,128]{3,0,2,1:T(8,128)} fusion(f32[32,32,32,128]{3,0,2,1:T(8,128)} %fusion.29, f32[32,32,32,128]{3,2,0,1:T(8,128)S(1)} %bitcast.228), kind=kOutput, calls=%fused_computation.52 | convolution fusion | flops 1619015680 | bytes 50331648 | tf_op jit(solution)/shard_map/abmc,mk->abkc/dot_general | solution.py:44
  1036.3 20.1 %multiply_subtract_fusion.4 = f32[32,32,32,128]{3,0,2,1:T(8,128)} fusion(f32[32,32,32,128]{3,0,2,1:T(8,128)} %fusion.47, f32[32,32,32,128]{3,2,0,1:T(8,128)S(1)} %bitcast.225), kind=kOutput, calls=%fused_computation.57 | convolution fusion | flops 1619015680 | bytes 50331648 | tf_op jit(solution)/shard_map/abmc,mk->abkc/dot_general | solution.py:44
  1056.4 40.1 %multiply_subtract_fusion.1 = (f32[32,32,32,128]{3,0,2,1:T(8,128)}, f32[32,32,32,128]{3,0,2,1:T(8,128)}) fusion(f32[32,32,32,128]{3,0,2,1:T(8,128)} %multiply_add_fusion.2, f32[32,32,32,128]{3,0,2,1:T(8,128)} %multiply_subtract_fusion.4, f32[32,32,32,128]{3,0,2,1:T(8,128)} %multiply_subtract_fusion.2, f32[32,32,32,128]{3,0,2,1:T(8,128)} %fusion.45, ...), kind=kOutput, calls=%fused_computation.51 | convolution fusion | flops 1644181504 | bytes 117440512 | tf_op jit(solution)/shard_map/abmc,mk->abkc/dot_general | solution.py:44
  1096.5 19.4 %fusion.5 = f32[32,32,32,128]{3,0,2,1:T(8,128)} fusion(f32[32,32,32,128]{3,0,2,1:T(8,128)} %get-tuple-element.15), kind=kOutput, calls=%fused_computation.12 | convolution fusion | flops 1610627072 | bytes 33554432 | tf_op jit(solution)/shard_map/abmc,mk->abkc/dot_general | solution.py:44
  1116.0 19.9 %fusion.7 = f32[32,32,32,128]{3,0,2,1:T(8,128)} fusion(f32[32,32,32,128]{3,0,2,1:T(8,128)} %get-tuple-element.15), kind=kOutput, calls=%fused_computation.14 | convolution fusion | flops 1610627072 | bytes 33554432 | tf_op jit(solution)/shard_map/abmc,mk->abkc/dot_general | solution.py:44
  1135.9 19.4 %subtract_bitcast_fusion = f32[32,32,32,128]{3,2,1,0:T(8,128)} fusion(f32[32,32,32,128]{3,0,2,1:T(8,128)} %fusion.7, f32[32,32,32,128]{3,0,2,1:T(8,128)S(1)} %bitcast.224), kind=kOutput, calls=%fused_computation.49 | convolution fusion | flops 1614821376 | bytes 50331648 | tf_op jit(solution)/shard_map/abmc,mk->abkc/dot_general | solution.py:44
  1155.3 19.3 %add_bitcast_fusion = f32[32,32,32,128]{3,2,1,0:T(8,128)} fusion(f32[32,32,32,128]{3,0,2,1:T(8,128)} %fusion.5, f32[32,32,32,128]{3,0,2,1:T(8,128)S(1)} %bitcast.224), kind=kOutput, calls=%fused_computation.48 | convolution fusion | flops 1614821376 | bytes 50331648 | tf_op jit(solution)/shard_map/abmc,mk->abkc/dot_general | solution.py:44
  1174.6 18.2 %reshape.227 = f32[32,32,4096]{2,1,0:T(8,128)} reshape(f32[32,32,32,128]{3,2,1,0:T(8,128)} %add_bitcast_fusion) | data formatting | bytes 33554432 | tf_op jit(solution)/shard_map/add | solution.py:87
  1192.8 18.4 %reshape.226 = f32[32,32,4096]{2,1,0:T(8,128)} reshape(f32[32,32,32,128]{3,2,1,0:T(8,128)} %subtract_bitcast_fusion) | data formatting | bytes 33554432 | tf_op jit(solution)/shard_map/sub | solution.py:86
  1211.2 34.8 %multiply_subtract_fusion = (f32[32,32,4096]{2,0,1:T(8,128)}, f32[32,32,4096]{2,0,1:T(8,128)}) fusion(f32[32,32,4096]{2,1,0:T(8,128)} %reshape.227, f32[32,32,4096]{2,1,0:T(8,128)} %reshape.226, f32[32,4096]{1,0:T(8,128)S(1)} %copy-done.7, f32[32,4096]{1,0:T(8,128)S(1)} %copy-done.5), kind=kLoop, calls=%fused_computation.47 | loop fusion | flops 25165824 | bytes 68157440 | tf_op jit(solution)/shard_map/sub | solution.py:86
  1246.0 41.9 %fusion.25 = f32[32,4096,32]{1,2,0:T(8,128)} fusion(f32[32,32,4096]{2,0,1:T(8,128)} %get-tuple-element.16), kind=kOutput, calls=%fused_computation.66 | convolution fusion | flops 1610627072 | bytes 33554432 | tf_op jit(solution)/shard_map/jb,abr->ajr/dot_general | solution.py:31
  1288.0 41.4 %fusion.27 = f32[32,4096,32]{1,2,0:T(8,128)} fusion(f32[32,32,4096]{2,0,1:T(8,128)} %get-tuple-element.16), kind=kOutput, calls=%fused_computation.68 | convolution fusion | flops 1610627072 | bytes 33554432 | tf_op jit(solution)/shard_map/jb,abr->ajr/dot_general | solution.py:31
  1329.4 41.5 %fusion.21 = f32[32,4096,32]{1,2,0:T(8,128)} fusion(f32[32,32,4096]{2,0,1:T(8,128)} %get-tuple-element.17), kind=kOutput, calls=%fused_computation.62 | convolution fusion | flops 1610627072 | bytes 33554432 | tf_op jit(solution)/shard_map/jb,abr->ajr/dot_general | solution.py:31
  1370.9 41.9 %fusion.23 = f32[32,4096,32]{1,2,0:T(8,128)} fusion(f32[32,32,4096]{2,0,1:T(8,128)} %get-tuple-element.17), kind=kOutput, calls=%fused_computation.64 | convolution fusion | flops 1610627072 | bytes 33554432 | tf_op jit(solution)/shard_map/jb,abr->ajr/dot_general | solution.py:31
  1412.9 90.4 %fusion.4 = (f32[32,32,4096]{2,0,1:T(8,128)}, f32[32,32,4096]{2,0,1:T(8,128)}) fusion(s32[4096]{0:T(1024)S(1)} %copy-done.9, s32[4096]{0:T(1024)S(1)} %copy-done.11, pred[4096]{0:T(1024)(128)(4,1)S(1)} %copy-done.13, s32[32]{0:T(128)S(1)} %copy-done.16, f32[32,4096,32]{1,2,0:T(8,128)} %fusion.23, f32[32,4096,32]{1,2,0:T(8,128)} %fusion.27, ...), kind=kLoop, calls=%fused_computation.9 | loop fusion | flops 100663296 | bytes 100700288 | tf_op jit(solution)/shard_map/add | solution.py:87
  1577.9 59.3 %rev.9 = bf16[16384,128]{1,0:T(8,128)(2,1)} reverse(bf16[16384,128]{1,0:T(8,128)(2,1)} %reshape.205), dimensions={0} | reverse | bytes 8388608 | tf_op jit(solution)/shard_map/jit(_flip)/rev | solution.py:122
  1657.2 34.0 %all-to-all-done.5 = bf16[8,2048,128]{2,1,0:T(8,128)(2,1)} async-done(((bf16[8,2048,128]{2,1,0:T(8,128)(2,1)}), bf16[8,2048,128]{2,1,0:T(8,128)(2,1)}, u32[]{:S(2)}, u32[]{:S(2)}) %all-to-all-start.5) | async-done | bytes 4194336 | tf_op jit(solution)/shard_map/all_to_all | solution.py:164
  1706.3 22.7 %fusion.76 = (bf16[2048,1024]{0,1:T(8,128)(2,1)}, bf16[2048,1024]{0,1:T(8,128)(2,1)}, bf16[2048,1024]{0,1:T(8,128)(2,1)}, bf16[2048,1024]{0,1:T(8,128)(2,1)}) fusion(bf16[2048,1024]{0,1:T(8,128)(2,1)} %copy.114, bf16[2048,1024]{0,1:T(8,128)(2,1)} %get-tuple-element.37, f32[2048,8,128]{0,2,1:T(8,128)} %copy.177, f32[1024]{0:T(1024)S(1)} %copy-done.14, ...), kind=kLoop, calls=%fused_computation.111 | loop fusion | flops 37748736 | bytes 58724352 | tf_op jit(solution)/shard_map/convert_element_type | solution.py:134
  (108 shorter events, 438.5 us)
Async XLA Ops:
  5.2 54.4 %all-to-all-start.2 = ((bf16[8,512,512]{2,1,0:T(8,128)(2,1)}), bf16[8,512,512]{2,1,0:T(8,128)(2,1)}, u32[]{:S(2)}, u32[]{:S(2)}) async-start(bf16[8,512,512]{2,1,0:T(8,128)(2,1)} %bitcast.242), calls=%async_computation.2 | async-start | bytes 8388608 | tf_op jit(solution)/shard_map/all_to_all | solution.py:149
  59.6 53.7 %all-to-all-start.1 = ((bf16[2048,8,128]{0,2,1:T(8,128)(2,1)}), bf16[2048,8,128]{0,2,1:T(8,128)(2,1)}, u32[]{:S(2)}, u32[]{:S(2)}) async-start(bf16[2048,8,128]{0,2,1:T(8,128)(2,1)} %bitcast.240), calls=%async_computation.1 | async-start | bytes 8388608 | tf_op jit(solution)/shard_map/all_to_all | solution.py:161
  113.3 53.7 %all-to-all-start = ((bf16[2048,8,128]{2,0,1:T(8,128)(2,1)}), bf16[2048,8,128]{2,0,1:T(8,128)(2,1)}, u32[]{:S(2)}, u32[]{:S(2)}) async-start(bf16[2048,8,128]{2,0,1:T(8,128)(2,1)} %copy.116), calls=%async_computation | async-start | bytes 8388608 | tf_op jit(solution)/shard_map/all_to_all | solution.py:160
  167.0 144.0 %all-to-all-start.3 = ((bf16[4,128,4096]{2,1,0:T(8,128)(2,1)}), bf16[4,128,4096]{2,1,0:T(8,128)(2,1)}, u32[]{:S(2)}, u32[]{:S(2)}) async-start(bf16[4,128,4096]{2,1,0:T(8,128)(2,1)} %all_to_all.80), calls=%async_computation.3 | async-start | bytes 8388608 | tf_op jit(solution)/shard_map/all_to_all | solution.py:148
  172.8 161.4 %copy-start.15 = (s32[32]{0:T(128)}, s32[32]{0:T(128)S(1)}, u32[]{:S(2)}) copy-start(s32[32]{0:T(128)S(1)} %iota_multiply_fusion) | copy-start | bytes 388
  172.9 161.4 %copy-start.12 = (pred[4096]{0:T(1024)(128)(4,1)}, pred[4096]{0:T(1024)(128)(4,1)S(1)}, u32[]{:S(2)}) copy-start(pred[4096]{0:T(1024)(128)(4,1)S(1)} %fusion.128) | copy-start | bytes 12292
  172.9 161.4 %copy-start.8 = (s32[4096]{0:T(1024)}, s32[4096]{0:T(1024)S(1)}, u32[]{:S(2)}) copy-start(s32[4096]{0:T(1024)S(1)} %get-tuple-element.34) | copy-start | bytes 49156
  172.9 161.4 %copy-start.10 = (s32[4096]{0:T(1024)}, s32[4096]{0:T(1024)S(1)}, u32[]{:S(2)}) copy-start(s32[4096]{0:T(1024)S(1)} %get-tuple-element.35) | copy-start | bytes 49156
  256.4 12.7 copy-start.2
  279.2 16.0 copy-start.1
  324.6 9.7 copy-start.3
  715.3 41.5 %copy-start.4 = (f32[32,4096]{1,0:T(8,128)S(1)}, f32[32,4096]{1,0:T(8,128)}, u32[]{:S(2)}) copy-start(f32[32,4096]{1,0:T(8,128)} %get-tuple-element.30) | copy-start | bytes 1572868
  715.3 41.5 %copy-start.6 = (f32[32,4096]{1,0:T(8,128)S(1)}, f32[32,4096]{1,0:T(8,128)}, u32[]{:S(2)}) copy-start(f32[32,4096]{1,0:T(8,128)} %get-tuple-element.31) | copy-start | bytes 1572868
  898.7 34.4 %slice-start.4 = ((s8[16777216]{0:T(1024)(128)(4,1)}), s8[4194304]{0:T(1024)(128)(4,1)S(1)}, s32[]{:S(2)}) async-start(s8[16777216]{0:T(1024)(128)(4,1)} %bitcast.235), calls=%async_computation.10 | async-start | bytes 8388608
  898.7 34.4 %slice-start.5 = ((s8[16777216]{0:T(1024)(128)(4,1)}), s8[4194304]{0:T(1024)(128)(4,1)S(1)}, s32[]{:S(2)}) async-start(s8[16777216]{0:T(1024)(128)(4,1)} %bitcast.235), calls=%async_computation.11 | async-start | bytes 8388608
  915.9 17.2 slice-start.6
  915.9 17.2 slice-start.7
  1030.5 5.8 copy-start
  1096.5 39.4 %slice-start = ((s8[16777216]{0:T(1024)(128)(4,1)}), s8[4194304]{0:T(1024)(128)(4,1)S(1)}, s32[]{:S(2)}) async-start(s8[16777216]{0:T(1024)(128)(4,1)} %bitcast.223), calls=%async_computation.6 | async-start | bytes 8388608
  1096.5 39.4 %slice-start.1 = ((s8[16777216]{0:T(1024)(128)(4,1)}), s8[4194304]{0:T(1024)(128)(4,1)S(1)}, s32[]{:S(2)}) async-start(s8[16777216]{0:T(1024)(128)(4,1)} %bitcast.223), calls=%async_computation.7 | async-start | bytes 8388608
  1116.0 19.9 %slice-start.2 = ((s8[16777216]{0:T(1024)(128)(4,1)}), s8[4194304]{0:T(1024)(128)(4,1)S(1)}, s32[]{:S(2)}) async-start(s8[16777216]{0:T(1024)(128)(4,1)} %bitcast.223), calls=%async_computation.8 | async-start | bytes 8388608
  1116.0 19.9 %slice-start.3 = ((s8[16777216]{0:T(1024)(128)(4,1)}), s8[4194304]{0:T(1024)(128)(4,1)S(1)}, s32[]{:S(2)}) async-start(s8[16777216]{0:T(1024)(128)(4,1)} %bitcast.223), calls=%async_computation.9 | async-start | bytes 8388608
  1192.8 18.5 %copy-start.5 = (f32[32,4096]{1,0:T(8,128)S(1)}, f32[32,4096]{1,0:T(8,128)}, u32[]{:S(2)}) copy-start(f32[32,4096]{1,0:T(8,128)} %get-tuple-element.30) | copy-start | bytes 1572868
  1192.8 18.5 %copy-start.7 = (f32[32,4096]{1,0:T(8,128)S(1)}, f32[32,4096]{1,0:T(8,128)}, u32[]{:S(2)}) copy-start(f32[32,4096]{1,0:T(8,128)} %get-tuple-element.31) | copy-start | bytes 1572868
  1370.9 41.9 %copy-start.9 = (s32[4096]{0:T(1024)S(1)}, s32[4096]{0:T(1024)}, u32[]{:S(2)}) copy-start(s32[4096]{0:T(1024)} %copy-done.8) | copy-start | bytes 49156
  1370.9 41.9 %copy-start.11 = (s32[4096]{0:T(1024)S(1)}, s32[4096]{0:T(1024)}, u32[]{:S(2)}) copy-start(s32[4096]{0:T(1024)} %copy-done.10) | copy-start | bytes 49156
  1370.9 41.9 %copy-start.13 = (pred[4096]{0:T(1024)(128)(4,1)S(1)}, pred[4096]{0:T(1024)(128)(4,1)}, u32[]{:S(2)}) copy-start(pred[4096]{0:T(1024)(128)(4,1)} %copy-done.12) | copy-start | bytes 12292
  1370.9 41.9 %copy-start.16 = (s32[32]{0:T(128)S(1)}, s32[32]{0:T(128)}, u32[]{:S(2)}) copy-start(s32[32]{0:T(128)} %copy-done.15) | copy-start | bytes 388
  1538.4 98.8 %all-to-all-start.4 = ((bf16[8,2048,128]{2,1,0:T(8,128)(2,1)}), bf16[8,2048,128]{2,1,0:T(8,128)(2,1)}, u32[]{:S(2)}, u32[]{:S(2)}) async-start(bf16[8,2048,128]{2,1,0:T(8,128)(2,1)} %convert_element_type.212), calls=%async_computation.4 | async-start | bytes 8388608 | tf_op jit(solution)/shard_map/all_to_all | solution.py:163
  1637.2 54.0 %all-to-all-start.5 = ((bf16[8,2048,128]{2,1,0:T(8,128)(2,1)}), bf16[8,2048,128]{2,1,0:T(8,128)(2,1)}, u32[]{:S(2)}, u32[]{:S(2)}) async-start(bf16[8,2048,128]{2,1,0:T(8,128)(2,1)} %bitcast.241), calls=%async_computation.5 | async-start | bytes 8388608 | tf_op jit(solution)/shard_map/all_to_all | solution.py:164
  1657.2 49.1 %copy-start.14 = (f32[1024]{0:T(1024)S(1)}, f32[1024]{0:T(1024)}, u32[]{:S(2)}) copy-start(f32[1024]{0:T(1024)} %param.11) | copy-start | bytes 12292
where the time goes:
time: 1780 us; the launch traced here: 1760 us
  matrix products  948 us (53%)
  local copies, waits for them, and re-layouts  346 us (19%)
  other arithmetic  306 us (17%)
  waiting for transfers between devices  125 us (7%)
  starting transfers between devices  29.5 us (2%)
    dot_general x12, matrix products, middle_product(): return jnp.einsum('jb,abr->ajr', matrix, signal, precision=highest)  500 us
    dot_general x12, matrix products, split_product(): jnp.einsum('abmc,mk->abkc', shaped, matrix, precision=highest)  248 us
    dot_general x10, matrix products, lead_product(): return jnp.einsum('ka,abr->kbr', matrix, signal, precision=highest)  200 us
    sub x2, other arithmetic, rotate(): new_real = product(cosine, real_part) - orient * product(sine, imag_part)  167 us
    add x1, other arithmetic, rotate(): new_imag = product(cosine, imag_part) + orient * product(sine, real_part)  90.4 us
    unnamed x62, local copies, waits for them, and re-layouts  89 us
    rev x1, local copies, waits for them, and re-layouts, convolve_pair(): signal_imag = jnp.flip(grad_ch, 0).astype(jnp.float32).reshape(grid_shape)  59.4 us
    rev x1, local copies, waits for them, and re-layouts, convolve_pair(): jnp.flip(back_imag.reshape(tokens, local_ch), 0).astype(jnp.bfloat16)  59.3 us
  transfers between devices with their start and end apart: 6, of which 4 were waited for; matrix products, arithmetic and copies ran while one was open for 17% of the time, Pallas kernels for 0%

commit v1 on v0

v1 whole, which is shorter than its diff:
```python
import functools
import math

import jax
import jax.numpy as jnp
import ml_dtypes
import numpy as np
from jax import lax
from jax.experimental import pallas as pl
from jax.experimental.pallas import tpu as pltpu
from jax.sharding import PartitionSpec as P

LANES = 128
TILE = 16
VMEM_BYTES = 56 * 1024 * 1024

f32 = jnp.float32
bf16 = jnp.bfloat16


def two_parts(matrix):
    high = matrix.astype(ml_dtypes.bfloat16)
    low = (matrix - high.astype(np.float64)).astype(ml_dtypes.bfloat16)
    return high, low


def make_tables(rows):
    points = rows * LANES
    n1, k1 = np.arange(rows), np.arange(rows)
    n2, k2 = np.arange(LANES), np.arange(LANES)
    lead = 2 * math.pi / rows * np.outer(k1 + 0.25, n1)
    twist = 2 * math.pi / points * np.outer(k1 + 0.25, n2)
    trail = 2 * math.pi / LANES * np.outer(n2, k2)
    lead_fwd = np.concatenate([np.cos(lead), -np.sin(lead)], 0)
    lead_inv = np.concatenate([np.cos(lead).T, -np.sin(lead).T], 1) / points
    cosine, sine = np.cos(trail), np.sin(trail)
    trail_fwd = np.block([[cosine, -sine], [sine, cosine]])
    trail_inv = np.block([[cosine, sine], [-sine, cosine]])
    lead_fwd = np.concatenate(two_parts(lead_fwd), 1)
    lead_inv = np.concatenate(two_parts(lead_inv), 0)
    trail_fwd = np.stack(two_parts(trail_fwd))
    trail_inv = np.stack(two_parts(trail_inv))
    twist = np.stack([np.cos(twist), -np.sin(twist)]).astype(np.float32)
    return lead_fwd, lead_inv, trail_fwd, trail_inv, twist


def dot(left, right):
    return jnp.dot(left, right, preferred_element_type=f32)


def split(value):
    high = value.astype(bf16)
    return high, (value - high.astype(f32)).astype(bf16)


def lead_stage(lead, twist, pair):
    rows = pair.shape[0]
    turned = dot(lead, jnp.concatenate([pair, pair], 0))
    real, imag = turned[:rows], turned[rows:]
    parts = []
    for side in range(2):
        lanes = slice(side * LANES, (side + 1) * LANES)
        re, im = real[:, lanes], imag[:, lanes]
        parts.append(
            jnp.concatenate([re * twist[0] - im * twist[1], re * twist[1] + im * twist[0]], 1)
        )
    return parts


def trail_stage(high, low, matrix_ref):
    return dot(high, matrix_ref[0]) + dot(low, matrix_ref[0]) + dot(high, matrix_ref[1])


def spectrum_kernel(pieces, group, lead_ref, trail_ref, twist_ref, *refs):
    taps = refs[:pieces]
    out_ref, scratch, high, low = refs[pieces:]
    sources, _, _, width = taps[0].shape
    count = pieces * sources
    for piece in range(pieces):
        for source in range(sources):
            row = (piece * sources + source) * group
            for part in range(width // LANES):
                lanes = slice(part * LANES, (part + 1) * LANES)
                scratch[part, row : row + group, :] = taps[piece][source, 0, :, lanes].astype(f32)
    lead, twist = lead_ref[...], (twist_ref[0], twist_ref[1])
    rows = count * (width // LANES)

    def channel(index):
        parts = [
            scratch[part, pl.ds(index, count, stride=group), :] for part in range(width // LANES)
        ]
        return jnp.concatenate(parts, 0).astype(bf16)

    for index in range(0, group, 2):
        pair = jnp.concatenate([channel(index), channel(index + 1)], 1)
        for side, value in enumerate(lead_stage(lead, twist, pair)):
            place = slice((index + side) * rows, (index + side + 1) * rows)
            high[place, :], low[place, :] = split(value)
    out_ref[...] = trail_stage(high[...], low[...], trail_ref).reshape(out_ref.shape)


def filter_spectrum(pieces, lead, trail, twist, group):
    sources, outer, inner, width = pieces[0].shape
    rows = lead.shape[1] // 2
    steps = inner // group
    whole = lambda ndim: (lambda *_: (0,) * ndim)
    return pl.pallas_call(
        functools.partial(spectrum_kernel, len(pieces), group),
        out_shape=jax.ShapeDtypeStruct((outer * inner, rows, 2 * LANES), f32),
        grid=(outer * steps,),
        in_specs=[
            pl.BlockSpec(lead.shape, whole(2)),
            pl.BlockSpec(trail.shape, whole(3)),
            pl.BlockSpec(twist.shape, whole(3)),
        ]
        + [
            pl.BlockSpec(
                (sources, 1, group, width), lambda step: (0, step // steps, step % steps, 0)
            )
        ]
        * len(pieces),
        out_specs=pl.BlockSpec((group, rows, 2 * LANES), lambda step: (step, 0, 0)),
        scratch_shapes=[
            pltpu.VMEM((width // LANES, len(pieces) * sources * group, LANES), f32),
            pltpu.VMEM((group * rows, 2 * LANES), bf16),
            pltpu.VMEM((group * rows, 2 * LANES), bf16),
        ],
        compiler_params=pltpu.CompilerParams(vmem_limit_bytes=VMEM_BYTES),
        cost_estimate=pl.CostEstimate(
            flops=outer * inner * 10**6, bytes_accessed=2**20, transcendentals=0
        ),
        name="filter_spectrum",
    )(lead, trail, twist, *pieces)


def convolve_kernel(
    group, lead_ref, inv_ref, trail_ref, back_ref, twist_ref, signal_ref, filter_ref, out_ref,
    high, low,
):
    sources, _, _, _, local, _ = signal_ref.shape
    rows = sources * local
    lead, inv, twist = lead_ref[...], inv_ref[...], (twist_ref[0], twist_ref[1])
    for index in range(group):
        pair = jnp.concatenate(
            [signal_ref[:, 0, index, side].reshape(rows, LANES) for side in range(2)], 1
        )
        for side, value in enumerate(lead_stage(lead, twist, pair)):
            place = slice((2 * index + side) * rows, (2 * index + side + 1) * rows)
            high[place, :], low[place, :] = split(value)
    spectra = trail_stage(high[...], low[...], trail_ref)
    for index in range(group):
        fre, fim = filter_ref[index, :, :LANES], filter_ref[index, :, LANES:]
        for side in range(2):
            place = slice((2 * index + side) * rows, (2 * index + side + 1) * rows)
            re, im = spectra[place, :LANES], spectra[place, LANES:]
            if side == 0:
                product = jnp.concatenate([re * fre - im * fim, re * fim + im * fre], 1)
            else:
                product = jnp.concatenate([re * fre + im * fim, im * fre - re * fim], 1)
            high[place, :], low[place, :] = split(product)
    spectra = trail_stage(high[...], low[...], back_ref)
    for index in range(group):
        reals, imags = [], []
        for side in range(2):
            place = slice((2 * index + side) * rows, (2 * index + side + 1) * rows)
            re, im = spectra[place, :LANES], spectra[place, LANES:]
            reals.append(re * twist[0] + im * twist[1])
            imags.append(im * twist[0] - re * twist[1])
        turned = jnp.concatenate([jnp.concatenate(reals, 1), jnp.concatenate(imags, 1)], 0)
        top, rest = split(turned)
        both = dot(inv, top)
        result = both[:rows] + both[rows:] + dot(inv[:rows], rest)
        result = result.astype(bf16)
        for side in range(2):
            lanes = slice(side * LANES, (side + 1) * LANES)
            out_ref[:, index, side] = result[:, lanes].reshape(sources, local, LANES)


def convolve(signals, spectrum, tables, which, place, group):
    lead_fwd, lead_inv, trail_fwd, trail_inv, twist = tables
    sources, _, inner, _, local, _ = signals.shape
    rows = sources * local
    whole = lambda ndim: (lambda *_: (0,) * ndim)
    return pl.pallas_call(
        functools.partial(convolve_kernel, group),
        out_shape=jax.ShapeDtypeStruct((sources, inner, 2, local, LANES), bf16),
        grid=(inner // group,),
        in_specs=[
            pl.BlockSpec(lead_fwd.shape, whole(2)),
            pl.BlockSpec(lead_inv.shape, whole(2)),
            pl.BlockSpec(trail_fwd.shape, whole(3)),
            pl.BlockSpec(trail_inv.shape, whole(3)),
            pl.BlockSpec(twist.shape, whole(3)),
            pl.BlockSpec(
                (sources, 1, group, 2, local, LANES), lambda step: (0, which, step, 0, 0, 0)
            ),
            pl.BlockSpec(
                (group, rows, 2 * LANES), lambda step: (place // group + step, 0, 0)
            ),
        ],
        out_specs=pl.BlockSpec((sources, group, 2, local, LANES), lambda step: (0, step, 0, 0, 0)),
        scratch_shapes=[pltpu.VMEM((2 * group * rows, 2 * LANES), bf16)] * 2,
        compiler_params=pltpu.CompilerParams(vmem_limit_bytes=VMEM_BYTES),
        cost_estimate=pl.CostEstimate(
            flops=inner * 10**6, bytes_accessed=2**20, transcendentals=0
        ),
        name="convolve",
    )(lead_fwd, lead_inv, trail_fwd, trail_inv, twist, signals, spectrum)


def gate_kernel(key_ref, value_ref, query_ref, grad_ref, out_ref, scratch):
    tokens, width = key_ref.shape
    local = tokens // LANES
    pitch = scratch.shape[0] // local
    dests, _, inner, _, _, _ = out_ref.shape
    for side, (one, two) in enumerate(((key_ref, value_ref), (grad_ref, query_ref))):
        for row in range(local):
            place = slice(row * LANES, (row + 1) * LANES)
            product = one[place, :].astype(f32) * two[place, :].astype(f32)
            scratch[row * pitch : row * pitch + width, :] = product.T
        for dest in range(dests):
            for index in range(inner):
                column = dest * inner + index
                out_ref[dest, 0, index, side] = scratch[
                    pl.ds(column, local, stride=pitch), :
                ].astype(bf16)


def gate(key_proj, value_proj, query_proj, out_grad, first, parts, groups, inner):
    tokens = key_proj.shape[0]
    local = tokens // LANES
    dests = LANES // inner
    blocks = groups // dests
    column = pl.BlockSpec((tokens, LANES), lambda step: (0, first * blocks + step))
    return pl.pallas_call(
        gate_kernel,
        out_shape=jax.ShapeDtypeStruct((groups, parts, inner, 2, local, LANES), bf16),
        grid=(parts * blocks,),
        in_specs=[column] * 4,
        out_specs=pl.BlockSpec(
            (dests, 1, inner, 2, local, LANES),
            lambda step: (step % blocks, step // blocks, 0, 0, 0, 0),
        ),
        scratch_shapes=[pltpu.VMEM((local * (LANES + 8), LANES), f32)],
        compiler_params=pltpu.CompilerParams(vmem_limit_bytes=VMEM_BYTES),
        cost_estimate=pl.CostEstimate(
            flops=0, bytes_accessed=2**20, transcendentals=0
        ),
        name="gate",
    )(key_proj, value_proj, query_proj, out_grad)


def finish_kernel(skip_ref, conv_ref, key_ref, value_ref, query_ref, grad_ref, *refs):
    out_ref, query_out, key_out, value_out, scratch = refs[-5:]
    tokens, width = key_ref.shape
    local = tokens // LANES
    dests, inner = conv_ref.shape[:2]
    skip = skip_ref[...]
    for side in range(2):
        for dest in range(dests):
            for index in range(inner):
                row = (dest * inner + index) * local
                scratch[side, row : row + local, :] = conv_ref[dest, index, side].astype(f32)
    for row in range(local):
        place = slice(row * LANES, (row + 1) * LANES)
        key, value = key_ref[place, :].astype(f32), value_ref[place, :].astype(f32)
        query, grad = query_ref[place, :].astype(f32), grad_ref[place, :].astype(f32)
        convolved = scratch[0, pl.ds(row, width, stride=local), :].T
        reflected = scratch[1, pl.ds(row, width, stride=local), :].T
        summed = convolved + skip * (key * value).astype(bf16).astype(f32)
        grad_sum = reflected + skip * (grad * query).astype(bf16).astype(f32)
        out_ref[place, :] = (query * summed).astype(bf16)
        query_out[place, :] = (grad * summed).astype(bf16)
        key_out[place, :] = (grad_sum * value).astype(bf16)
        value_out[place, :] = (grad_sum * key).astype(bf16)


def finish(skip, conv, key_proj, value_proj, query_proj, out_grad, part, previous):
    groups, inner = conv.shape[:2]
    tokens = key_proj.shape[0]
    dests = LANES // inner
    blocks = groups // dests
    local = tokens // LANES
    column = pl.BlockSpec((tokens, LANES), lambda step: (0, part * blocks + step))
    keep = [pl.BlockSpec(memory_space=pl.ANY)] * len(previous)
    return pl.pallas_call(
        finish_kernel,
        out_shape=[jax.ShapeDtypeStruct(key_proj.shape, bf16)] * 4,
        grid=(blocks,),
        in_specs=[
            pl.BlockSpec((1, LANES), lambda step: (0, part * blocks + step)),
            pl.BlockSpec((dests, inner, 2, local, LANES), lambda step: (step, 0, 0, 0, 0)),
        ]
        + [column] * 4
        + keep,
        out_specs=[column] * 4,
        scratch_shapes=[pltpu.VMEM((2, LANES * local, LANES), f32)],
        input_output_aliases={6 + index: index for index in range(len(previous))},
        compiler_params=pltpu.CompilerParams(vmem_limit_bytes=VMEM_BYTES),
        cost_estimate=pl.CostEstimate(
            flops=0, bytes_accessed=2**20, transcendentals=0
        ),
        name="finish",
    )(skip, conv, key_proj, value_proj, query_proj, out_grad, *previous)


def swap(value, axis="ctx"):
    return lax.all_to_all(value, axis, split_axis=0, concat_axis=0, tiled=True)


def fast_shards(query_proj, key_proj, value_proj, out_grad, long_filter, skip_gain, parts, halves):
    groups, planes = lax.axis_size("ctx"), lax.axis_size("ch")
    tokens, width = key_proj.shape
    channels, taps = long_filter.shape
    rows = groups * tokens // LANES
    inner = width // (groups * parts)
    tables = make_tables(rows)
    lead_fwd, lead_inv, trail_fwd, trail_inv, twist = (jnp.asarray(table) for table in tables)
    tables = (lead_fwd, lead_inv, trail_fwd, trail_inv, twist)
    plane = lax.axis_index("ch")

    sent = long_filter.reshape(planes, parts, groups, inner, taps).transpose(2, 0, 1, 3, 4)
    taken = swap(sent)
    per_half = parts // halves

    tiles = taps // LANES
    order = lead_fwd.reshape(2 * rows, 2, planes, groups, tiles).transpose(0, 1, 4, 2, 3)
    index = jnp.arange(planes) ^ plane
    lead_taps = jnp.take(order, index, axis=3).reshape(lead_fwd.shape)

    def pieces_of(taken, half):
        cut = taken[:, :, half * per_half : (half + 1) * per_half]
        found = []
        for step in range(planes):
            piece = lax.dynamic_index_in_dim(cut, plane ^ step, 1, keepdims=False)
            if step:
                piece = lax.ppermute(piece, "ch", [(i, i ^ step) for i in range(planes)])
            found.append(piece)
        return found

    outputs = []
    skip = skip_gain.reshape(1, width)
    signals = []
    gates = [
        gate(key_proj, value_proj, query_proj, out_grad, half * per_half, per_half, groups, inner)
        for half in range(halves)
    ]
    pieces = []
    for half in range(halves):
        before = (taken, signals[-1], pieces[-1]) if half else taken
        gates[half], before = lax.optimization_barrier((gates[half], before))
        taken = before[0] if half else before
        signals.append(swap(gates[half]))
        pieces.append(pieces_of(taken, half))
    for half in range(halves):
        spectra = filter_spectrum(pieces[half], lead_taps, trail_fwd, twist, TILE)
        for part in range(per_half):
            conv = convolve(signals[half], spectra, tables, part, part * inner, 16)
            if half < halves - 1:
                conv, pieces[half + 1], signals[half + 1] = lax.optimization_barrier(
                    (conv, pieces[half + 1], signals[half + 1])
                )
            outputs = finish(
                skip, swap(conv), key_proj, value_proj, query_proj, out_grad,
                half * per_half + part, outputs,
            )
    return tuple(outputs)


def plain_shards(query_proj, key_proj, value_proj, out_grad, long_filter, skip_gain):
    groups, planes = lax.axis_size("ctx"), lax.axis_size("ch")
    tokens, width = key_proj.shape
    channels, taps = long_filter.shape
    inner = width // groups
    length = groups * tokens
    rows = length // LANES
    tables = tuple(jnp.asarray(table) for table in make_tables(rows))
    group = 2 if inner % 2 == 0 else 1
    sent = long_filter.reshape(planes, groups, inner, taps).transpose(1, 0, 2, 3)
    taken = swap(swap(sent).transpose(1, 0, 2, 3), "ch")
    filters = taken.transpose(2, 0, 1, 3).reshape(inner, rows, LANES)
    lead, twist = tables[0].astype(f32), tables[4]
    lead = lead[:, :rows] + lead[:, rows:]
    trail = tables[2].astype(f32)
    highest = lax.Precision.HIGHEST
    turned = jnp.einsum("kn,cnm->ckm", lead, filters.astype(f32), precision=highest)
    real, imag = turned[:, :rows], turned[:, rows:]
    turned = jnp.concatenate(
        [real * twist[0] - imag * twist[1], real * twist[1] + imag * twist[0]], 2
    )
    spectrum = jnp.einsum("ckm,mj->ckj", turned, trail[0] + trail[1], precision=highest)
    gated_kv = (key_proj.astype(f32) * value_proj.astype(f32)).astype(bf16)
    grad_gate = (out_grad.astype(f32) * query_proj.astype(f32)).astype(bf16)
    both = jnp.stack([gated_kv.T, grad_gate.T], 1)
    taken = swap(both.reshape(groups, inner, 2, tokens))
    signals = taken.transpose(1, 2, 0, 3).reshape(1, 1, inner, 2, rows, LANES)
    conv = convolve(signals, spectrum, tables, 0, 0, group)
    back = conv.reshape(inner, 2, groups, tokens).transpose(2, 0, 1, 3)
    back = swap(back).reshape(width, 2, tokens)
    convolved, reflected = back[:, 0].T, back[:, 1].T
    summed = convolved.astype(f32) + skip_gain[None, :] * gated_kv.astype(f32)
    grad_sum = reflected.astype(f32) + skip_gain[None, :] * grad_gate.astype(f32)
    return (
        (query_proj.astype(f32) * summed).astype(bf16),
        (out_grad.astype(f32) * summed).astype(bf16),
        (grad_sum * value_proj.astype(f32)).astype(bf16),
        (grad_sum * key_proj.astype(f32)).astype(bf16),
    )


def shards(query_proj, key_proj, value_proj, out_grad, long_filter, skip_gain):
    groups = lax.axis_size("ctx")
    tokens, width = key_proj.shape
    planes = lax.axis_size("ch")
    taps = long_filter.shape[1]
    args = (query_proj, key_proj, value_proj, out_grad, long_filter, skip_gain)
    parts = 2
    inner = width // (groups * parts)
    fits = (
        tokens % (TILE * LANES) == 0
        and taps % LANES == 0
        and width % (groups * parts) == 0
        and inner % TILE == 0
        and LANES % inner == 0
        and groups % (LANES // inner) == 0
        and planes & (planes - 1) == 0
    )
    if fits:
        return fast_shards(*args, parts, 2)
    return plain_shards(*args)


def solution(mesh):
    placed = (
        P("ctx", "ch"),
        P("ctx", "ch"),
        P("ctx", "ch"),
        P("ctx", "ch"),
        P(None, ("ch", "ctx")),
        P("ch"),
    )
    return jax.shard_map(
        shards,
        mesh=mesh,
        in_specs=placed,
        out_specs=(P("ctx", "ch"), P("ctx", "ch"), P("ctx", "ch"), P("ctx", "ch")),
        check_vma=False,
    )
```

time: 1780 us -> 293 us (0.16); the launches traced: 1760 us -> 293 us
  matrix products: 948 us -> 0 us
  local copies, waits for them, and re-layouts: 346 us -> 13.3 us
  other arithmetic: 306 us -> 0.68 us
  Pallas kernels: 0 us -> 120 us
    dot_general x34 -> x0, matrix products: 948 us -> none  [the longest x12 500 us: middle_product(): return jnp.einsum('jb,abr->ajr', matrix, signal, precision=highest)]
    sub x2 -> x0, other arithmetic: 167 us -> none  [rotate(): new_real = product(cosine, real_part) - orient * product(sine, imag_part)]
    pallas_call x0 -> x8, Pallas kernels: none -> 120 us  [the longest x2 64.5 us: convolve(): pl.pallas_call(functools.partial(convolve_kernel, group), out_shape=jax.S...]
    rev x2 -> x0, local copies, waits for them, and re-layouts: 119 us -> none  [the longest x1 59.4 us: convolve_pair(): signal_imag = jnp.flip(grad_ch, 0).astype(jnp.float32).reshape(grid_shape)]
    add x1 -> x0, other arithmetic: 90.4 us -> none  [rotate(): new_imag = product(cosine, imag_part) + orient * product(sine, real_part)]
    unnamed x62 -> x14, local copies, waits for them, and re-layouts: 89 us -> 2.08 us
    convert_element_type x4 -> x0, other arithmetic: 44.9 us -> none  [the longest x1 22.7 us: finish_tokens(): value_grad = (grad_sum * key_proj.astype(jnp.float32)).astype(jnp.bfloat16)]
    all_to_all x6 -> x5, waiting for transfers between devices: 125 us -> 87.1 us  [swap(): return lax.all_to_all(value, axis, split_axis=0, concat_axis=0, tiled=True)]
  transfers between devices with their start and end apart: 6 -> 11, of which waited for: 4 -> 5; matrix products, arithmetic and copies ran while one was open for 17% -> 2% of each run, Pallas kernels for 0% -> 37%
where the time goes in v1:
time: 293 us
  waiting for transfers between devices  124 us (42%)
  Pallas kernels  120 us (41%)
  starting transfers between devices  33.3 us (11%)
  local copies, waits for them, and re-layouts  13.3 us (5%)
    all_to_all x5, waiting for transfers between devices, swap(): return lax.all_to_all(value, axis, split_axis=0, concat_axis=0, tiled=True)  87.1 us
    pallas_call x2, Pallas kernels, convolve(): pl.pallas_call(functools.partial(convolve_kernel, group), out_shape=jax.S...  64.5 us
    ppermute x6, waiting for transfers between devices, pieces_of(): piece = lax.ppermute(piece, 'ch', [(i, i ^ step) for i in range(planes)])  37.1 us
    all_to_all x5, starting transfers between devices, swap(): return lax.all_to_all(value, axis, split_axis=0, concat_axis=0, tiled=True)  24 us
    pallas_call x2, Pallas kernels, finish(): pl.pallas_call(finish_kernel, out_shape=[jax.ShapeDtypeStruct(key_proj.sh...  21.3 us
    pallas_call x2, Pallas kernels, filter_spectrum(): pl.pallas_call(functools.partial(spectrum_kernel, len(pieces), group), ou...  19.2 us
    pallas_call x2, Pallas kernels, gate(): pl.pallas_call(gate_kernel, out_shape=jax.ShapeDtypeStruct((groups, parts...  15.2 us
    ppermute x6, starting transfers between devices, pieces_of(): piece = lax.ppermute(piece, 'ch', [(i, i ^ step) for i in range(planes)])  9.3 us
  transfers between devices with their start and end apart: 11, of which 5 were waited for; matrix products, arithmetic and copies ran while one was open for 2% of the time, Pallas kernels for 37%

profile of v1, /device:TPU:0, one launch (start us, length us, event | category | flops | bytes accessed | tf_op | source)
XLA Modules:
  0.0 292.6 jit_solution(1542028721039508927)
XLA Ops:
  0.6 4.7 %copy.23 = bf16[8,4,2,64,512]{4,3,2,1,0:T(8,128)(2,1)} copy(bf16[8,4,2,64,512]{4,3,0,2,1:T(8,128)(2,1)} %bitcast.25) | data formatting | bytes 8388608 | tf_op jit(solution)/shard_map/transpose | solution.py:322
  5.3 5.2 %all-to-all-start = ((bf16[8,4,2,64,512]{4,3,2,1,0:T(8,128)(2,1)}), bf16[8,4,2,64,512]{4,3,2,1,0:T(8,128)(2,1)}, u32[]{:S(2)}, u32[]{:S(2)}) async-start(bf16[8,4,2,64,512]{4,3,2,1,0:T(8,128)(2,1)} %copy.23), calls=%async_computation | async-start | bytes 8388608 | tf_op jit(solution)/shard_map/all_to_all | solution.py:308
  10.5 7.6 %gate.2 = bf16[8,1,64,2,16,128]{5,4,3,2,1,0:T(8,128)(2,1)} custom-call(bf16[2048,1024]{1,0:T(8,128)(2,1)} %key_ref.7, bf16[2048,1024]{1,0:T(8,128)(2,1)} %value_ref.7, bf16[2048,1024]{1,0:T(8,128)(2,1)} %query_ref.7, bf16[2048,1024]{1,0:T(8,128)(2,1)} %grad_ref.7), custom_call_target="tpu_custom_call" | custom-call | bytes 1048576 | tf_op jit(solution)/shard_map/gate/pallas_call | solution.py:235
  18.1 41.6 %all-to-all-done = bf16[8,4,2,64,512]{4,3,2,1,0:T(8,128)(2,1)} async-done(((bf16[8,4,2,64,512]{4,3,2,1,0:T(8,128)(2,1)}), bf16[8,4,2,64,512]{4,3,2,1,0:T(8,128)(2,1)}, u32[]{:S(2)}, u32[]{:S(2)}) %all-to-all-start) | async-done | bytes 4194336 | tf_op jit(solution)/shard_map/all_to_all | solution.py:308
  59.7 4.6 %all-to-all-start.1 = ((bf16[8,1,64,2,16,128]{5,4,3,2,1,0:T(8,128)(2,1)}), bf16[8,1,64,2,16,128]{5,4,3,2,1,0:T(8,128)(2,1)}, u32[]{:S(2)}, u32[]{:S(2)}) async-start(bf16[8,1,64,2,16,128]{5,4,3,2,1,0:T(8,128)(2,1)} %gate.2), calls=%async_computation.1 | async-start | bytes 8388608 | tf_op jit(solution)/shard_map/all_to_all | solution.py:308
  64.4 1.8 slice.6
  66.2 1.0 dynamic-slice_bitcast_fusion.4
  67.2 4.3 %collective-permute-start.2 = (bf16[8,1,64,512]{3,2,1,0:T(8,128)(2,1)S(1)}, bf16[8,1,64,512]{3,2,1,0:T(8,128)(2,1)S(1)}, u32[]{:S(2)}, u32[]{:S(2)}) collective-permute-start(bf16[8,1,64,512]{3,2,1,0:T(8,128)(2,1)S(1)} %get-tuple-element.36), channel_id=1, source_target_pairs={{0,3},{1,2},{2,1},{3,0},{4,7},{5,6},{6,5},{7,4},{8,11},{9,10},{10,... | collective-permute-start | bytes 1572872 | tf_op jit(solution)/shard_map/ppermute | solution.py:337
  71.6 0.6 collective-permute-start
  72.1 7.6 %gate.3 = bf16[8,1,64,2,16,128]{5,4,3,2,1,0:T(8,128)(2,1)} custom-call(bf16[2048,1024]{1,0:T(8,128)(2,1)} %key_ref.7, bf16[2048,1024]{1,0:T(8,128)(2,1)} %value_ref.7, bf16[2048,1024]{1,0:T(8,128)(2,1)} %query_ref.7, bf16[2048,1024]{1,0:T(8,128)(2,1)} %grad_ref.7), custom_call_target="tpu_custom_call" | custom-call | bytes 1048576 | tf_op jit(solution)/shard_map/gate/pallas_call | solution.py:235
  79.7 4.8 %collective-permute-done.2.refs_3_ = bf16[8,1,64,512]{3,2,1,0:T(8,128)(2,1)S(1)} collective-permute-done((bf16[8,1,64,512]{3,2,1,0:T(8,128)(2,1)S(1)}, bf16[8,1,64,512]{3,2,1,0:T(8,128)(2,1)S(1)}, u32[]{:S(2)}, u32[]{:S(2)}) %collective-permute-start.2) | collective-permute-done | bytes 524320 | tf_op jit(solution)/shard_map/ppermute | solution.py:337
  84.5 32.4 %collective-permute-done.1.refs_2_ = bf16[8,1,64,512]{3,2,1,0:T(8,128)(2,1)S(1)} collective-permute-done((bf16[8,1,64,512]{3,2,1,0:T(8,128)(2,1)S(1)}, bf16[8,1,64,512]{3,2,1,0:T(8,128)(2,1)S(1)}, u32[]{:S(2)}, u32[]{:S(2)}) %collective-permute-start.1) | collective-permute-done | bytes 524320 | tf_op jit(solution)/shard_map/ppermute | solution.py:337
  116.9 0.8 copy-done.2
  117.7 0.2 copy-done.3
  117.9 4.8 %all-to-all-start.2 = ((bf16[8,1,64,2,16,128]{5,4,3,2,1,0:T(8,128)(2,1)}), bf16[8,1,64,2,16,128]{5,4,3,2,1,0:T(8,128)(2,1)}, u32[]{:S(2)}, u32[]{:S(2)}) async-start(bf16[8,1,64,2,16,128]{5,4,3,2,1,0:T(8,128)(2,1)} %gate.3), calls=%async_computation.2 | async-start | bytes 8388608 | tf_op jit(solution)/shard_map/all_to_all | solution.py:308
  122.7 1.9 slice.7
  124.6 1.0 dynamic-slice_bitcast_fusion
  125.6 2.5 collective-permute-start.5
  128.0 1.9 collective-permute-start.3
  130.2 0.6 gather_fusion
  130.9 0.7 broadcast_select_fusion.lead_ref
  131.5 9.6 %filter_spectrum.2.filter_ref = f32[64,128,256]{2,1,0:T(8,128)} custom-call(bf16[256,256]{1,0:T(8,128)(2,1)} %broadcast_select_fusion.lead_ref, bf16[2,256,256]{2,1,0:T(8,128)(2,1)} %constant.55.clone.trail_ref, f32[2,128,128]{2,1,0:T(8,128)} %constant.57.clone.twist_ref, bf16[8,1,64,512]{3,2,1,0:T(8,128)(2,1)} %get-tuple-element.39.refs_0_, ...), custom_call_target="tpu_custom_call" | custom-call | flops 64000000 | bytes 1048576 | tf_op jit(solution)/shard_map/filter_spectrum/pallas_call | solution.py:107
  141.1 32.2 %convolve.2 = bf16[8,64,2,16,128]{4,3,2,1,0:T(8,128)(2,1)} custom-call(bf16[256,256]{1,0:T(8,128)(2,1)} %constant.53.clone.lead_ref, bf16[256,256]{1,0:T(8,128)(2,1)} %constant.54.clone.inv_ref, bf16[2,256,256]{2,1,0:T(8,128)(2,1)} %constant.55.clone.trail_ref, bf16[2,256,256]{2,1,0:T(8,128)(2,1)} %constant.56.clone.back_ref, ...), custom_call_target="tpu_custom_call" | custom-call | flops 64000000 | bytes 1048576 | tf_op jit(solution)/shard_map/convolve/pallas_call | solution.py:184
  173.4 0.7 copy-done.4
  174.5 4.8 %all-to-all-start.4 = ((bf16[8,64,2,16,128]{4,3,2,1,0:T(8,128)(2,1)}), bf16[8,64,2,16,128]{4,3,2,1,0:T(8,128)(2,1)}, u32[]{:S(2)}, u32[]{:S(2)}) async-start(bf16[8,64,2,16,128]{4,3,2,1,0:T(8,128)(2,1)} %convolve.2), calls=%async_computation.4 | async-start | bytes 8388608 | tf_op jit(solution)/shard_map/all_to_all | solution.py:308
  179.3 9.6 %filter_spectrum.3.filter_ref = f32[64,128,256]{2,1,0:T(8,128)} custom-call(bf16[256,256]{1,0:T(8,128)(2,1)} %broadcast_select_fusion.lead_ref, bf16[2,256,256]{2,1,0:T(8,128)(2,1)} %constant.55.clone.trail_ref, f32[2,128,128]{2,1,0:T(8,128)} %constant.57.clone.twist_ref, bf16[8,1,64,512]{3,2,1,0:T(8,128)(2,1)} %get-tuple-element.23.refs_0_, ...), custom_call_target="tpu_custom_call" | custom-call | flops 64000000 | bytes 1048576 | tf_op jit(solution)/shard_map/filter_spectrum/pallas_call | solution.py:107
  189.0 32.2 %convolve.3 = bf16[8,64,2,16,128]{4,3,2,1,0:T(8,128)(2,1)} custom-call(bf16[256,256]{1,0:T(8,128)(2,1)} %constant.53.clone.lead_ref, bf16[256,256]{1,0:T(8,128)(2,1)} %constant.54.clone.inv_ref, bf16[2,256,256]{2,1,0:T(8,128)(2,1)} %constant.55.clone.trail_ref, bf16[2,256,256]{2,1,0:T(8,128)(2,1)} %constant.56.clone.back_ref, ...), custom_call_target="tpu_custom_call" | custom-call | flops 64000000 | bytes 1048576 | tf_op jit(solution)/shard_map/convolve/pallas_call | solution.py:184
  221.2 7.0 %all-to-all-done.4.conv_ref = bf16[8,64,2,16,128]{4,3,2,1,0:T(8,128)(2,1)} async-done(((bf16[8,64,2,16,128]{4,3,2,1,0:T(8,128)(2,1)}), bf16[8,64,2,16,128]{4,3,2,1,0:T(8,128)(2,1)}, u32[]{:S(2)}, u32[]{:S(2)}) %all-to-all-start.4) | async-done | bytes 4194336 | tf_op jit(solution)/shard_map/all_to_all | solution.py:308
  228.2 4.6 %all-to-all-start.3 = ((bf16[8,64,2,16,128]{4,3,2,1,0:T(8,128)(2,1)}), bf16[8,64,2,16,128]{4,3,2,1,0:T(8,128)(2,1)}, u32[]{:S(2)}, u32[]{:S(2)}) async-start(bf16[8,64,2,16,128]{4,3,2,1,0:T(8,128)(2,1)} %convolve.3), calls=%async_computation.3 | async-start | bytes 8388608 | tf_op jit(solution)/shard_map/all_to_all | solution.py:308
  232.8 10.6 %finish.2 = (bf16[2048,1024]{1,0:T(8,128)(2,1)}, bf16[2048,1024]{1,0:T(8,128)(2,1)}, bf16[2048,1024]{1,0:T(8,128)(2,1)}, bf16[2048,1024]{1,0:T(8,128)(2,1)}) custom-call(f32[1,1024]{1,0:T(1,128)} %bitcast.27, bf16[8,64,2,16,128]{4,3,2,1,0:T(8,128)(2,1)} %all-to-all-done.4.conv_ref, bf16[2048,1024]{1,0:T(8,128)(2,1)} %key_ref.7, ...), custom_call_target="tpu_custom_call" | custom-call | bytes 1048576 | tf_op jit(solution)/shard_map/finish/pallas_call | solution.py:286
  243.4 38.5 %all-to-all-done.3.conv_ref = bf16[8,64,2,16,128]{4,3,2,1,0:T(8,128)(2,1)} async-done(((bf16[8,64,2,16,128]{4,3,2,1,0:T(8,128)(2,1)}), bf16[8,64,2,16,128]{4,3,2,1,0:T(8,128)(2,1)}, u32[]{:S(2)}, u32[]{:S(2)}) %all-to-all-start.3) | async-done | bytes 4194336 | tf_op jit(solution)/shard_map/all_to_all | solution.py:308
  281.9 10.7 %finish.3 = (bf16[2048,1024]{1,0:T(8,128)(2,1)}, bf16[2048,1024]{1,0:T(8,128)(2,1)}, bf16[2048,1024]{1,0:T(8,128)(2,1)}, bf16[2048,1024]{1,0:T(8,128)(2,1)}) custom-call(f32[1,1024]{1,0:T(1,128)} %bitcast.28, bf16[8,64,2,16,128]{4,3,2,1,0:T(8,128)(2,1)} %all-to-all-done.3.conv_ref, ...), custom_call_target="tpu_custom_call", output_to_operand_aliasing={{0}: (6, {}), {1}: (7, {}), {2}: (8, {}), {3}: (9, {})} | custom-call | bytes 1048576 | tf_op jit(solution)/shard_map/finish/pallas_call | solution.py:286
  (26 shorter events, 0.7 us)
Async XLA Ops:
  5.3 54.4 %all-to-all-start = ((bf16[8,4,2,64,512]{4,3,2,1,0:T(8,128)(2,1)}), bf16[8,4,2,64,512]{4,3,2,1,0:T(8,128)(2,1)}, u32[]{:S(2)}, u32[]{:S(2)}) async-start(bf16[8,4,2,64,512]{4,3,2,1,0:T(8,128)(2,1)} %copy.23), calls=%async_computation | async-start | bytes 8388608 | tf_op jit(solution)/shard_map/all_to_all | solution.py:308
  59.7 57.2 %all-to-all-start.1 = ((bf16[8,1,64,2,16,128]{5,4,3,2,1,0:T(8,128)(2,1)}), bf16[8,1,64,2,16,128]{5,4,3,2,1,0:T(8,128)(2,1)}, u32[]{:S(2)}, u32[]{:S(2)}) async-start(bf16[8,1,64,2,16,128]{5,4,3,2,1,0:T(8,128)(2,1)} %gate.2), calls=%async_computation.1 | async-start | bytes 8388608 | tf_op jit(solution)/shard_map/all_to_all | solution.py:308
  67.2 17.3 %collective-permute-start.2 = (bf16[8,1,64,512]{3,2,1,0:T(8,128)(2,1)S(1)}, bf16[8,1,64,512]{3,2,1,0:T(8,128)(2,1)S(1)}, u32[]{:S(2)}, u32[]{:S(2)}) collective-permute-start(bf16[8,1,64,512]{3,2,1,0:T(8,128)(2,1)S(1)} %get-tuple-element.36), channel_id=1, source_target_pairs={{0,3},{1,2},{2,1},{3,0},{4,7},{5,6},{6,5},{7,4},{8,11},{9,10},{10,... | collective-permute-start | bytes 1572872 | tf_op jit(solution)/shard_map/ppermute | solution.py:337
  71.6 45.3 %collective-permute-start.1 = (bf16[8,1,64,512]{3,2,1,0:T(8,128)(2,1)S(1)}, bf16[8,1,64,512]{3,2,1,0:T(8,128)(2,1)S(1)}, u32[]{:S(2)}, u32[]{:S(2)}) collective-permute-start(bf16[8,1,64,512]{3,2,1,0:T(8,128)(2,1)S(1)} %get-tuple-element.37), channel_id=1, source_target_pairs={{0,2},{1,3},{2,0},{3,1},{4,6},{5,7},{6,4},{7,5},{8,10},{9,11},{10,... | collective-permute-start | bytes 1572872 | tf_op jit(solution)/shard_map/ppermute | solution.py:337
  71.6 45.3 %collective-permute-start = (bf16[8,1,64,512]{3,2,1,0:T(8,128)(2,1)S(1)}, bf16[8,1,64,512]{3,2,1,0:T(8,128)(2,1)S(1)}, u32[]{:S(2)}, u32[]{:S(2)}) collective-permute-start(bf16[8,1,64,512]{3,2,1,0:T(8,128)(2,1)S(1)} %get-tuple-element.38), channel_id=1, source_target_pairs={{0,1},{1,0},{2,3},{3,2},{4,5},{5,4},{6,7},{7,6},{8,9},{9,8},{10,11... | collective-permute-start | bytes 1572872 | tf_op jit(solution)/shard_map/ppermute | solution.py:337
  84.5 32.4 %copy-start.1 = (bf16[8,1,64,512]{3,2,1,0:T(8,128)(2,1)}, bf16[8,1,64,512]{3,2,1,0:T(8,128)(2,1)S(1)}, u32[]{:S(2)}) copy-start(bf16[8,1,64,512]{3,2,1,0:T(8,128)(2,1)S(1)} %collective-permute-done.2.refs_3_) | copy-start | bytes 1572868
  116.9 0.8 copy-start.2
  116.9 1.0 copy-start.3
  117.9 55.5 %all-to-all-start.2 = ((bf16[8,1,64,2,16,128]{5,4,3,2,1,0:T(8,128)(2,1)}), bf16[8,1,64,2,16,128]{5,4,3,2,1,0:T(8,128)(2,1)}, u32[]{:S(2)}, u32[]{:S(2)}) async-start(bf16[8,1,64,2,16,128]{5,4,3,2,1,0:T(8,128)(2,1)} %gate.3), calls=%async_computation.2 | async-start | bytes 8388608 | tf_op jit(solution)/shard_map/all_to_all | solution.py:308
  122.7 7.5 %copy-start = (bf16[256,2,4,4,8]{0,4,3,2,1:T(8,128)(2,1)S(1)}, bf16[256,2,4,4,8]{0,4,3,2,1:T(8,128)(2,1)}, u32[]{:S(2)}) copy-start(bf16[256,2,4,4,8]{0,4,3,2,1:T(8,128)(2,1)} %constant.59) | copy-start | bytes 393220
  125.6 47.8 %collective-permute-start.5 = (bf16[8,1,64,512]{3,2,1,0:T(8,128)(2,1)S(1)}, bf16[8,1,64,512]{3,2,1,0:T(8,128)(2,1)S(1)}, u32[]{:S(2)}, u32[]{:S(2)}) collective-permute-start(bf16[8,1,64,512]{3,2,1,0:T(8,128)(2,1)S(1)} %get-tuple-element.32), channel_id=1, source_target_pairs={{0,3},{1,2},{2,1},{3,0},{4,7},{5,6},{6,5},{7,4},{8,11},{9,10},{10,... | collective-permute-start | bytes 1572872 | tf_op jit(solution)/shard_map/ppermute | solution.py:337
  128.0 45.3 %collective-permute-start.4 = (bf16[8,1,64,512]{3,2,1,0:T(8,128)(2,1)S(1)}, bf16[8,1,64,512]{3,2,1,0:T(8,128)(2,1)S(1)}, u32[]{:S(2)}, u32[]{:S(2)}) collective-permute-start(bf16[8,1,64,512]{3,2,1,0:T(8,128)(2,1)S(1)} %get-tuple-element.33), channel_id=1, source_target_pairs={{0,2},{1,3},{2,0},{3,1},{4,6},{5,7},{6,4},{7,5},{8,10},{9,11},{10,... | collective-permute-start | bytes 1572872 | tf_op jit(solution)/shard_map/ppermute | solution.py:337
  128.0 45.3 %collective-permute-start.3 = (bf16[8,1,64,512]{3,2,1,0:T(8,128)(2,1)S(1)}, bf16[8,1,64,512]{3,2,1,0:T(8,128)(2,1)S(1)}, u32[]{:S(2)}, u32[]{:S(2)}) collective-permute-start(bf16[8,1,64,512]{3,2,1,0:T(8,128)(2,1)S(1)} %get-tuple-element.34), channel_id=1, source_target_pairs={{0,1},{1,0},{2,3},{3,2},{4,5},{5,4},{6,7},{7,6},{8,9},{9,8},{10,11... | collective-permute-start | bytes 1572872 | tf_op jit(solution)/shard_map/ppermute | solution.py:337
  173.3 0.8 copy-start.4
  173.4 1.0 copy-start.5
  173.4 1.1 copy-start.6
  174.5 53.7 %all-to-all-start.4 = ((bf16[8,64,2,16,128]{4,3,2,1,0:T(8,128)(2,1)}), bf16[8,64,2,16,128]{4,3,2,1,0:T(8,128)(2,1)}, u32[]{:S(2)}, u32[]{:S(2)}) async-start(bf16[8,64,2,16,128]{4,3,2,1,0:T(8,128)(2,1)} %convolve.2), calls=%async_computation.4 | async-start | bytes 8388608 | tf_op jit(solution)/shard_map/all_to_all | solution.py:308
  228.2 53.7 %all-to-all-start.3 = ((bf16[8,64,2,16,128]{4,3,2,1,0:T(8,128)(2,1)}), bf16[8,64,2,16,128]{4,3,2,1,0:T(8,128)(2,1)}, u32[]{:S(2)}, u32[]{:S(2)}) async-start(bf16[8,64,2,16,128]{4,3,2,1,0:T(8,128)(2,1)} %convolve.3), calls=%async_computation.3 | async-start | bytes 8388608 | tf_op jit(solution)/shard_map/all_to_all | solution.py:308

commit v2 on v1

v2 whole, which is shorter than its diff:
```python
import functools
import math

import jax
import jax.numpy as jnp
import ml_dtypes
import numpy as np
from jax import lax
from jax.experimental import pallas as pl
from jax.experimental.pallas import tpu as pltpu
from jax.sharding import PartitionSpec as P

LANES = 128
TILE = 16
VMEM_BYTES = 56 * 1024 * 1024

f32 = jnp.float32
bf16 = jnp.bfloat16


def two_parts(matrix):
    high = matrix.astype(ml_dtypes.bfloat16)
    low = (matrix - high.astype(np.float64)).astype(ml_dtypes.bfloat16)
    return high, low


def make_tables(rows):
    points = rows * LANES
    n1, k1 = np.arange(rows), np.arange(rows)
    n2, k2 = np.arange(LANES), np.arange(LANES)
    lead = 2 * math.pi / rows * np.outer(k1 + 0.25, n1)
    twist = 2 * math.pi / points * np.outer(k1 + 0.25, n2)
    trail = 2 * math.pi / LANES * np.outer(n2, k2)
    lead_fwd = np.concatenate([np.cos(lead), -np.sin(lead)], 0)
    lead_inv = np.concatenate([np.cos(lead).T, -np.sin(lead).T], 1) / points
    cosine, sine = np.cos(trail), np.sin(trail)
    trail_fwd = np.block([[cosine, -sine], [sine, cosine]])
    trail_inv = np.block([[cosine, sine], [-sine, cosine]])
    lead_fwd = np.concatenate(two_parts(lead_fwd), 1)
    lead_inv = np.concatenate(two_parts(lead_inv), 0)
    high, low = two_parts(trail_fwd)
    trail_fwd = np.concatenate([high, high, low], 0)
    high, low = two_parts(trail_inv)
    trail_inv = np.concatenate([high, high, low], 0)
    twist = np.stack([np.cos(twist), -np.sin(twist)]).astype(np.float32)
    return lead_fwd, lead_inv, trail_fwd, trail_inv, twist


def dot(left, right):
    return jnp.dot(left, right, preferred_element_type=f32)


def split(value):
    high = value.astype(bf16)
    return high, (value - high.astype(f32)).astype(bf16)


def lead_stage(lead, twist, pair):
    rows = pair.shape[0]
    turned = dot(lead, jnp.concatenate([pair, pair], 0))
    real, imag = turned[:rows], turned[rows:]
    parts = []
    for side in range(2):
        lanes = slice(side * LANES, (side + 1) * LANES)
        re, im = real[:, lanes], imag[:, lanes]
        parts.append(
            jnp.concatenate([re * twist[0] - im * twist[1], re * twist[1] + im * twist[0]], 1)
        )
    return parts


def store_split(ref, place, value):
    high, low = split(value)
    width = value.shape[1]
    ref[place, :width] = high
    ref[place, width : 2 * width] = low
    ref[place, 2 * width :] = high


def spectrum_kernel(pieces, group, lead_ref, trail_ref, twist_ref, *refs):
    taps = refs[:pieces]
    out_ref, scratch, wide = refs[pieces:]
    sources, _, _, width = taps[0].shape
    count = pieces * sources
    for piece in range(pieces):
        for source in range(sources):
            row = (piece * sources + source) * group
            for part in range(width // LANES):
                lanes = slice(part * LANES, (part + 1) * LANES)
                scratch[part, row : row + group, :] = taps[piece][source, 0, :, lanes].astype(f32)
    lead, twist = lead_ref[...], (twist_ref[0], twist_ref[1])
    rows = count * (width // LANES)

    def channel(index):
        parts = [
            scratch[part, pl.ds(index, count, stride=group), :] for part in range(width // LANES)
        ]
        return jnp.concatenate(parts, 0).astype(bf16)

    for index in range(0, group, 2):
        pair = jnp.concatenate([channel(index), channel(index + 1)], 1)
        for side, value in enumerate(lead_stage(lead, twist, pair)):
            place = slice((index + side) * rows, (index + side + 1) * rows)
            store_split(wide, place, value)
    step = 4
    for index in range(0, group, step):
        product = dot(wide[index * rows : (index + step) * rows, :], trail_ref[...])
        out_ref[index : index + step] = product.reshape(step, rows, 2 * LANES)


def filter_spectrum(pieces, lead, trail, twist, group):
    sources, outer, inner, width = pieces[0].shape
    rows = lead.shape[1] // 2
    steps = inner // group
    whole = lambda ndim: (lambda *_: (0,) * ndim)
    return pl.pallas_call(
        functools.partial(spectrum_kernel, len(pieces), group),
        out_shape=jax.ShapeDtypeStruct((outer * inner, rows, 2 * LANES), f32),
        grid=(outer * steps,),
        in_specs=[
            pl.BlockSpec(lead.shape, whole(2)),
            pl.BlockSpec(trail.shape, whole(2)),
            pl.BlockSpec(twist.shape, whole(3)),
        ]
        + [
            pl.BlockSpec(
                (sources, 1, group, width), lambda step: (0, step // steps, step % steps, 0)
            )
        ]
        * len(pieces),
        out_specs=pl.BlockSpec((group, rows, 2 * LANES), lambda step: (step, 0, 0)),
        scratch_shapes=[
            pltpu.VMEM((width // LANES, len(pieces) * sources * group, LANES), f32),
            pltpu.VMEM((group * rows, 6 * LANES), bf16),
        ],
        compiler_params=pltpu.CompilerParams(vmem_limit_bytes=VMEM_BYTES),
        cost_estimate=pl.CostEstimate(
            flops=outer * inner * 10**6, bytes_accessed=2**20, transcendentals=0
        ),
        name="filter_spectrum",
    )(lead, trail, twist, *pieces)


def convolve_kernel(
    group, sources, lead_ref, inv_ref, trail_ref, back_ref, twist_ref, filter_ref, *refs
):
    signals, outs, (wide, spectra) = refs[:sources], refs[sources:-2], refs[-2:]
    local = signals[0].shape[2]
    rows = sources * local
    lead, inv, twist = lead_ref[...], inv_ref[...], (twist_ref[0], twist_ref[1])
    for index in range(group):
        pair = jnp.concatenate(
            [jnp.concatenate([ref[index, side] for ref in signals], 0) for side in range(2)], 1
        )
        for side, value in enumerate(lead_stage(lead, twist, pair)):
            place = slice((2 * index + side) * rows, (2 * index + side + 1) * rows)
            store_split(wide, place, value)
    for row in range(0, wide.shape[0], 512):
        spectra[row : row + 512, :] = dot(wide[row : row + 512, :], trail_ref[...])
    for index in range(group):
        fre, fim = filter_ref[index, :, :LANES], filter_ref[index, :, LANES:]
        for side in range(2):
            place = slice((2 * index + side) * rows, (2 * index + side + 1) * rows)
            re, im = spectra[place, :LANES], spectra[place, LANES:]
            if side == 0:
                product = jnp.concatenate([re * fre - im * fim, re * fim + im * fre], 1)
            else:
                product = jnp.concatenate([re * fre + im * fim, im * fre - re * fim], 1)
            store_split(wide, place, product)
    for row in range(0, wide.shape[0], 512):
        spectra[row : row + 512, :] = dot(wide[row : row + 512, :], back_ref[...])
    for index in range(group):
        reals, imags = [], []
        for side in range(2):
            place = slice((2 * index + side) * rows, (2 * index + side + 1) * rows)
            re, im = spectra[place, :LANES], spectra[place, LANES:]
            reals.append(re * twist[0] + im * twist[1])
            imags.append(im * twist[0] - re * twist[1])
        turned = jnp.concatenate([jnp.concatenate(reals, 1), jnp.concatenate(imags, 1)], 0)
        top, rest = split(turned)
        both = dot(inv, top)
        result = both[:rows] + both[rows:] + dot(inv[:rows], rest)
        result = result.astype(bf16)
        for side in range(2):
            lanes = slice(side * LANES, (side + 1) * LANES)
            for source in range(sources):
                value = result[source * local : (source + 1) * local, lanes]
                if len(outs[0].shape) == 5:
                    outs[0][source, index, side] = value
                else:
                    outs[source][index, side] = value


def convolve(signals, spectrum, tables, group, whole_out=False):
    lead_fwd, lead_inv, trail_fwd, trail_inv, twist = tables
    sources = len(signals)
    inner, _, local, _ = signals[0].shape
    rows = sources * local
    whole = lambda ndim: (lambda *_: (0,) * ndim)
    piece = pl.BlockSpec((group, 2, local, LANES), lambda step: (step, 0, 0, 0))
    if whole_out:
        out_shape = [jax.ShapeDtypeStruct((sources, inner, 2, local, LANES), bf16)]
        out_specs = [
            pl.BlockSpec((sources, group, 2, local, LANES), lambda step: (0, step, 0, 0, 0))
        ]
    else:
        out_shape = [jax.ShapeDtypeStruct((inner, 2, local, LANES), bf16)] * sources
        out_specs = [piece] * sources
    return pl.pallas_call(
        functools.partial(convolve_kernel, group, sources),
        out_shape=out_shape,
        grid=(inner // group,),
        in_specs=[
            pl.BlockSpec(lead_fwd.shape, whole(2)),
            pl.BlockSpec(lead_inv.shape, whole(2)),
            pl.BlockSpec(trail_fwd.shape, whole(2)),
            pl.BlockSpec(trail_inv.shape, whole(2)),
            pl.BlockSpec(twist.shape, whole(3)),
            pl.BlockSpec((group, rows, 2 * LANES), lambda step: (step, 0, 0)),
        ]
        + [piece] * sources,
        out_specs=out_specs,
        scratch_shapes=[
            pltpu.VMEM((2 * group * rows, 6 * LANES), bf16),
            pltpu.VMEM((2 * group * rows, 2 * LANES), f32),
        ],
        compiler_params=pltpu.CompilerParams(vmem_limit_bytes=VMEM_BYTES),
        cost_estimate=pl.CostEstimate(
            flops=inner * 10**6, bytes_accessed=2**20, transcendentals=0
        ),
        name="convolve",
    )(lead_fwd, lead_inv, trail_fwd, trail_inv, twist, spectrum, *signals)


def gate_kernel(me_ref, key_ref, value_ref, query_ref, grad_ref, *refs):
    outs, scratch = refs[:-1], refs[-1]
    tokens, width = key_ref.shape
    local = tokens // LANES
    pitch = scratch.shape[1] // local
    inner = outs[0].shape[0]
    dests = width // inner
    mine = lax.rem(me_ref[0], dests)
    for side, (one, two) in enumerate(((key_ref, value_ref), (grad_ref, query_ref))):
        for row in range(local):
            place = slice(row * LANES, (row + 1) * LANES)
            product = one[place, :].astype(f32) * two[place, :].astype(f32)
            scratch[side, row * pitch : row * pitch + width, :] = product.T
    for block in range(len(outs) // dests):

        @pl.when(pl.program_id(0) == block)
        def _():
            for slot in range(dests):
                base = (mine ^ slot) * inner
                for side in range(2):
                    for index in range(inner):
                        outs[block * dests + slot][index, side] = scratch[
                            side, pl.ds(base + index, local, stride=pitch), :
                        ].astype(bf16)


def gate(me, key_proj, value_proj, query_proj, out_grad, part, groups, inner):
    tokens = key_proj.shape[0]
    local = tokens // LANES
    dests = LANES // inner
    blocks = groups // dests
    column = pl.BlockSpec(
        (tokens, LANES), lambda step, me: (0, part * blocks + ((me[0] // dests) ^ step))
    )
    piece = (inner, 2, local, LANES)
    return pl.pallas_call(
        gate_kernel,
        out_shape=[jax.ShapeDtypeStruct(piece, bf16)] * groups,
        grid_spec=pltpu.PrefetchScalarGridSpec(
            num_scalar_prefetch=1,
            grid=(blocks,),
            in_specs=[column] * 4,
            out_specs=[pl.BlockSpec(piece, lambda step, me: (0, 0, 0, 0))] * groups,
            scratch_shapes=[pltpu.VMEM((2, local * (LANES + 8), LANES), f32)],
        ),
        compiler_params=pltpu.CompilerParams(vmem_limit_bytes=VMEM_BYTES),
        cost_estimate=pl.CostEstimate(flops=0, bytes_accessed=2**20, transcendentals=0),
        name="gate",
    )(me, key_proj, value_proj, query_proj, out_grad)


def finish_kernel(pieces_count, me_ref, skip_ref, key_ref, value_ref, query_ref, grad_ref, *refs):
    pieces = refs[:pieces_count]
    out_ref, query_out, key_out, value_out, scratch = refs[-5:]
    tokens, width = key_ref.shape
    local = tokens // LANES
    pitch = scratch.shape[1] // width
    inner = pieces[0].shape[-4]
    dests = width // inner
    mine = lax.rem(me_ref[0], dests)
    skip = skip_ref[...]
    if pieces_count == 1:
        for slot in range(dests):
            for side in range(2):
                for index in range(inner):
                    row = (slot * inner + index) * pitch
                    scratch[side, row : row + local, :] = pieces[0][slot, index, side].astype(f32)
    for block in range(pieces_count // dests):

        @pl.when(pl.program_id(0) == block)
        def _():
            for slot in range(dests):
                base = (mine ^ slot) * (inner * pitch)
                for side in range(2):
                    for index in range(inner):
                        scratch[side, pl.ds(base + index * pitch, local), :] = pieces[
                            block * dests + slot
                        ][index, side].astype(f32)

    for row in range(local):
        place = slice(row * LANES, (row + 1) * LANES)
        key, value = key_ref[place, :].astype(f32), value_ref[place, :].astype(f32)
        query, grad = query_ref[place, :].astype(f32), grad_ref[place, :].astype(f32)
        convolved = scratch[0, pl.ds(row, width, stride=pitch), :].T
        reflected = scratch[1, pl.ds(row, width, stride=pitch), :].T
        summed = convolved + skip * (key * value).astype(bf16).astype(f32)
        grad_sum = reflected + skip * (grad * query).astype(bf16).astype(f32)
        out_ref[place, :] = (query * summed).astype(bf16)
        query_out[place, :] = (grad * summed).astype(bf16)
        key_out[place, :] = (grad_sum * value).astype(bf16)
        value_out[place, :] = (grad_sum * key).astype(bf16)


def finish(me, skip, pieces, key_proj, value_proj, query_proj, out_grad, part, groups, previous):
    inner, _, local, _ = pieces[0].shape[-4:]
    tokens = key_proj.shape[0]
    dests = LANES // inner
    blocks = groups // dests
    whole = len(pieces) == 1

    def place(step, me):
        return 0, part * blocks + (step if whole else (me[0] // dests) ^ step)

    column = pl.BlockSpec((tokens, LANES), place)
    if whole:
        piece = pl.BlockSpec((dests, inner, 2, local, LANES), lambda step, me: (step, 0, 0, 0, 0))
    else:
        piece = pl.BlockSpec(pieces[0].shape, lambda step, me: (0, 0, 0, 0))
    return pl.pallas_call(
        functools.partial(finish_kernel, len(pieces)),
        out_shape=[jax.ShapeDtypeStruct(key_proj.shape, bf16)] * 4,
        grid_spec=pltpu.PrefetchScalarGridSpec(
            num_scalar_prefetch=1,
            grid=(blocks,),
            in_specs=[pl.BlockSpec((1, LANES), place)]
            + [column] * 4
            + [piece] * len(pieces)
            + [pl.BlockSpec(memory_space=pl.ANY)] * len(previous),
            out_specs=[column] * 4,
            scratch_shapes=[pltpu.VMEM((2, LANES * (local + 1), LANES), f32)],
        ),
        input_output_aliases={6 + len(pieces) + index: index for index in range(len(previous))},
        compiler_params=pltpu.CompilerParams(vmem_limit_bytes=VMEM_BYTES),
        cost_estimate=pl.CostEstimate(flops=0, bytes_accessed=2**20, transcendentals=0),
        name="finish",
    )(me, skip, key_proj, value_proj, query_proj, out_grad, *pieces, *previous)


def swap(value, axis="ctx"):
    return lax.all_to_all(value, axis, split_axis=0, concat_axis=0, tiled=True)


def tie(values, *others):
    return lax.optimization_barrier((values, others))[0]


def exchange(pieces, axis, order=None):
    count = len(pieces)
    taken = list(pieces)
    for step in order or range(1, count):
        taken[step] = lax.ppermute(pieces[step], axis, [(i, i ^ step) for i in range(count)])
    return taken


def fast_shards(query_proj, key_proj, value_proj, out_grad, long_filter, skip_gain, parts):
    groups, planes = lax.axis_size("ctx"), lax.axis_size("ch")
    tokens, width = key_proj.shape
    channels, taps = long_filter.shape
    rows = groups * tokens // LANES
    local, tiles = tokens // LANES, taps // LANES
    inner = width // (groups * parts)
    tables = make_tables(rows)
    lead_taps = tables[0].reshape(2 * rows, 2, planes * groups, tiles).transpose(0, 1, 3, 2)
    lead_taps = jnp.asarray(lead_taps.reshape(2 * rows, 2 * rows))
    lead_fwd, lead_inv, trail_fwd, trail_inv, twist = (jnp.asarray(table) for table in tables)
    me = lax.axis_index("ctx")
    place = jnp.full((1,), me, jnp.int32)

    sources = jnp.arange(groups) ^ me
    lead = jnp.take(lead_fwd.reshape(2 * rows, 2, groups, local), sources, axis=2)
    lead = lead.reshape(lead_fwd.shape)
    back = jnp.take(lead_inv.reshape(2, groups, local, 2 * rows), sources, axis=1)
    back = back.reshape(lead_inv.shape)

    skip = skip_gain.reshape(1, width)
    shaped = long_filter.reshape(planes, parts, groups, inner, taps)
    gates = [
        gate(place, key_proj, value_proj, query_proj, out_grad, part, groups, inner)
        for part in range(parts)
    ]
    late = (1,)

    slabs = [shaped[:, 0]] + [tie(shaped, gates[0])[:, part] for part in range(1, parts)]

    def send_filter(part, *others):
        slab = slabs[part].reshape(planes * groups, inner, taps)
        return swap(tie(slab, *others), ("ch", "ctx"))

    filters = send_filter(0)
    signals = exchange(gates[0], "ctx")
    outputs = []
    for part in range(parts):
        last = part == parts - 1
        if not last:
            following = send_filter(part + 1, filters, signals, gates[part + 1])
            early = [step for step in range(groups) if step not in late]
            pieces = tie(gates[part + 1], filters, signals)
            coming = exchange(pieces, "ctx", early)
        spectrum = filter_spectrum([filters[:, None]], lead_taps, trail_fwd, twist, TILE)
        tables = (lead, back if last else lead_inv, trail_fwd, trail_inv, twist)
        conv = convolve(signals, spectrum, tables, TILE, not last)
        if last:
            taken = exchange(conv, "ctx")
        else:
            for step in late:
                coming[step] = tie(pieces[step], conv[0])
            rest = exchange(coming, "ctx", late)
            coming = [rest[step] if step in late else coming[step] for step in range(groups)]
            conv, following, coming = lax.optimization_barrier((conv[0], following, coming))
            taken = [swap(conv)]
            filters, signals = following, coming
        outputs = finish(
            place, skip, taken, key_proj, value_proj, query_proj, out_grad, part, groups, outputs
        )
    return tuple(outputs)


def plain_shards(query_proj, key_proj, value_proj, out_grad, long_filter, skip_gain):
    groups, planes = lax.axis_size("ctx"), lax.axis_size("ch")
    tokens, width = key_proj.shape
    channels, taps = long_filter.shape
    inner = width // groups
    length = groups * tokens
    rows = length // LANES
    tables = tuple(jnp.asarray(table) for table in make_tables(rows))
    group = 2 if inner % 2 == 0 else 1
    sent = long_filter.reshape(planes, groups, inner, taps).transpose(1, 0, 2, 3)
    taken = swap(swap(sent).transpose(1, 0, 2, 3), "ch")
    filters = taken.transpose(2, 0, 1, 3).reshape(inner, rows, LANES)
    lead, twist = tables[0].astype(f32), tables[4]
    lead = lead[:, :rows] + lead[:, rows:]
    trail = tables[2].astype(f32)[2 * LANES :]
    trail = trail[: 2 * LANES] + trail[2 * LANES :]
    highest = lax.Precision.HIGHEST
    turned = jnp.einsum("kn,cnm->ckm", lead, filters.astype(f32), precision=highest)
    real, imag = turned[:, :rows], turned[:, rows:]
    turned = jnp.concatenate(
        [real * twist[0] - imag * twist[1], real * twist[1] + imag * twist[0]], 2
    )
    spectrum = jnp.einsum("ckm,mj->ckj", turned, trail, precision=highest)
    gated_kv = (key_proj.astype(f32) * value_proj.astype(f32)).astype(bf16)
    grad_gate = (out_grad.astype(f32) * query_proj.astype(f32)).astype(bf16)
    both = jnp.stack([gated_kv.T, grad_gate.T], 1)
    taken = swap(both.reshape(groups, inner, 2, tokens))
    signals = taken.transpose(1, 2, 0, 3).reshape(inner, 2, rows, LANES)
    (conv,) = convolve([signals], spectrum, tables, group)
    back = conv.reshape(inner, 2, groups, tokens).transpose(2, 0, 1, 3)
    back = swap(back).reshape(width, 2, tokens)
    convolved, reflected = back[:, 0].T, back[:, 1].T
    summed = convolved.astype(f32) + skip_gain[None, :] * gated_kv.astype(f32)
    grad_sum = reflected.astype(f32) + skip_gain[None, :] * grad_gate.astype(f32)
    return (
        (query_proj.astype(f32) * summed).astype(bf16),
        (out_grad.astype(f32) * summed).astype(bf16),
        (grad_sum * value_proj.astype(f32)).astype(bf16),
        (grad_sum * key_proj.astype(f32)).astype(bf16),
    )


def shards(query_proj, key_proj, value_proj, out_grad, long_filter, skip_gain):
    groups = lax.axis_size("ctx")
    tokens, width = key_proj.shape
    planes = lax.axis_size("ch")
    taps = long_filter.shape[1]
    args = (query_proj, key_proj, value_proj, out_grad, long_filter, skip_gain)
    parts = 2
    inner = width // (groups * parts)
    fits = (
        tokens % (TILE * LANES) == 0
        and taps % LANES == 0
        and width % (groups * parts) == 0
        and inner % TILE == 0
        and LANES % inner == 0
        and groups % (LANES // inner) == 0
        and planes & (planes - 1) == 0
        and groups & (groups - 1) == 0
    )
    if fits:
        return fast_shards(*args, parts)
    return plain_shards(*args)


def solution(mesh):
    placed = (
        P("ctx", "ch"),
        P("ctx", "ch"),
        P("ctx", "ch"),
        P("ctx", "ch"),
        P(None, ("ch", "ctx")),
        P("ch"),
    )
    return jax.shard_map(
        shards,
        mesh=mesh,
        in_specs=placed,
        out_specs=(P("ctx", "ch"), P("ctx", "ch"), P("ctx", "ch"), P("ctx", "ch")),
        check_vma=False,
    )
```

time: 293 us -> 267 us (0.911)
  Pallas kernels: 120 us -> 105 us
  waiting for transfers between devices: 124 us -> 116 us
  local copies, waits for them, and re-layouts: 13.3 us -> 7.57 us
  starting transfers between devices: 33.3 us -> 36.8 us
    all_to_all x5 -> x3, waiting for transfers between devices: 87.1 us -> 0.01 us  [swap(): return lax.all_to_all(value, axis, split_axis=0, concat_axis=0, tiled=True)]
    ppermute x6 -> x22, waiting for transfers between devices: 37.1 us -> 116 us  [exchange(): lax.ppermute(pieces[step], axis, [(i, i ^ step) for i in range(count)])]
    pallas_call x6, Pallas kernels: 101 us -> 86.5 us  [the longest x2 49.8 us: convolve(): pl.pallas_call(functools.partial(convolve_kernel, group, sources), out_sh...]
    ppermute x6 -> x22, starting transfers between devices: 9.3 us -> 21 us  [exchange(): lax.ppermute(pieces[step], axis, [(i, i ^ step) for i in range(count)])]
    all_to_all x5 -> x3, starting transfers between devices: 24 us -> 15.8 us  [swap(): return lax.all_to_all(value, axis, split_axis=0, concat_axis=0, tiled=True)]
    transpose x1 -> x0, local copies, waits for them, and re-layouts: 4.7 us -> none  [fast_shards(): long_filter.reshape(planes, parts, groups, inner, taps)]
  transfers between devices with their start and end apart: 11 -> 25, of which waited for: 5 -> 11; matrix products, arithmetic and copies ran while one was open for 2% -> 2% of each run, Pallas kernels for 37% -> 35%
where the time goes in v2:
time: 267 us
  waiting for transfers between devices  116 us (43%)
  Pallas kernels  105 us (39%)
  starting transfers between devices  36.8 us (14%)
  local copies, waits for them, and re-layouts  7.57 us (3%)
    ppermute x22, waiting for transfers between devices, exchange(): lax.ppermute(pieces[step], axis, [(i, i ^ step) for i in range(count)])  116 us
    pallas_call x2, Pallas kernels, convolve(): pl.pallas_call(functools.partial(convolve_kernel, group, sources), out_sh...  49.8 us
    ppermute x22, starting transfers between devices, exchange(): lax.ppermute(pieces[step], axis, [(i, i ^ step) for i in range(count)])  21 us
    pallas_call x2, Pallas kernels, finish(): pl.pallas_call(functools.partial(finish_kernel, len(pieces)), out_shape=[...  19.8 us
    pallas_call x2, Pallas kernels, filter_spectrum(): pl.pallas_call(functools.partial(spectrum_kernel, len(pieces), group), ou...  18.3 us
    pallas_call x2, Pallas kernels, gate(): pl.pallas_call(gate_kernel, out_shape=[jax.ShapeDtypeStruct(piece, bf16)]...  16.9 us
    all_to_all x3, starting transfers between devices, swap(): return lax.all_to_all(value, axis, split_axis=0, concat_axis=0, tiled=True)  15.8 us
  transfers between devices with their start and end apart: 25, of which 11 were waited for; matrix products, arithmetic and copies ran while one was open for 2% of the time, Pallas kernels for 35%

profile of v2, /device:TPU:0, one launch (start us, length us, event | category | flops | bytes accessed | tf_op | source)
XLA Modules:
  0.0 266.8 jit_solution(2957866552625430374)
XLA Ops:
  0.6 3.1 %slice.12 = bf16[4,1,8,64,512]{4,3,2,1,0:T(8,128)(2,1)} slice(bf16[4,2,8,64,512]{4,3,2,1,0:T(8,128)(2,1)} %bitcast.17), slice={[0:4], [0:1], [0:8], [0:64], [0:512]} | slice | bytes 4194304 | tf_op jit(solution)/shard_map/slice | solution.py:407
  3.8 7.3 %all-to-all-start = ((bf16[32,64,512]{2,1,0:T(8,128)(2,1)}), bf16[32,64,512]{2,1,0:T(8,128)(2,1)S(1)}, u32[]{:S(2)}, u32[]{:S(2)}) async-start(bf16[32,64,512]{2,1,0:T(8,128)(2,1)} %bitcast.8), calls=%async_computation | async-start | bytes 4194304 | tf_op jit(solution)/shard_map/all_to_all | solution.py:364
  11.1 8.3 %gate.2 = (bf16[64,2,16,128]{3,2,1,0:T(8,128)(2,1)}, bf16[64,2,16,128]{3,2,1,0:T(8,128)(2,1)}, bf16[64,2,16,128]{3,2,1,0:T(8,128)(2,1)}, bf16[64,2,16,128]{3,2,1...) custom-call(s32[1]{0:T(128)} %bitcast.me_ref, ...), custom_call_target="tpu_custom_call" | custom-call | bytes 1048576 | tf_op jit(solution)/shard_map/gate/pallas_call | solution.py:270
  19.6 1.7 collective-permute-start.1
  21.3 1.7 collective-permute-start.3
  23.1 2.6 collective-permute-start.5
  25.7 19.6 %collective-permute-done.1.refs_2_ = bf16[64,2,16,128]{3,2,1,0:T(8,128)(2,1)S(1)} collective-permute-done((bf16[64,2,16,128]{3,2,1,0:T(8,128)(2,1)}, bf16[64,2,16,128]{3,2,1,0:T(8,128)(2,1)S(1)}, u32[]{:S(2)}, u32[]{:S(2)}) %collective-permute-start.1) | collective-permute-done | bytes 524320 | tf_op jit(solution)/shard_map/ppermute | solution.py:375
  45.6 8.6 %gate.3 = (bf16[64,2,16,128]{3,2,1,0:T(8,128)(2,1)}, bf16[64,2,16,128]{3,2,1,0:T(8,128)(2,1)}, bf16[64,2,16,128]{3,2,1,0:T(8,128)(2,1)}, bf16[64,2,16,128]{3,2,1...) custom-call(s32[1]{0:T(128)} %bitcast.me_ref, ...), custom_call_target="tpu_custom_call" | custom-call | bytes 1048576 | tf_op jit(solution)/shard_map/gate/pallas_call | solution.py:270
  54.8 1.5 slice.13
  56.3 2.8 %collective-permute-done.2.refs_3_ = bf16[64,2,16,128]{3,2,1,0:T(8,128)(2,1)S(1)} collective-permute-done((bf16[64,2,16,128]{3,2,1,0:T(8,128)(2,1)}, bf16[64,2,16,128]{3,2,1,0:T(8,128)(2,1)S(1)}, u32[]{:S(2)}, u32[]{:S(2)}) %collective-permute-start.2) | collective-permute-done | bytes 524320 | tf_op jit(solution)/shard_map/ppermute | solution.py:375
  59.1 24.0 %collective-permute-done.4.refs_5_ = bf16[64,2,16,128]{3,2,1,0:T(8,128)(2,1)} collective-permute-done((bf16[64,2,16,128]{3,2,1,0:T(8,128)(2,1)}, bf16[64,2,16,128]{3,2,1,0:T(8,128)(2,1)}, u32[]{:S(2)}, u32[]{:S(2)}) %collective-permute-start.4) | collective-permute-done | bytes 524320 | tf_op jit(solution)/shard_map/ppermute | solution.py:375
  83.1 3.7 %all-to-all-start.1 = ((bf16[32,64,512]{2,1,0:T(8,128)(2,1)}), bf16[32,64,512]{2,1,0:T(8,128)(2,1)}, u32[]{:S(2)}, u32[]{:S(2)}) async-start(bf16[32,64,512]{2,1,0:T(8,128)(2,1)} %bitcast.10), calls=%async_computation.1 | async-start | bytes 4194304 | tf_op jit(solution)/shard_map/all_to_all | solution.py:364
  87.9 1.4 collective-permute-start.9
  91.6 1.5 collective-permute-start.11
  93.7 9.1 %filter_spectrum.2.filter_ref = f32[64,128,256]{2,1,0:T(8,128)} custom-call(bf16[256,256]{1,0:T(8,128)(2,1)} %constant.46.clone.lead_ref, bf16[768,256]{1,0:T(8,128)(2,1)} %constant.49.clone.trail_ref, f32[2,128,128]{2,1,0:T(8,128)} %constant.51.clone.twist_ref, bf16[32,1,64,512]{3,2,1,0:T(8,128)(2,1)} %bitcast.19), custom_call_target="tpu_custom_call" | custom-call | flops 64000000 | bytes 1048576 | tf_op jit(solution)/shard_map/filter_spectrum/pallas_call | solution.py:116
  102.8 25.0 %convolve.2 = bf16[8,64,2,16,128]{4,3,2,1,0:T(8,128)(2,1)} custom-call(bf16[256,256]{1,0:T(8,128)(2,1)} %get-tuple-element.103.lead_ref, bf16[256,256]{1,0:T(8,128)(2,1)} %constant.48.clone.inv_ref, bf16[768,256]{1,0:T(8,128)(2,1)} %constant.49.clone.trail_ref, bf16[768,256]{1,0:T(8,128)(2,1)} %constant.50.clone.back_ref, ...), custom_call_target="tpu_custom_call" | custom-call | flops 64000000 | bytes 1048576 | tf_op jit(solution)/shard_map/convolve/pallas_call | solution.py:209
  127.8 2.4 collective-permute-start.13
  130.3 3.6 %collective-permute-done.10.refs_3_ = bf16[64,2,16,128]{3,2,1,0:T(8,128)(2,1)} collective-permute-done((bf16[64,2,16,128]{3,2,1,0:T(8,128)(2,1)}, bf16[64,2,16,128]{3,2,1,0:T(8,128)(2,1)}, u32[]{:S(2)}, u32[]{:S(2)}) %collective-permute-start.10) | collective-permute-done | bytes 524320 | tf_op jit(solution)/shard_map/ppermute | solution.py:375
  134.7 12.2 %collective-permute-done.13.refs_6_ = bf16[64,2,16,128]{3,2,1,0:T(8,128)(2,1)S(1)} collective-permute-done((bf16[64,2,16,128]{3,2,1,0:T(8,128)(2,1)S(1)}, bf16[64,2,16,128]{3,2,1,0:T(8,128)(2,1)S(1)}, u32[]{:S(2)}, u32[]{:S(2)}) %collective-permute-start.13) | collective-permute-done | bytes 524320 | tf_op jit(solution)/shard_map/ppermute | solution.py:375
  146.9 10.3 %collective-permute-done.14.refs_7_ = bf16[64,2,16,128]{3,2,1,0:T(8,128)(2,1)S(1)} collective-permute-done((bf16[64,2,16,128]{3,2,1,0:T(8,128)(2,1)S(1)}, bf16[64,2,16,128]{3,2,1,0:T(8,128)(2,1)S(1)}, u32[]{:S(2)}, u32[]{:S(2)}) %collective-permute-start.14) | collective-permute-done | bytes 524320 | tf_op jit(solution)/shard_map/ppermute | solution.py:375
  158.1 4.8 %all-to-all-start.2 = ((bf16[8,64,2,16,128]{4,3,2,1,0:T(8,128)(2,1)}), bf16[8,64,2,16,128]{4,3,2,1,0:T(8,128)(2,1)}, u32[]{:S(2)}, u32[]{:S(2)}) async-start(bf16[8,64,2,16,128]{4,3,2,1,0:T(8,128)(2,1)} %convolve.2), calls=%async_computation.2 | async-start | bytes 8388608 | tf_op jit(solution)/shard_map/all_to_all | solution.py:364
  162.9 9.2 %filter_spectrum.3.filter_ref = f32[64,128,256]{2,1,0:T(8,128)} custom-call(bf16[256,256]{1,0:T(8,128)(2,1)} %constant.46.clone.lead_ref, bf16[768,256]{1,0:T(8,128)(2,1)} %constant.49.clone.trail_ref, f32[2,128,128]{2,1,0:T(8,128)} %constant.51.clone.twist_ref, bf16[32,1,64,512]{3,2,1,0:T(8,128)(2,1)} %bitcast.11.refs_0_), custom_call_target="tpu_custom_call" | custom-call | flops 64000000 | bytes 1048576 | tf_op jit(solution)/shard_map/filter_spectrum/pallas_call | solution.py:116
  172.1 24.8 %convolve.3 = (bf16[64,2,16,128]{3,2,1,0:T(8,128)(2,1)}, bf16[64,2,16,128]{3,2,1,0:T(8,128)(2,1)}, bf16[64,2,16,128]{3,2,1,0:T(8,128)(2,1)}, bf16[64,2,16,128]{3...) custom-call(bf16[256,256]{1,0:T(8,128)(2,1)} %get-tuple-element.103., ...), custom_call_target="tpu_custom_call" | custom-call | flops 64000000 | bytes 1048576 | tf_op jit(solution)/shard_map/convolve/pallas_call | solution.py:209
  197.2 1.6 collective-permute-start.16
  198.9 1.6 collective-permute-start.18
  200.7 2.5 collective-permute-start.20
  203.2 19.3 %collective-permute-done.16.refs_2_ = bf16[64,2,16,128]{3,2,1,0:T(8,128)(2,1)S(1)} collective-permute-done((bf16[64,2,16,128]{3,2,1,0:T(8,128)(2,1)}, bf16[64,2,16,128]{3,2,1,0:T(8,128)(2,1)S(1)}, u32[]{:S(2)}, u32[]{:S(2)}) %collective-permute-start.16) | collective-permute-done | bytes 524320 | tf_op jit(solution)/shard_map/ppermute | solution.py:375
  222.8 9.6 %finish.2 = (bf16[2048,1024]{1,0:T(8,128)(2,1)}, bf16[2048,1024]{1,0:T(8,128)(2,1)}, bf16[2048,1024]{1,0:T(8,128)(2,1)}, bf16[2048,1024]{1,0:T(8,128)(2,1)}) custom-call(s32[1]{0:T(128)} %bitcast.me_ref, f32[1,1024]{1,0:T(1,128)} %bitcast.22, bf16[2048,1024]{1,0:T(8,128)(2,1)} %key_ref.7, bf16[2048,1024]{1,0:T(8,128)(2,1)} %value_ref.7, ...), custom_call_target="tpu_custom_call" | custom-call | bytes 1048576 | tf_op jit(solution)/shard_map/finish/pallas_call | solution.py:343
  232.8 1.7 collective-permute-done.19.refs_5_
  234.5 11.4 %collective-permute-done.20.refs_6_ = bf16[64,2,16,128]{3,2,1,0:T(8,128)(2,1)S(1)} collective-permute-done((bf16[64,2,16,128]{3,2,1,0:T(8,128)(2,1)}, bf16[64,2,16,128]{3,2,1,0:T(8,128)(2,1)S(1)}, u32[]{:S(2)}, u32[]{:S(2)}) %collective-permute-start.20) | collective-permute-done | bytes 524320 | tf_op jit(solution)/shard_map/ppermute | solution.py:375
  246.0 10.4 %collective-permute-done.21.refs_7_ = bf16[64,2,16,128]{3,2,1,0:T(8,128)(2,1)} collective-permute-done((bf16[64,2,16,128]{3,2,1,0:T(8,128)(2,1)}, bf16[64,2,16,128]{3,2,1,0:T(8,128)(2,1)}, u32[]{:S(2)}, u32[]{:S(2)}) %collective-permute-start.21) | collective-permute-done | bytes 524320 | tf_op jit(solution)/shard_map/ppermute | solution.py:375
  256.4 10.2 %finish.3 = (bf16[2048,1024]{1,0:T(8,128)(2,1)}, bf16[2048,1024]{1,0:T(8,128)(2,1)}, bf16[2048,1024]{1,0:T(8,128)(2,1)}, bf16[2048,1024]{1,0:T(8,128)(2,1)}) custom-call(s32[1]{0:T(128)} %bitcast.me_ref, f32[1,1024]{1,0:T(1,128)} %bitcast.23, ...), custom_call_target="tpu_custom_call", output_to_operand_aliasing={{0}: (14, {}), {1}: (15, {}), {2}: (16, {}), {3}: (17, {})} | custom-call | bytes 1048576 | tf_op jit(solution)/shard_map/finish/pallas_call | solution.py:343
  (82 shorter events, 8.1 us)
Async XLA Ops:
  3.8 79.4 %all-to-all-start = ((bf16[32,64,512]{2,1,0:T(8,128)(2,1)}), bf16[32,64,512]{2,1,0:T(8,128)(2,1)S(1)}, u32[]{:S(2)}, u32[]{:S(2)}) async-start(bf16[32,64,512]{2,1,0:T(8,128)(2,1)} %bitcast.8), calls=%async_computation | async-start | bytes 4194304 | tf_op jit(solution)/shard_map/all_to_all | solution.py:364
  19.3 3.7 %collective-permute-start = (bf16[64,2,16,128]{3,2,1,0:T(8,128)(2,1)}, bf16[64,2,16,128]{3,2,1,0:T(8,128)(2,1)S(1)}, u32[]{:S(2)}, u32[]{:S(2)}) collective-permute-start(bf16[64,2,16,128]{3,2,1,0:T(8,128)(2,1)} %get-tuple-element.54), channel_id=1, source_target_pairs={{0,4},{4,0},{8,12},{12,8},{16,20},{20,16},{24,28},{28,24},{1,5},{5... | collective-permute-start | bytes 1572872 | tf_op jit(solution)/shard_map/ppermute | solution.py:375
  19.6 25.6 %collective-permute-start.1 = (bf16[64,2,16,128]{3,2,1,0:T(8,128)(2,1)}, bf16[64,2,16,128]{3,2,1,0:T(8,128)(2,1)S(1)}, u32[]{:S(2)}, u32[]{:S(2)}) collective-permute-start(bf16[64,2,16,128]{3,2,1,0:T(8,128)(2,1)} %get-tuple-element.55), channel_id=1, source_target_pairs={{0,8},{4,12},{8,0},{12,4},{16,24},{20,28},{24,16},{28,20},{1,9},{5... | collective-permute-start | bytes 1572872 | tf_op jit(solution)/shard_map/ppermute | solution.py:375
  21.3 37.8 %collective-permute-start.2 = (bf16[64,2,16,128]{3,2,1,0:T(8,128)(2,1)}, bf16[64,2,16,128]{3,2,1,0:T(8,128)(2,1)S(1)}, u32[]{:S(2)}, u32[]{:S(2)}) collective-permute-start(bf16[64,2,16,128]{3,2,1,0:T(8,128)(2,1)} %get-tuple-element.56), channel_id=1, source_target_pairs={{0,12},{4,8},{8,4},{12,0},{16,28},{20,24},{24,20},{28,16},{1,13},{... | collective-permute-start | bytes 1572872 | tf_op jit(solution)/shard_map/ppermute | solution.py:375
  21.3 37.8 %collective-permute-start.3 = (bf16[64,2,16,128]{3,2,1,0:T(8,128)(2,1)}, bf16[64,2,16,128]{3,2,1,0:T(8,128)(2,1)}, u32[]{:S(2)}, u32[]{:S(2)}) collective-permute-start(bf16[64,2,16,128]{3,2,1,0:T(8,128)(2,1)} %get-tuple-element.57), channel_id=1, source_target_pairs={{0,16},{4,20},{8,24},{12,28},{16,0},{20,4},{24,8},{28,12},{1,17},{... | collective-permute-start | bytes 1572872 | tf_op jit(solution)/shard_map/ppermute | solution.py:375
  23.0 60.1 %collective-permute-start.4 = (bf16[64,2,16,128]{3,2,1,0:T(8,128)(2,1)}, bf16[64,2,16,128]{3,2,1,0:T(8,128)(2,1)}, u32[]{:S(2)}, u32[]{:S(2)}) collective-permute-start(bf16[64,2,16,128]{3,2,1,0:T(8,128)(2,1)} %get-tuple-element.58), channel_id=1, source_target_pairs={{0,20},{4,16},{8,28},{12,24},{16,4},{20,0},{24,12},{28,8},{1,21},{... | collective-permute-start | bytes 1572872 | tf_op jit(solution)/shard_map/ppermute | solution.py:375
  23.1 31.2 %copy-start.9 = (bf16[64,2,16,128]{3,2,1,0:T(8,128)(2,1)}, bf16[64,2,16,128]{3,2,1,0:T(8,128)(2,1)S(1)}, u32[]{:S(2)}) copy-start(bf16[64,2,16,128]{3,2,1,0:T(8,128)(2,1)S(1)} %collective-permute-done.refs_1_) | copy-start | bytes 1572868
  23.1 60.0 %collective-permute-start.5 = (bf16[64,2,16,128]{3,2,1,0:T(8,128)(2,1)}, bf16[64,2,16,128]{3,2,1,0:T(8,128)(2,1)}, u32[]{:S(2)}, u32[]{:S(2)}) collective-permute-start(bf16[64,2,16,128]{3,2,1,0:T(8,128)(2,1)} %get-tuple-element.59), channel_id=1, source_target_pairs={{0,24},{4,28},{8,16},{12,20},{16,8},{20,12},{24,0},{28,4},{1,25},{... | collective-permute-start | bytes 1572872 | tf_op jit(solution)/shard_map/ppermute | solution.py:375
  45.2 37.9 %collective-permute-start.6 = (bf16[64,2,16,128]{3,2,1,0:T(8,128)(2,1)}, bf16[64,2,16,128]{3,2,1,0:T(8,128)(2,1)}, u32[]{:S(2)}, u32[]{:S(2)}) collective-permute-start(bf16[64,2,16,128]{3,2,1,0:T(8,128)(2,1)} %get-tuple-element.60), channel_id=1, source_target_pairs={{0,28},{4,24},{8,20},{12,16},{16,12},{20,8},{24,4},{28,0},{1,29},{... | collective-permute-start | bytes 1572872 | tf_op jit(solution)/shard_map/ppermute | solution.py:375
  54.8 34.8 %copy-start.17 = (bf16[2,8,16,256]{3,2,1,0:T(8,128)(2,1)S(1)}, bf16[2,8,16,256]{3,2,1,0:T(8,128)(2,1)}, u32[]{:S(2)}) copy-start(bf16[2,8,16,256]{3,2,1,0:T(8,128)(2,1)} %constant.53) | copy-start | bytes 393220
  54.8 35.4 %copy-start.1 = (bf16[256,2,8,16]{0,3,2,1:T(8,128)(2,1)S(1)}, bf16[256,2,8,16]{0,3,2,1:T(8,128)(2,1)}, u32[]{:S(2)}) copy-start(bf16[256,2,8,16]{0,3,2,1:T(8,128)(2,1)} %constant.52) | copy-start | bytes 393220
  83.1 74.0 %all-to-all-start.1 = ((bf16[32,64,512]{2,1,0:T(8,128)(2,1)}), bf16[32,64,512]{2,1,0:T(8,128)(2,1)}, u32[]{:S(2)}, u32[]{:S(2)}) async-start(bf16[32,64,512]{2,1,0:T(8,128)(2,1)} %bitcast.10), calls=%async_computation.1 | async-start | bytes 4194304 | tf_op jit(solution)/shard_map/all_to_all | solution.py:364
  86.9 40.9 %collective-permute-start.7 = (bf16[64,2,16,128]{3,2,1,0:T(8,128)(2,1)}, bf16[64,2,16,128]{3,2,1,0:T(8,128)(2,1)S(1)}, u32[]{:S(2)}, u32[]{:S(2)}) collective-permute-start(bf16[64,2,16,128]{3,2,1,0:T(8,128)(2,1)} %get-tuple-element.71), channel_id=1, source_target_pairs={{0,0},{4,4},{8,8},{12,12},{16,16},{20,20},{24,24},{28,28},{1,1},{5... | collective-permute-start | bytes 1572872 | tf_op jit(solution)/shard_map/ppermute | solution.py:375
  87.9 42.3 %collective-permute-start.9 = (bf16[64,2,16,128]{3,2,1,0:T(8,128)(2,1)}, bf16[64,2,16,128]{3,2,1,0:T(8,128)(2,1)S(1)}, u32[]{:S(2)}, u32[]{:S(2)}) collective-permute-start(bf16[64,2,16,128]{3,2,1,0:T(8,128)(2,1)} %get-tuple-element.74), channel_id=1, source_target_pairs={{0,8},{4,12},{8,0},{12,4},{16,24},{20,28},{24,16},{28,20},{1,9},{5... | collective-permute-start | bytes 1572872 | tf_op jit(solution)/shard_map/ppermute | solution.py:375
  89.3 44.5 %collective-permute-start.10 = (bf16[64,2,16,128]{3,2,1,0:T(8,128)(2,1)}, bf16[64,2,16,128]{3,2,1,0:T(8,128)(2,1)}, u32[]{:S(2)}, u32[]{:S(2)}) collective-permute-start(bf16[64,2,16,128]{3,2,1,0:T(8,128)(2,1)} %get-tuple-element.75), channel_id=1, source_target_pairs={{0,12},{4,8},{8,4},{12,0},{16,28},{20,24},{24,20},{28,16},{1,13},{... | collective-permute-start | bytes 1572872 | tf_op jit(solution)/shard_map/ppermute | solution.py:375
  91.6 43.1 %collective-permute-start.11 = (bf16[64,2,16,128]{3,2,1,0:T(8,128)(2,1)}, bf16[64,2,16,128]{3,2,1,0:T(8,128)(2,1)}, u32[]{:S(2)}, u32[]{:S(2)}) collective-permute-start(bf16[64,2,16,128]{3,2,1,0:T(8,128)(2,1)} %get-tuple-element.76), channel_id=1, source_target_pairs={{0,16},{4,20},{8,24},{12,28},{16,0},{20,4},{24,8},{28,12},{1,17},{... | collective-permute-start | bytes 1572872 | tf_op jit(solution)/shard_map/ppermute | solution.py:375
  93.1 41.6 %collective-permute-start.12 = (bf16[64,2,16,128]{3,2,1,0:T(8,128)(2,1)}, bf16[64,2,16,128]{3,2,1,0:T(8,128)(2,1)}, u32[]{:S(2)}, u32[]{:S(2)}) collective-permute-start(bf16[64,2,16,128]{3,2,1,0:T(8,128)(2,1)} %get-tuple-element.77), channel_id=1, source_target_pairs={{0,20},{4,16},{8,28},{12,24},{16,4},{20,0},{24,12},{28,8},{1,21},{... | collective-permute-start | bytes 1572872 | tf_op jit(solution)/shard_map/ppermute | solution.py:375
  102.8 27.4 %copy-start.19 = (bf16[64,2,16,128]{3,2,1,0:T(8,128)(2,1)S(1)}, bf16[64,2,16,128]{3,2,1,0:T(8,128)(2,1)}, u32[]{:S(2)}) copy-start(bf16[64,2,16,128]{3,2,1,0:T(8,128)(2,1)} %get-tuple-element.79) | copy-start | bytes 1572868
  102.8 31.1 %copy-start.18 = (bf16[64,2,16,128]{3,2,1,0:T(8,128)(2,1)S(1)}, bf16[64,2,16,128]{3,2,1,0:T(8,128)(2,1)}, u32[]{:S(2)}) copy-start(bf16[64,2,16,128]{3,2,1,0:T(8,128)(2,1)} %get-tuple-element.73) | copy-start | bytes 1572868
  127.8 29.4 %copy-start.12 = (bf16[64,2,16,128]{3,2,1,0:T(8,128)(2,1)}, bf16[64,2,16,128]{3,2,1,0:T(8,128)(2,1)S(1)}, u32[]{:S(2)}) copy-start(bf16[64,2,16,128]{3,2,1,0:T(8,128)(2,1)S(1)} %collective-permute-done.7.refs_0_) | copy-start | bytes 1572868
  127.8 19.1 %collective-permute-start.13 = (bf16[64,2,16,128]{3,2,1,0:T(8,128)(2,1)S(1)}, bf16[64,2,16,128]{3,2,1,0:T(8,128)(2,1)S(1)}, u32[]{:S(2)}, u32[]{:S(2)}) collective-permute-start(bf16[64,2,16,128]{3,2,1,0:T(8,128)(2,1)S(1)} %copy-done.20), channel_id=1, source_target_pairs={{0,24},{4,28},{8,16},{12,20},{16,8},{20,12},{24,0},{28,4},{1,25},{... | collective-permute-start | bytes 1572872 | tf_op jit(solution)/shard_map/ppermute | solution.py:375
  130.2 27.0 %collective-permute-start.14 = (bf16[64,2,16,128]{3,2,1,0:T(8,128)(2,1)S(1)}, bf16[64,2,16,128]{3,2,1,0:T(8,128)(2,1)S(1)}, u32[]{:S(2)}, u32[]{:S(2)}) collective-permute-start(bf16[64,2,16,128]{3,2,1,0:T(8,128)(2,1)S(1)} %copy-done.19), channel_id=1, source_target_pairs={{0,28},{4,24},{8,20},{12,16},{16,12},{20,8},{24,4},{28,0},{1,29},{... | collective-permute-start | bytes 1572872 | tf_op jit(solution)/shard_map/ppermute | solution.py:375
  133.9 23.3 %collective-permute-start.8 = (bf16[64,2,16,128]{3,2,1,0:T(8,128)(2,1)S(1)}, bf16[64,2,16,128]{3,2,1,0:T(8,128)(2,1)S(1)}, u32[]{:S(2)}, u32[]{:S(2)}) collective-permute-start(bf16[64,2,16,128]{3,2,1,0:T(8,128)(2,1)S(1)} %copy-done.18), channel_id=1, source_target_pairs={{0,4},{4,0},{8,12},{12,8},{16,20},{20,16},{24,28},{28,24},{1,5},{5... | collective-permute-start | bytes 1572872 | tf_op jit(solution)/shard_map/ppermute | solution.py:375
  158.1 64.7 %all-to-all-start.2 = ((bf16[8,64,2,16,128]{4,3,2,1,0:T(8,128)(2,1)}), bf16[8,64,2,16,128]{4,3,2,1,0:T(8,128)(2,1)}, u32[]{:S(2)}, u32[]{:S(2)}) async-start(bf16[8,64,2,16,128]{4,3,2,1,0:T(8,128)(2,1)} %convolve.2), calls=%async_computation.2 | async-start | bytes 8388608 | tf_op jit(solution)/shard_map/all_to_all | solution.py:364
  197.0 3.8 %collective-permute-start.15 = (bf16[64,2,16,128]{3,2,1,0:T(8,128)(2,1)}, bf16[64,2,16,128]{3,2,1,0:T(8,128)(2,1)S(1)}, u32[]{:S(2)}, u32[]{:S(2)}) collective-permute-start(bf16[64,2,16,128]{3,2,1,0:T(8,128)(2,1)} %get-tuple-element.90), channel_id=1, source_target_pairs={{0,4},{4,0},{8,12},{12,8},{16,20},{20,16},{24,28},{28,24},{1,5},{5... | collective-permute-start | bytes 1572872 | tf_op jit(solution)/shard_map/ppermute | solution.py:375
  197.2 25.3 %collective-permute-start.16 = (bf16[64,2,16,128]{3,2,1,0:T(8,128)(2,1)}, bf16[64,2,16,128]{3,2,1,0:T(8,128)(2,1)S(1)}, u32[]{:S(2)}, u32[]{:S(2)}) collective-permute-start(bf16[64,2,16,128]{3,2,1,0:T(8,128)(2,1)} %get-tuple-element.91), channel_id=1, source_target_pairs={{0,8},{4,12},{8,0},{12,4},{16,24},{20,28},{24,16},{28,20},{1,9},{5... | collective-permute-start | bytes 1572872 | tf_op jit(solution)/shard_map/ppermute | solution.py:375
  198.8 34.0 %collective-permute-start.17 = (bf16[64,2,16,128]{3,2,1,0:T(8,128)(2,1)}, bf16[64,2,16,128]{3,2,1,0:T(8,128)(2,1)S(1)}, u32[]{:S(2)}, u32[]{:S(2)}) collective-permute-start(bf16[64,2,16,128]{3,2,1,0:T(8,128)(2,1)} %get-tuple-element.92), channel_id=1, source_target_pairs={{0,12},{4,8},{8,4},{12,0},{16,28},{20,24},{24,20},{28,16},{1,13},{... | collective-permute-start | bytes 1572872 | tf_op jit(solution)/shard_map/ppermute | solution.py:375
  198.9 34.0 %collective-permute-start.18 = (bf16[64,2,16,128]{3,2,1,0:T(8,128)(2,1)}, bf16[64,2,16,128]{3,2,1,0:T(8,128)(2,1)S(1)}, u32[]{:S(2)}, u32[]{:S(2)}) collective-permute-start(bf16[64,2,16,128]{3,2,1,0:T(8,128)(2,1)} %get-tuple-element.93), channel_id=1, source_target_pairs={{0,16},{4,20},{8,24},{12,28},{16,0},{20,4},{24,8},{28,12},{1,17},{... | collective-permute-start | bytes 1572872 | tf_op jit(solution)/shard_map/ppermute | solution.py:375
  200.5 34.0 %collective-permute-start.19 = (bf16[64,2,16,128]{3,2,1,0:T(8,128)(2,1)}, bf16[64,2,16,128]{3,2,1,0:T(8,128)(2,1)S(1)}, u32[]{:S(2)}, u32[]{:S(2)}) collective-permute-start(bf16[64,2,16,128]{3,2,1,0:T(8,128)(2,1)} %get-tuple-element.94), channel_id=1, source_target_pairs={{0,20},{4,16},{8,28},{12,24},{16,4},{20,0},{24,12},{28,8},{1,21},{... | collective-permute-start | bytes 1572872 | tf_op jit(solution)/shard_map/ppermute | solution.py:375
  200.7 31.7 %copy-start.3 = (bf16[64,2,16,128]{3,2,1,0:T(8,128)(2,1)}, bf16[64,2,16,128]{3,2,1,0:T(8,128)(2,1)S(1)}, u32[]{:S(2)}) copy-start(bf16[64,2,16,128]{3,2,1,0:T(8,128)(2,1)S(1)} %collective-permute-done.15.refs_1_) | copy-start | bytes 1572868
  200.7 45.2 %collective-permute-start.20 = (bf16[64,2,16,128]{3,2,1,0:T(8,128)(2,1)}, bf16[64,2,16,128]{3,2,1,0:T(8,128)(2,1)S(1)}, u32[]{:S(2)}, u32[]{:S(2)}) collective-permute-start(bf16[64,2,16,128]{3,2,1,0:T(8,128)(2,1)} %get-tuple-element.95), channel_id=1, source_target_pairs={{0,24},{4,28},{8,16},{12,20},{16,8},{20,12},{24,0},{28,4},{1,25},{... | collective-permute-start | bytes 1572872 | tf_op jit(solution)/shard_map/ppermute | solution.py:375
  222.6 33.8 %collective-permute-start.21 = (bf16[64,2,16,128]{3,2,1,0:T(8,128)(2,1)}, bf16[64,2,16,128]{3,2,1,0:T(8,128)(2,1)}, u32[]{:S(2)}, u32[]{:S(2)}) collective-permute-start(bf16[64,2,16,128]{3,2,1,0:T(8,128)(2,1)} %get-tuple-element.96), channel_id=1, source_target_pairs={{0,28},{4,24},{8,20},{12,16},{16,12},{20,8},{24,4},{28,0},{1,29},{... | collective-permute-start | bytes 1572872 | tf_op jit(solution)/shard_map/ppermute | solution.py:375
  (14 other events, 205.7 us)

commit v3 on v2

--- a/solution.py
+++ b/solution.py
@@ -325,15 +325,17 @@
         value_out[place, :] = (grad_sum * key).astype(bf16)
 
 
-def finish(me, skip, pieces, key_proj, value_proj, query_proj, out_grad, part, groups, previous):
+def finish(me, skip, pieces, spots, key_proj, value_proj, query_proj, out_grad, part, groups, previous):
     inner, _, local, _ = pieces[0].shape[-4:]
     tokens = key_proj.shape[0]
     dests = LANES // inner
     blocks = groups // dests
     whole = len(pieces) == 1
+    if not whole:
+        pieces = pieces[spots[0] * dests : (spots[-1] + 1) * dests]
 
     def place(step, me):
-        return 0, part * blocks + (step if whole else (me[0] // dests) ^ step)
+        return 0, part * blocks + (step if whole else (me[0] // dests) ^ (spots[0] + step))
 
     column = pl.BlockSpec((tokens, LANES), place)
     if whole:
@@ -345,7 +347,7 @@
         out_shape=[jax.ShapeDtypeStruct(key_proj.shape, bf16)] * 4,
         grid_spec=pltpu.PrefetchScalarGridSpec(
             num_scalar_prefetch=1,
-            grid=(blocks,),
+            grid=(len(spots),),
             in_specs=[pl.BlockSpec((1, LANES), place)]
             + [column] * 4
             + [piece] * len(pieces)
@@ -402,13 +404,16 @@
         gate(place, key_proj, value_proj, query_proj, out_grad, part, groups, inner)
         for part in range(parts)
     ]
-    late = (1,)
+    late = (1, groups - 1)
 
     slabs = [shaped[:, 0]] + [tie(shaped, gates[0])[:, part] for part in range(1, parts)]
 
     def send_filter(part, *others):
         slab = slabs[part].reshape(planes * groups, inner, taps)
         return swap(tie(slab, *others), ("ch", "ctx"))
+
+    def spectrum_of(taps):
+        return filter_spectrum([taps[:, None]], lead_taps, trail_fwd, twist, TILE)
 
     filters = send_filter(0)
     signals = exchange(gates[0], "ctx")
@@ -417,10 +422,11 @@
         last = part == parts - 1
         if not last:
             following = send_filter(part + 1, filters, signals, gates[part + 1])
-            early = [step for step in range(groups) if step not in late]
+            early = [step for step in range(1, groups) if step not in late]
             pieces = tie(gates[part + 1], filters, signals)
             coming = exchange(pieces, "ctx", early)
-        spectrum = filter_spectrum([filters[:, None]], lead_taps, trail_fwd, twist, TILE)
+        if not part:
+            spectrum = spectrum_of(filters)
         tables = (lead, back if last else lead_inv, trail_fwd, trail_inv, twist)
         conv = convolve(signals, spectrum, tables, TILE, not last)
         if last:
@@ -430,12 +436,16 @@
                 coming[step] = tie(pieces[step], conv[0])
             rest = exchange(coming, "ctx", late)
             coming = [rest[step] if step in late else coming[step] for step in range(groups)]
-            conv, following, coming = lax.optimization_barrier((conv[0], following, coming))
-            taken = [swap(conv)]
+            conv, following = lax.optimization_barrier((conv[0], following))
+            spectrum = spectrum_of(following)
+            taken = [swap(tie(conv, spectrum, coming))]
             filters, signals = following, coming
-        outputs = finish(
-            place, skip, taken, key_proj, value_proj, query_proj, out_grad, part, groups, outputs
-        )
+        blocks = range(groups * inner // LANES)
+        for spots in (blocks[:-1], blocks[-1:]) if last else (blocks,):
+            outputs = finish(
+                place, skip, taken, spots, key_proj, value_proj, query_proj, out_grad, part,
+                groups, outputs,
+            )
     return tuple(outputs)
 
 

time: 267 us -> 262 us (0.981)
  waiting for transfers between devices: 116 us -> 105 us
  Pallas kernels: 105 us -> 108 us
    ppermute x22 -> x21, waiting for transfers between devices: 116 us -> 105 us  [exchange(): lax.ppermute(pieces[step], axis, [(i, i ^ step) for i in range(count)])]
    pallas_call x2 -> x3, Pallas kernels: 19.8 us -> 22.5 us  [finish(): pl.pallas_call(functools.partial(finish_kernel, len(pieces)), out_shape=[...]
    ppermute x22 -> x21, starting transfers between devices: 21 us -> 21.5 us  [exchange(): lax.ppermute(pieces[step], axis, [(i, i ^ step) for i in range(count)])]
  transfers between devices with their start and end apart: 25 -> 24, of which waited for: 11 -> 10; matrix products, arithmetic and copies ran while one was open for 2% -> 2% of each run, Pallas kernels for 35% -> 40%
where the time goes in v3:
time: 262 us; the launch traced here: 261 us
  Pallas kernels  108 us (41%)
  waiting for transfers between devices  105 us (40%)
  starting transfers between devices  37.3 us (14%)
  local copies, waits for them, and re-layouts  9.19 us (4%)
    ppermute x21, waiting for transfers between devices, exchange(): lax.ppermute(pieces[step], axis, [(i, i ^ step) for i in range(count)])  105 us
    pallas_call x2, Pallas kernels, convolve(): pl.pallas_call(functools.partial(convolve_kernel, group, sources), out_sh...  49.8 us
    pallas_call x3, Pallas kernels, finish(): pl.pallas_call(functools.partial(finish_kernel, len(pieces)), out_shape=[...  22.5 us
    ppermute x21, starting transfers between devices, exchange(): lax.ppermute(pieces[step], axis, [(i, i ^ step) for i in range(count)])  21.5 us
    pallas_call x2, Pallas kernels, filter_spectrum(): pl.pallas_call(functools.partial(spectrum_kernel, len(pieces), group), ou...  18.2 us
    pallas_call x2, Pallas kernels, gate(): pl.pallas_call(gate_kernel, out_shape=[jax.ShapeDtypeStruct(piece, bf16)]...  16.9 us
    all_to_all x3, starting transfers between devices, swap(): return lax.all_to_all(value, axis, split_axis=0, concat_axis=0, tiled=True)  15.8 us
  transfers between devices with their start and end apart: 24, of which 10 were waited for; matrix products, arithmetic and copies ran while one was open for 2% of the time, Pallas kernels for 40%

profile of v3, /device:TPU:0, one launch (start us, length us, event | category | flops | bytes accessed | tf_op | source)
XLA Modules:
  0.0 261.0 jit_solution(12296662345928331203)
XLA Ops:
  0.6 3.1 %slice.12 = bf16[4,1,8,64,512]{4,3,2,1,0:T(8,128)(2,1)} slice(bf16[4,2,8,64,512]{4,3,2,1,0:T(8,128)(2,1)} %bitcast.17), slice={[0:4], [0:1], [0:8], [0:64], [0:512]} | slice | bytes 4194304 | tf_op jit(solution)/shard_map/slice | solution.py:409
  3.8 7.3 %all-to-all-start = ((bf16[32,64,512]{2,1,0:T(8,128)(2,1)}), bf16[32,64,512]{2,1,0:T(8,128)(2,1)S(1)}, u32[]{:S(2)}, u32[]{:S(2)}) async-start(bf16[32,64,512]{2,1,0:T(8,128)(2,1)} %bitcast.8), calls=%async_computation | async-start | bytes 4194304 | tf_op jit(solution)/shard_map/all_to_all | solution.py:366
  11.1 8.3 %gate.2 = (bf16[64,2,16,128]{3,2,1,0:T(8,128)(2,1)}, bf16[64,2,16,128]{3,2,1,0:T(8,128)(2,1)}, bf16[64,2,16,128]{3,2,1,0:T(8,128)(2,1)}, bf16[64,2,16,128]{3,2,1...) custom-call(s32[1]{0:T(128)} %bitcast.me_ref, ...), custom_call_target="tpu_custom_call" | custom-call | bytes 1048576 | tf_op jit(solution)/shard_map/gate/pallas_call | solution.py:270
  19.6 1.7 collective-permute-start.1
  21.3 1.7 collective-permute-start.3
  23.1 2.6 collective-permute-start.5
  25.7 19.6 %collective-permute-done.1.refs_2_ = bf16[64,2,16,128]{3,2,1,0:T(8,128)(2,1)S(1)} collective-permute-done((bf16[64,2,16,128]{3,2,1,0:T(8,128)(2,1)}, bf16[64,2,16,128]{3,2,1,0:T(8,128)(2,1)S(1)}, u32[]{:S(2)}, u32[]{:S(2)}) %collective-permute-start.1) | collective-permute-done | bytes 524320 | tf_op jit(solution)/shard_map/ppermute | solution.py:377
  45.6 8.7 %gate.3 = (bf16[64,2,16,128]{3,2,1,0:T(8,128)(2,1)}, bf16[64,2,16,128]{3,2,1,0:T(8,128)(2,1)}, bf16[64,2,16,128]{3,2,1,0:T(8,128)(2,1)}, bf16[64,2,16,128]{3,2,1...) custom-call(s32[1]{0:T(128)} %bitcast.me_ref, ...), custom_call_target="tpu_custom_call" | custom-call | bytes 1048576 | tf_op jit(solution)/shard_map/gate/pallas_call | solution.py:270
  54.8 1.5 slice.13
  56.4 2.7 %collective-permute-done.2.refs_3_ = bf16[64,2,16,128]{3,2,1,0:T(8,128)(2,1)S(1)} collective-permute-done((bf16[64,2,16,128]{3,2,1,0:T(8,128)(2,1)}, bf16[64,2,16,128]{3,2,1,0:T(8,128)(2,1)S(1)}, u32[]{:S(2)}, u32[]{:S(2)}) %collective-permute-start.2) | collective-permute-done | bytes 524320 | tf_op jit(solution)/shard_map/ppermute | solution.py:377
  59.1 24.0 %collective-permute-done.4.refs_5_ = bf16[64,2,16,128]{3,2,1,0:T(8,128)(2,1)} collective-permute-done((bf16[64,2,16,128]{3,2,1,0:T(8,128)(2,1)}, bf16[64,2,16,128]{3,2,1,0:T(8,128)(2,1)}, u32[]{:S(2)}, u32[]{:S(2)}) %collective-permute-start.4) | collective-permute-done | bytes 524320 | tf_op jit(solution)/shard_map/ppermute | solution.py:377
  83.1 3.7 %all-to-all-start.1 = ((bf16[32,64,512]{2,1,0:T(8,128)(2,1)}), bf16[32,64,512]{2,1,0:T(8,128)(2,1)}, u32[]{:S(2)}, u32[]{:S(2)}) async-start(bf16[32,64,512]{2,1,0:T(8,128)(2,1)} %bitcast.10), calls=%async_computation.1 | async-start | bytes 4194304 | tf_op jit(solution)/shard_map/all_to_all | solution.py:366
  90.6 1.5 collective-permute-start.10
  92.7 2.3 collective-permute-start.12
  95.0 9.1 %filter_spectrum.2.filter_ref = f32[64,128,256]{2,1,0:T(8,128)} custom-call(bf16[256,256]{1,0:T(8,128)(2,1)} %constant.46.clone.lead_ref, bf16[768,256]{1,0:T(8,128)(2,1)} %constant.49.clone.trail_ref, f32[2,128,128]{2,1,0:T(8,128)} %constant.51.clone.twist_ref, bf16[32,1,64,512]{3,2,1,0:T(8,128)(2,1)} %bitcast.19), custom_call_target="tpu_custom_call" | custom-call | flops 64000000 | bytes 1048576 | tf_op jit(solution)/shard_map/filter_spectrum/pallas_call | solution.py:116
  104.1 25.0 %convolve.2 = bf16[8,64,2,16,128]{4,3,2,1,0:T(8,128)(2,1)} custom-call(bf16[256,256]{1,0:T(8,128)(2,1)} %get-tuple-element.99.lead_ref, bf16[256,256]{1,0:T(8,128)(2,1)} %constant.48.clone.inv_ref, bf16[768,256]{1,0:T(8,128)(2,1)} %constant.49.clone.trail_ref, bf16[768,256]{1,0:T(8,128)(2,1)} %constant.50.clone.back_ref, ...), custom_call_target="tpu_custom_call" | custom-call | flops 64000000 | bytes 1048576 | tf_op jit(solution)/shard_map/convolve/pallas_call | solution.py:209
  129.2 4.6 %collective-permute-done.9.refs_3_ = bf16[64,2,16,128]{3,2,1,0:T(8,128)(2,1)S(1)} collective-permute-done((bf16[64,2,16,128]{3,2,1,0:T(8,128)(2,1)}, bf16[64,2,16,128]{3,2,1,0:T(8,128)(2,1)S(1)}, u32[]{:S(2)}, u32[]{:S(2)}) %collective-permute-start.9) | collective-permute-done | bytes 524320 | tf_op jit(solution)/shard_map/ppermute | solution.py:377
  133.8 2.2 collective-permute-start.13
  136.0 9.1 %filter_spectrum.3.filter_ref = f32[64,128,256]{2,1,0:T(8,128)} custom-call(bf16[256,256]{1,0:T(8,128)(2,1)} %constant.46.clone.lead_ref, bf16[768,256]{1,0:T(8,128)(2,1)} %constant.49.clone.trail_ref, f32[2,128,128]{2,1,0:T(8,128)} %constant.51.clone.twist_ref, bf16[32,1,64,512]{3,2,1,0:T(8,128)(2,1)} %bitcast.11.refs_0_), custom_call_target="tpu_custom_call" | custom-call | flops 64000000 | bytes 1048576 | tf_op jit(solution)/shard_map/filter_spectrum/pallas_call | solution.py:116
  145.2 1.8 collective-permute-done.12.refs_6_
  147.0 10.2 %collective-permute-done.13.refs_7_ = bf16[64,2,16,128]{3,2,1,0:T(8,128)(2,1)S(1)} collective-permute-done((bf16[64,2,16,128]{3,2,1,0:T(8,128)(2,1)S(1)}, bf16[64,2,16,128]{3,2,1,0:T(8,128)(2,1)S(1)}, u32[]{:S(2)}, u32[]{:S(2)}) %collective-permute-start.13) | collective-permute-done | bytes 524320 | tf_op jit(solution)/shard_map/ppermute | solution.py:377
  158.0 4.8 %all-to-all-start.2 = ((bf16[8,64,2,16,128]{4,3,2,1,0:T(8,128)(2,1)}), bf16[8,64,2,16,128]{4,3,2,1,0:T(8,128)(2,1)}, u32[]{:S(2)}, u32[]{:S(2)}) async-start(bf16[8,64,2,16,128]{4,3,2,1,0:T(8,128)(2,1)} %convolve.2), calls=%async_computation.2 | async-start | bytes 8388608 | tf_op jit(solution)/shard_map/all_to_all | solution.py:366
  162.8 24.9 %convolve.3 = (bf16[64,2,16,128]{3,2,1,0:T(8,128)(2,1)}, bf16[64,2,16,128]{3,2,1,0:T(8,128)(2,1)}, bf16[64,2,16,128]{3,2,1,0:T(8,128)(2,1)}, bf16[64,2,16,128]{3...) custom-call(bf16[256,256]{1,0:T(8,128)(2,1)} %get-tuple-element.99.l, ...), custom_call_target="tpu_custom_call" | custom-call | flops 64000000 | bytes 1048576 | tf_op jit(solution)/shard_map/convolve/pallas_call | solution.py:209
  188.0 1.6 collective-permute-start.17
  189.6 1.7 collective-permute-start.19
  191.5 2.5 collective-permute-start.14
  194.0 28.4 %collective-permute-done.17.refs_2_ = bf16[64,2,16,128]{3,2,1,0:T(8,128)(2,1)S(1)} collective-permute-done((bf16[64,2,16,128]{3,2,1,0:T(8,128)(2,1)}, bf16[64,2,16,128]{3,2,1,0:T(8,128)(2,1)S(1)}, u32[]{:S(2)}, u32[]{:S(2)}) %collective-permute-start.17) | collective-permute-done | bytes 524320 | tf_op jit(solution)/shard_map/ppermute | solution.py:377
  222.6 9.6 %finish.3 = (bf16[2048,1024]{1,0:T(8,128)(2,1)}, bf16[2048,1024]{1,0:T(8,128)(2,1)}, bf16[2048,1024]{1,0:T(8,128)(2,1)}, bf16[2048,1024]{1,0:T(8,128)(2,1)}) custom-call(s32[1]{0:T(128)} %bitcast.me_ref, f32[1,1024]{1,0:T(1,128)} %bitcast.22, bf16[2048,1024]{1,0:T(8,128)(2,1)} %key_ref.9, bf16[2048,1024]{1,0:T(8,128)(2,1)} %value_ref.9, ...), custom_call_target="tpu_custom_call" | custom-call | bytes 1048576 | tf_op jit(solution)/shard_map/finish/pallas_call | solution.py:345
  233.7 8.8 %finish.4 = (bf16[2048,1024]{1,0:T(8,128)(2,1)}, bf16[2048,1024]{1,0:T(8,128)(2,1)}, bf16[2048,1024]{1,0:T(8,128)(2,1)}, bf16[2048,1024]{1,0:T(8,128)(2,1)}) custom-call(s32[1]{0:T(128)} %bitcast.me_ref, f32[1,1024]{1,0:T(1,128)} %bitcast.23, ...), custom_call_target="tpu_custom_call", output_to_operand_aliasing={{0}: (12, {}), {1}: (13, {}), {2}: (14, {}), {3}: (15, {})} | custom-call | bytes 1048576 | tf_op jit(solution)/shard_map/finish/pallas_call | solution.py:345
  242.5 3.3 %collective-permute-done.14.refs_0_ = bf16[64,2,16,128]{3,2,1,0:T(8,128)(2,1)S(1)} collective-permute-done((bf16[64,2,16,128]{3,2,1,0:T(8,128)(2,1)}, bf16[64,2,16,128]{3,2,1,0:T(8,128)(2,1)S(1)}, u32[]{:S(2)}, u32[]{:S(2)}) %collective-permute-start.14) | collective-permute-done | bytes 524320 | tf_op jit(solution)/shard_map/ppermute | solution.py:377
  245.8 10.3 %collective-permute-done.15.refs_1_ = bf16[64,2,16,128]{3,2,1,0:T(8,128)(2,1)S(1)} collective-permute-done((bf16[64,2,16,128]{3,2,1,0:T(8,128)(2,1)}, bf16[64,2,16,128]{3,2,1,0:T(8,128)(2,1)S(1)}, u32[]{:S(2)}, u32[]{:S(2)}) %collective-permute-start.15) | collective-permute-done | bytes 524320 | tf_op jit(solution)/shard_map/ppermute | solution.py:377
  256.9 4.1 %finish.5 = (bf16[2048,1024]{1,0:T(8,128)(2,1)}, bf16[2048,1024]{1,0:T(8,128)(2,1)}, bf16[2048,1024]{1,0:T(8,128)(2,1)}, bf16[2048,1024]{1,0:T(8,128)(2,1)}) custom-call(s32[1]{0:T(128)} %bitcast.me_ref, f32[1,1024]{1,0:T(1,128)} %bitcast.24, bf16[2048,1024]{1,0:T(8,128)(2,1)} %key_ref.9, ...), custom_call_target="tpu_custom_call", output_to_operand_aliasing={{0}: (8, {}), {1}: (9, {}), {2}: (10, {}), {3}: (11, {})} | custom-call | bytes 1048576 | tf_op jit(solution)/shard_map/finish/pallas_call | solution.py:345
  (77 shorter events, 9.4 us)
Async XLA Ops:
  3.8 79.4 %all-to-all-start = ((bf16[32,64,512]{2,1,0:T(8,128)(2,1)}), bf16[32,64,512]{2,1,0:T(8,128)(2,1)S(1)}, u32[]{:S(2)}, u32[]{:S(2)}) async-start(bf16[32,64,512]{2,1,0:T(8,128)(2,1)} %bitcast.8), calls=%async_computation | async-start | bytes 4194304 | tf_op jit(solution)/shard_map/all_to_all | solution.py:366
  19.3 3.7 %collective-permute-start = (bf16[64,2,16,128]{3,2,1,0:T(8,128)(2,1)}, bf16[64,2,16,128]{3,2,1,0:T(8,128)(2,1)S(1)}, u32[]{:S(2)}, u32[]{:S(2)}) collective-permute-start(bf16[64,2,16,128]{3,2,1,0:T(8,128)(2,1)} %get-tuple-element.52), channel_id=1, source_target_pairs={{0,4},{4,0},{8,12},{12,8},{16,20},{20,16},{24,28},{28,24},{1,5},{5... | collective-permute-start | bytes 1572872 | tf_op jit(solution)/shard_map/ppermute | solution.py:377
  19.6 25.6 %collective-permute-start.1 = (bf16[64,2,16,128]{3,2,1,0:T(8,128)(2,1)}, bf16[64,2,16,128]{3,2,1,0:T(8,128)(2,1)S(1)}, u32[]{:S(2)}, u32[]{:S(2)}) collective-permute-start(bf16[64,2,16,128]{3,2,1,0:T(8,128)(2,1)} %get-tuple-element.53), channel_id=1, source_target_pairs={{0,8},{4,12},{8,0},{12,4},{16,24},{20,28},{24,16},{28,20},{1,9},{5... | collective-permute-start | bytes 1572872 | tf_op jit(solution)/shard_map/ppermute | solution.py:377
  21.3 37.8 %collective-permute-start.2 = (bf16[64,2,16,128]{3,2,1,0:T(8,128)(2,1)}, bf16[64,2,16,128]{3,2,1,0:T(8,128)(2,1)S(1)}, u32[]{:S(2)}, u32[]{:S(2)}) collective-permute-start(bf16[64,2,16,128]{3,2,1,0:T(8,128)(2,1)} %get-tuple-element.54), channel_id=1, source_target_pairs={{0,12},{4,8},{8,4},{12,0},{16,28},{20,24},{24,20},{28,16},{1,13},{... | collective-permute-start | bytes 1572872 | tf_op jit(solution)/shard_map/ppermute | solution.py:377
  21.3 37.8 %collective-permute-start.3 = (bf16[64,2,16,128]{3,2,1,0:T(8,128)(2,1)}, bf16[64,2,16,128]{3,2,1,0:T(8,128)(2,1)}, u32[]{:S(2)}, u32[]{:S(2)}) collective-permute-start(bf16[64,2,16,128]{3,2,1,0:T(8,128)(2,1)} %get-tuple-element.55), channel_id=1, source_target_pairs={{0,16},{4,20},{8,24},{12,28},{16,0},{20,4},{24,8},{28,12},{1,17},{... | collective-permute-start | bytes 1572872 | tf_op jit(solution)/shard_map/ppermute | solution.py:377
  23.0 60.1 %collective-permute-start.4 = (bf16[64,2,16,128]{3,2,1,0:T(8,128)(2,1)}, bf16[64,2,16,128]{3,2,1,0:T(8,128)(2,1)}, u32[]{:S(2)}, u32[]{:S(2)}) collective-permute-start(bf16[64,2,16,128]{3,2,1,0:T(8,128)(2,1)} %get-tuple-element.56), channel_id=1, source_target_pairs={{0,20},{4,16},{8,28},{12,24},{16,4},{20,0},{24,12},{28,8},{1,21},{... | collective-permute-start | bytes 1572872 | tf_op jit(solution)/shard_map/ppermute | solution.py:377
  23.1 31.2 %copy-start.9 = (bf16[64,2,16,128]{3,2,1,0:T(8,128)(2,1)}, bf16[64,2,16,128]{3,2,1,0:T(8,128)(2,1)S(1)}, u32[]{:S(2)}) copy-start(bf16[64,2,16,128]{3,2,1,0:T(8,128)(2,1)S(1)} %collective-permute-done.refs_1_) | copy-start | bytes 1572868
  23.1 60.0 %collective-permute-start.5 = (bf16[64,2,16,128]{3,2,1,0:T(8,128)(2,1)}, bf16[64,2,16,128]{3,2,1,0:T(8,128)(2,1)}, u32[]{:S(2)}, u32[]{:S(2)}) collective-permute-start(bf16[64,2,16,128]{3,2,1,0:T(8,128)(2,1)} %get-tuple-element.57), channel_id=1, source_target_pairs={{0,24},{4,28},{8,16},{12,20},{16,8},{20,12},{24,0},{28,4},{1,25},{... | collective-permute-start | bytes 1572872 | tf_op jit(solution)/shard_map/ppermute | solution.py:377
  45.2 37.9 %collective-permute-start.6 = (bf16[64,2,16,128]{3,2,1,0:T(8,128)(2,1)}, bf16[64,2,16,128]{3,2,1,0:T(8,128)(2,1)}, u32[]{:S(2)}, u32[]{:S(2)}) collective-permute-start(bf16[64,2,16,128]{3,2,1,0:T(8,128)(2,1)} %get-tuple-element.58), channel_id=1, source_target_pairs={{0,28},{4,24},{8,20},{12,16},{16,12},{20,8},{24,4},{28,0},{1,29},{... | collective-permute-start | bytes 1572872 | tf_op jit(solution)/shard_map/ppermute | solution.py:377
  54.8 33.8 %copy-start.16 = (bf16[2,8,16,256]{3,2,1,0:T(8,128)(2,1)S(1)}, bf16[2,8,16,256]{3,2,1,0:T(8,128)(2,1)}, u32[]{:S(2)}) copy-start(bf16[2,8,16,256]{3,2,1,0:T(8,128)(2,1)} %constant.53) | copy-start | bytes 393220
  54.8 34.3 %copy-start.1 = (bf16[256,2,8,16]{0,3,2,1:T(8,128)(2,1)S(1)}, bf16[256,2,8,16]{0,3,2,1:T(8,128)(2,1)}, u32[]{:S(2)}) copy-start(bf16[256,2,8,16]{0,3,2,1:T(8,128)(2,1)} %constant.52) | copy-start | bytes 393220
  59.1 24.0 %copy-start.11 = (bf16[64,2,16,128]{3,2,1,0:T(8,128)(2,1)}, bf16[64,2,16,128]{3,2,1,0:T(8,128)(2,1)S(1)}, u32[]{:S(2)}) copy-start(bf16[64,2,16,128]{3,2,1,0:T(8,128)(2,1)S(1)} %collective-permute-done.2.refs_3_) | copy-start | bytes 1572868
  83.1 52.9 %all-to-all-start.1 = ((bf16[32,64,512]{2,1,0:T(8,128)(2,1)}), bf16[32,64,512]{2,1,0:T(8,128)(2,1)}, u32[]{:S(2)}, u32[]{:S(2)}) async-start(bf16[32,64,512]{2,1,0:T(8,128)(2,1)} %bitcast.10), calls=%async_computation.1 | async-start | bytes 4194304 | tf_op jit(solution)/shard_map/all_to_all | solution.py:366
  86.9 42.2 %collective-permute-start.8 = (bf16[64,2,16,128]{3,2,1,0:T(8,128)(2,1)}, bf16[64,2,16,128]{3,2,1,0:T(8,128)(2,1)S(1)}, u32[]{:S(2)}, u32[]{:S(2)}) collective-permute-start(bf16[64,2,16,128]{3,2,1,0:T(8,128)(2,1)} %get-tuple-element.73), channel_id=1, source_target_pairs={{0,8},{4,12},{8,0},{12,4},{16,24},{20,28},{24,16},{28,20},{1,9},{5... | collective-permute-start | bytes 1572872 | tf_op jit(solution)/shard_map/ppermute | solution.py:377
  88.4 45.4 %collective-permute-start.9 = (bf16[64,2,16,128]{3,2,1,0:T(8,128)(2,1)}, bf16[64,2,16,128]{3,2,1,0:T(8,128)(2,1)S(1)}, u32[]{:S(2)}, u32[]{:S(2)}) collective-permute-start(bf16[64,2,16,128]{3,2,1,0:T(8,128)(2,1)} %get-tuple-element.74), channel_id=1, source_target_pairs={{0,12},{4,8},{8,4},{12,0},{16,28},{20,24},{24,20},{28,16},{1,13},{... | collective-permute-start | bytes 1572872 | tf_op jit(solution)/shard_map/ppermute | solution.py:377
  90.6 54.5 %collective-permute-start.10 = (bf16[64,2,16,128]{3,2,1,0:T(8,128)(2,1)}, bf16[64,2,16,128]{3,2,1,0:T(8,128)(2,1)}, u32[]{:S(2)}, u32[]{:S(2)}) collective-permute-start(bf16[64,2,16,128]{3,2,1,0:T(8,128)(2,1)} %get-tuple-element.75), channel_id=1, source_target_pairs={{0,16},{4,20},{8,24},{12,28},{16,0},{20,4},{24,8},{28,12},{1,17},{... | collective-permute-start | bytes 1572872 | tf_op jit(solution)/shard_map/ppermute | solution.py:377
  92.1 53.0 %collective-permute-start.11 = (bf16[64,2,16,128]{3,2,1,0:T(8,128)(2,1)}, bf16[64,2,16,128]{3,2,1,0:T(8,128)(2,1)}, u32[]{:S(2)}, u32[]{:S(2)}) collective-permute-start(bf16[64,2,16,128]{3,2,1,0:T(8,128)(2,1)} %get-tuple-element.76), channel_id=1, source_target_pairs={{0,20},{4,16},{8,28},{12,24},{16,4},{20,0},{24,12},{28,8},{1,21},{... | collective-permute-start | bytes 1572872 | tf_op jit(solution)/shard_map/ppermute | solution.py:377
  92.7 54.3 %collective-permute-start.12 = (bf16[64,2,16,128]{3,2,1,0:T(8,128)(2,1)}, bf16[64,2,16,128]{3,2,1,0:T(8,128)(2,1)}, u32[]{:S(2)}, u32[]{:S(2)}) collective-permute-start(bf16[64,2,16,128]{3,2,1,0:T(8,128)(2,1)} %get-tuple-element.77), channel_id=1, source_target_pairs={{0,24},{4,28},{8,16},{12,20},{16,8},{20,12},{24,0},{28,4},{1,25},{... | collective-permute-start | bytes 1572872 | tf_op jit(solution)/shard_map/ppermute | solution.py:377
  104.1 25.0 %copy-start.18 = (bf16[64,2,16,128]{3,2,1,0:T(8,128)(2,1)S(1)}, bf16[64,2,16,128]{3,2,1,0:T(8,128)(2,1)}, u32[]{:S(2)}) copy-start(bf16[64,2,16,128]{3,2,1,0:T(8,128)(2,1)} %get-tuple-element.72) | copy-start | bytes 1572868
  104.1 29.7 %copy-start.17 = (bf16[64,2,16,128]{3,2,1,0:T(8,128)(2,1)S(1)}, bf16[64,2,16,128]{3,2,1,0:T(8,128)(2,1)}, u32[]{:S(2)}) copy-start(bf16[64,2,16,128]{3,2,1,0:T(8,128)(2,1)} %get-tuple-element.79) | copy-start | bytes 1572868
  129.1 16.1 %copy-start.12 = (bf16[64,2,16,128]{3,2,1,0:T(8,128)(2,1)}, bf16[64,2,16,128]{3,2,1,0:T(8,128)(2,1)S(1)}, u32[]{:S(2)}) copy-start(bf16[64,2,16,128]{3,2,1,0:T(8,128)(2,1)S(1)} %collective-permute-done.8.refs_2_) | copy-start | bytes 1572868
  129.1 17.9 %collective-permute-start.7 = (bf16[64,2,16,128]{3,2,1,0:T(8,128)(2,1)S(1)}, bf16[64,2,16,128]{3,2,1,0:T(8,128)(2,1)S(1)}, u32[]{:S(2)}, u32[]{:S(2)}) collective-permute-start(bf16[64,2,16,128]{3,2,1,0:T(8,128)(2,1)S(1)} %copy-done.18), channel_id=1, source_target_pairs={{0,4},{4,0},{8,12},{12,8},{16,20},{20,16},{24,28},{28,24},{1,5},{5... | collective-permute-start | bytes 1572872 | tf_op jit(solution)/shard_map/ppermute | solution.py:377
  133.8 23.4 %collective-permute-start.13 = (bf16[64,2,16,128]{3,2,1,0:T(8,128)(2,1)S(1)}, bf16[64,2,16,128]{3,2,1,0:T(8,128)(2,1)S(1)}, u32[]{:S(2)}, u32[]{:S(2)}) collective-permute-start(bf16[64,2,16,128]{3,2,1,0:T(8,128)(2,1)S(1)} %copy-done.17), channel_id=1, source_target_pairs={{0,28},{4,24},{8,20},{12,16},{16,12},{20,8},{24,4},{28,0},{1,29},{... | collective-permute-start | bytes 1572872 | tf_op jit(solution)/shard_map/ppermute | solution.py:377
  158.0 64.7 %all-to-all-start.2 = ((bf16[8,64,2,16,128]{4,3,2,1,0:T(8,128)(2,1)}), bf16[8,64,2,16,128]{4,3,2,1,0:T(8,128)(2,1)}, u32[]{:S(2)}, u32[]{:S(2)}) async-start(bf16[8,64,2,16,128]{4,3,2,1,0:T(8,128)(2,1)} %convolve.2), calls=%async_computation.2 | async-start | bytes 8388608 | tf_op jit(solution)/shard_map/all_to_all | solution.py:366
  187.7 3.8 %collective-permute-start.16 = (bf16[64,2,16,128]{3,2,1,0:T(8,128)(2,1)}, bf16[64,2,16,128]{3,2,1,0:T(8,128)(2,1)S(1)}, u32[]{:S(2)}, u32[]{:S(2)}) collective-permute-start(bf16[64,2,16,128]{3,2,1,0:T(8,128)(2,1)} %get-tuple-element.83), channel_id=1, source_target_pairs={{0,4},{4,0},{8,12},{12,8},{16,20},{20,16},{24,28},{28,24},{1,5},{5... | collective-permute-start | bytes 1572872 | tf_op jit(solution)/shard_map/ppermute | solution.py:377
  188.0 34.4 %collective-permute-start.17 = (bf16[64,2,16,128]{3,2,1,0:T(8,128)(2,1)}, bf16[64,2,16,128]{3,2,1,0:T(8,128)(2,1)S(1)}, u32[]{:S(2)}, u32[]{:S(2)}) collective-permute-start(bf16[64,2,16,128]{3,2,1,0:T(8,128)(2,1)} %get-tuple-element.84), channel_id=1, source_target_pairs={{0,8},{4,12},{8,0},{12,4},{16,24},{20,28},{24,16},{28,20},{1,9},{5... | collective-permute-start | bytes 1572872 | tf_op jit(solution)/shard_map/ppermute | solution.py:377
  189.6 43.1 %collective-permute-start.18 = (bf16[64,2,16,128]{3,2,1,0:T(8,128)(2,1)}, bf16[64,2,16,128]{3,2,1,0:T(8,128)(2,1)S(1)}, u32[]{:S(2)}, u32[]{:S(2)}) collective-permute-start(bf16[64,2,16,128]{3,2,1,0:T(8,128)(2,1)} %get-tuple-element.85), channel_id=1, source_target_pairs={{0,12},{4,8},{8,4},{12,0},{16,28},{20,24},{24,20},{28,16},{1,13},{... | collective-permute-start | bytes 1572872 | tf_op jit(solution)/shard_map/ppermute | solution.py:377
  189.6 43.1 %collective-permute-start.19 = (bf16[64,2,16,128]{3,2,1,0:T(8,128)(2,1)}, bf16[64,2,16,128]{3,2,1,0:T(8,128)(2,1)S(1)}, u32[]{:S(2)}, u32[]{:S(2)}) collective-permute-start(bf16[64,2,16,128]{3,2,1,0:T(8,128)(2,1)} %get-tuple-element.86), channel_id=1, source_target_pairs={{0,16},{4,20},{8,24},{12,28},{16,0},{20,4},{24,8},{28,12},{1,17},{... | collective-permute-start | bytes 1572872 | tf_op jit(solution)/shard_map/ppermute | solution.py:377
  191.3 41.4 %collective-permute-start.20 = (bf16[64,2,16,128]{3,2,1,0:T(8,128)(2,1)}, bf16[64,2,16,128]{3,2,1,0:T(8,128)(2,1)}, u32[]{:S(2)}, u32[]{:S(2)}) collective-permute-start(bf16[64,2,16,128]{3,2,1,0:T(8,128)(2,1)} %get-tuple-element.87), channel_id=1, source_target_pairs={{0,20},{4,16},{8,28},{12,24},{16,4},{20,0},{24,12},{28,8},{1,21},{... | collective-permute-start | bytes 1572872 | tf_op jit(solution)/shard_map/ppermute | solution.py:377
  191.5 40.8 %copy-start.3 = (bf16[64,2,16,128]{3,2,1,0:T(8,128)(2,1)}, bf16[64,2,16,128]{3,2,1,0:T(8,128)(2,1)S(1)}, u32[]{:S(2)}) copy-start(bf16[64,2,16,128]{3,2,1,0:T(8,128)(2,1)S(1)} %collective-permute-done.16.refs_1_) | copy-start | bytes 1572868
  191.5 54.3 %collective-permute-start.14 = (bf16[64,2,16,128]{3,2,1,0:T(8,128)(2,1)}, bf16[64,2,16,128]{3,2,1,0:T(8,128)(2,1)S(1)}, u32[]{:S(2)}, u32[]{:S(2)}) collective-permute-start(bf16[64,2,16,128]{3,2,1,0:T(8,128)(2,1)} %get-tuple-element.80), channel_id=1, source_target_pairs={{0,24},{4,28},{8,16},{12,20},{16,8},{20,12},{24,0},{28,4},{1,25},{... | collective-permute-start | bytes 1572872 | tf_op jit(solution)/shard_map/ppermute | solution.py:377
  222.4 33.7 %collective-permute-start.15 = (bf16[64,2,16,128]{3,2,1,0:T(8,128)(2,1)}, bf16[64,2,16,128]{3,2,1,0:T(8,128)(2,1)S(1)}, u32[]{:S(2)}, u32[]{:S(2)}) collective-permute-start(bf16[64,2,16,128]{3,2,1,0:T(8,128)(2,1)} %get-tuple-element.81), channel_id=1, source_target_pairs={{0,28},{4,24},{8,20},{12,16},{16,12},{20,8},{24,4},{28,0},{1,29},{... | collective-permute-start | bytes 1572872 | tf_op jit(solution)/shard_map/ppermute | solution.py:377
  (11 other events, 75.1 us)

commit v4 on v3

--- a/solution.py
+++ b/solution.py
@@ -130,7 +130,7 @@
         * len(pieces),
         out_specs=pl.BlockSpec((group, rows, 2 * LANES), lambda step: (step, 0, 0)),
         scratch_shapes=[
-            pltpu.VMEM((width // LANES, len(pieces) * sources * group, LANES), f32),
+            pltpu.VMEM((width // LANES, (len(pieces) * sources + 1) * group, LANES), f32),
             pltpu.VMEM((group * rows, 6 * LANES), bf16),
         ],
         compiler_params=pltpu.CompilerParams(vmem_limit_bytes=VMEM_BYTES),
@@ -236,7 +236,7 @@
     outs, scratch = refs[:-1], refs[-1]
     tokens, width = key_ref.shape
     local = tokens // LANES
-    pitch = scratch.shape[1] // local
+    pitch = LANES + 8
     inner = outs[0].shape[0]
     dests = width // inner
     mine = lax.rem(me_ref[0], dests)
@@ -275,7 +275,7 @@
             grid=(blocks,),
             in_specs=[column] * 4,
             out_specs=[pl.BlockSpec(piece, lambda step, me: (0, 0, 0, 0))] * groups,
-            scratch_shapes=[pltpu.VMEM((2, local * (LANES + 8), LANES), f32)],
+            scratch_shapes=[pltpu.VMEM((2, local * (LANES + 8) + LANES, LANES), f32)],
         ),
         compiler_params=pltpu.CompilerParams(vmem_limit_bytes=VMEM_BYTES),
         cost_estimate=pl.CostEstimate(flops=0, bytes_accessed=2**20, transcendentals=0),
@@ -288,7 +288,7 @@
     out_ref, query_out, key_out, value_out, scratch = refs[-5:]
     tokens, width = key_ref.shape
     local = tokens // LANES
-    pitch = scratch.shape[1] // width
+    pitch = local + 1
     inner = pieces[0].shape[-4]
     dests = width // inner
     mine = lax.rem(me_ref[0], dests)
@@ -353,7 +353,7 @@
             + [piece] * len(pieces)
             + [pl.BlockSpec(memory_space=pl.ANY)] * len(previous),
             out_specs=[column] * 4,
-            scratch_shapes=[pltpu.VMEM((2, LANES * (local + 1), LANES), f32)],
+            scratch_shapes=[pltpu.VMEM((2, LANES * (local + 1) + local + 8, LANES), f32)],
         ),
         input_output_aliases={6 + len(pieces) + index: index for index in range(len(previous))},
         compiler_params=pltpu.CompilerParams(vmem_limit_bytes=VMEM_BYTES),

time: 262 us -> 262 us (level)
  no operation moved by 1% of the time
where the time goes in v4:
time: 262 us; the launch traced here: 261 us
  Pallas kernels  107 us (41%)
  waiting for transfers between devices  105 us (40%)
  starting transfers between devices  37.3 us (14%)
  local copies, waits for them, and re-layouts  9.19 us (4%)
    ppermute x21, waiting for transfers between devices, exchange(): lax.ppermute(pieces[step], axis, [(i, i ^ step) for i in range(count)])  105 us
    pallas_call x2, Pallas kernels, convolve(): pl.pallas_call(functools.partial(convolve_kernel, group, sources), out_sh...  49.8 us
    pallas_call x3, Pallas kernels, finish(): pl.pallas_call(functools.partial(finish_kernel, len(pieces)), out_shape=[...  22.5 us
    ppermute x21, starting transfers between devices, exchange(): lax.ppermute(pieces[step], axis, [(i, i ^ step) for i in range(count)])  21.5 us
    pallas_call x2, Pallas kernels, filter_spectrum(): pl.pallas_call(functools.partial(spectrum_kernel, len(pieces), group), ou...  18.2 us
    pallas_call x2, Pallas kernels, gate(): pl.pallas_call(gate_kernel, out_shape=[jax.ShapeDtypeStruct(piece, bf16)]...  16.9 us
    all_to_all x3, starting transfers between devices, swap(): return lax.all_to_all(value, axis, split_axis=0, concat_axis=0, tiled=True)  15.8 us
  transfers between devices with their start and end apart: 24, of which 10 were waited for; matrix products, arithmetic and copies ran while one was open for 2% of the time, Pallas kernels for 40%

profile of v4, /device:TPU:0, one launch (start us, length us, event | category | flops | bytes accessed | tf_op | source)
XLA Modules:
  0.0 261.0 jit_solution(10976098503029585755)
XLA Ops:
  0.6 3.1 %slice.12 = bf16[4,1,8,64,512]{4,3,2,1,0:T(8,128)(2,1)} slice(bf16[4,2,8,64,512]{4,3,2,1,0:T(8,128)(2,1)} %bitcast.17), slice={[0:4], [0:1], [0:8], [0:64], [0:512]} | slice | bytes 4194304 | tf_op jit(solution)/shard_map/slice | solution.py:409
  3.8 7.3 %all-to-all-start = ((bf16[32,64,512]{2,1,0:T(8,128)(2,1)}), bf16[32,64,512]{2,1,0:T(8,128)(2,1)S(1)}, u32[]{:S(2)}, u32[]{:S(2)}) async-start(bf16[32,64,512]{2,1,0:T(8,128)(2,1)} %bitcast.8), calls=%async_computation | async-start | bytes 4194304 | tf_op jit(solution)/shard_map/all_to_all | solution.py:366
  11.1 8.3 %gate.2 = (bf16[64,2,16,128]{3,2,1,0:T(8,128)(2,1)}, bf16[64,2,16,128]{3,2,1,0:T(8,128)(2,1)}, bf16[64,2,16,128]{3,2,1,0:T(8,128)(2,1)}, bf16[64,2,16,128]{3,2,1...) custom-call(s32[1]{0:T(128)} %bitcast.me_ref, ...), custom_call_target="tpu_custom_call" | custom-call | bytes 1048576 | tf_op jit(solution)/shard_map/gate/pallas_call | solution.py:270
  19.6 1.7 collective-permute-start.1
  21.3 1.7 collective-permute-start.3
  23.1 2.6 collective-permute-start.5
  25.7 19.6 %collective-permute-done.1.refs_2_ = bf16[64,2,16,128]{3,2,1,0:T(8,128)(2,1)S(1)} collective-permute-done((bf16[64,2,16,128]{3,2,1,0:T(8,128)(2,1)}, bf16[64,2,16,128]{3,2,1,0:T(8,128)(2,1)S(1)}, u32[]{:S(2)}, u32[]{:S(2)}) %collective-permute-start.1) | collective-permute-done | bytes 524320 | tf_op jit(solution)/shard_map/ppermute | solution.py:377
  45.6 8.7 %gate.3 = (bf16[64,2,16,128]{3,2,1,0:T(8,128)(2,1)}, bf16[64,2,16,128]{3,2,1,0:T(8,128)(2,1)}, bf16[64,2,16,128]{3,2,1,0:T(8,128)(2,1)}, bf16[64,2,16,128]{3,2,1...) custom-call(s32[1]{0:T(128)} %bitcast.me_ref, ...), custom_call_target="tpu_custom_call" | custom-call | bytes 1048576 | tf_op jit(solution)/shard_map/gate/pallas_call | solution.py:270
  54.8 1.5 slice.13
  56.4 2.7 %collective-permute-done.2.refs_3_ = bf16[64,2,16,128]{3,2,1,0:T(8,128)(2,1)S(1)} collective-permute-done((bf16[64,2,16,128]{3,2,1,0:T(8,128)(2,1)}, bf16[64,2,16,128]{3,2,1,0:T(8,128)(2,1)S(1)}, u32[]{:S(2)}, u32[]{:S(2)}) %collective-permute-start.2) | collective-permute-done | bytes 524320 | tf_op jit(solution)/shard_map/ppermute | solution.py:377
  59.1 24.0 %collective-permute-done.4.refs_5_ = bf16[64,2,16,128]{3,2,1,0:T(8,128)(2,1)} collective-permute-done((bf16[64,2,16,128]{3,2,1,0:T(8,128)(2,1)}, bf16[64,2,16,128]{3,2,1,0:T(8,128)(2,1)}, u32[]{:S(2)}, u32[]{:S(2)}) %collective-permute-start.4) | collective-permute-done | bytes 524320 | tf_op jit(solution)/shard_map/ppermute | solution.py:377
  83.1 3.7 %all-to-all-start.1 = ((bf16[32,64,512]{2,1,0:T(8,128)(2,1)}), bf16[32,64,512]{2,1,0:T(8,128)(2,1)}, u32[]{:S(2)}, u32[]{:S(2)}) async-start(bf16[32,64,512]{2,1,0:T(8,128)(2,1)} %bitcast.10), calls=%async_computation.1 | async-start | bytes 4194304 | tf_op jit(solution)/shard_map/all_to_all | solution.py:366
  90.6 1.5 collective-permute-start.10
  92.7 2.3 collective-permute-start.12
  95.0 9.1 %filter_spectrum.2.filter_ref = f32[64,128,256]{2,1,0:T(8,128)} custom-call(bf16[256,256]{1,0:T(8,128)(2,1)} %constant.46.clone.lead_ref, bf16[768,256]{1,0:T(8,128)(2,1)} %constant.49.clone.trail_ref, f32[2,128,128]{2,1,0:T(8,128)} %constant.51.clone.twist_ref, bf16[32,1,64,512]{3,2,1,0:T(8,128)(2,1)} %bitcast.19), custom_call_target="tpu_custom_call" | custom-call | flops 64000000 | bytes 1048576 | tf_op jit(solution)/shard_map/filter_spectrum/pallas_call | solution.py:116
  104.1 25.0 %convolve.2 = bf16[8,64,2,16,128]{4,3,2,1,0:T(8,128)(2,1)} custom-call(bf16[256,256]{1,0:T(8,128)(2,1)} %get-tuple-element.99.lead_ref, bf16[256,256]{1,0:T(8,128)(2,1)} %constant.48.clone.inv_ref, bf16[768,256]{1,0:T(8,128)(2,1)} %constant.49.clone.trail_ref, bf16[768,256]{1,0:T(8,128)(2,1)} %constant.50.clone.back_ref, ...), custom_call_target="tpu_custom_call" | custom-call | flops 64000000 | bytes 1048576 | tf_op jit(solution)/shard_map/convolve/pallas_call | solution.py:209
  129.2 4.6 %collective-permute-done.9.refs_3_ = bf16[64,2,16,128]{3,2,1,0:T(8,128)(2,1)S(1)} collective-permute-done((bf16[64,2,16,128]{3,2,1,0:T(8,128)(2,1)}, bf16[64,2,16,128]{3,2,1,0:T(8,128)(2,1)S(1)}, u32[]{:S(2)}, u32[]{:S(2)}) %collective-permute-start.9) | collective-permute-done | bytes 524320 | tf_op jit(solution)/shard_map/ppermute | solution.py:377
  133.8 2.2 collective-permute-start.13
  136.0 9.1 %filter_spectrum.3.filter_ref = f32[64,128,256]{2,1,0:T(8,128)} custom-call(bf16[256,256]{1,0:T(8,128)(2,1)} %constant.46.clone.lead_ref, bf16[768,256]{1,0:T(8,128)(2,1)} %constant.49.clone.trail_ref, f32[2,128,128]{2,1,0:T(8,128)} %constant.51.clone.twist_ref, bf16[32,1,64,512]{3,2,1,0:T(8,128)(2,1)} %bitcast.11.refs_0_), custom_call_target="tpu_custom_call" | custom-call | flops 64000000 | bytes 1048576 | tf_op jit(solution)/shard_map/filter_spectrum/pallas_call | solution.py:116
  145.2 1.8 collective-permute-done.12.refs_6_
  147.0 10.2 %collective-permute-done.13.refs_7_ = bf16[64,2,16,128]{3,2,1,0:T(8,128)(2,1)S(1)} collective-permute-done((bf16[64,2,16,128]{3,2,1,0:T(8,128)(2,1)S(1)}, bf16[64,2,16,128]{3,2,1,0:T(8,128)(2,1)S(1)}, u32[]{:S(2)}, u32[]{:S(2)}) %collective-permute-start.13) | collective-permute-done | bytes 524320 | tf_op jit(solution)/shard_map/ppermute | solution.py:377
  158.0 4.8 %all-to-all-start.2 = ((bf16[8,64,2,16,128]{4,3,2,1,0:T(8,128)(2,1)}), bf16[8,64,2,16,128]{4,3,2,1,0:T(8,128)(2,1)}, u32[]{:S(2)}, u32[]{:S(2)}) async-start(bf16[8,64,2,16,128]{4,3,2,1,0:T(8,128)(2,1)} %convolve.2), calls=%async_computation.2 | async-start | bytes 8388608 | tf_op jit(solution)/shard_map/all_to_all | solution.py:366
  162.8 24.9 %convolve.3 = (bf16[64,2,16,128]{3,2,1,0:T(8,128)(2,1)}, bf16[64,2,16,128]{3,2,1,0:T(8,128)(2,1)}, bf16[64,2,16,128]{3,2,1,0:T(8,128)(2,1)}, bf16[64,2,16,128]{3...) custom-call(bf16[256,256]{1,0:T(8,128)(2,1)} %get-tuple-element.99.l, ...), custom_call_target="tpu_custom_call" | custom-call | flops 64000000 | bytes 1048576 | tf_op jit(solution)/shard_map/convolve/pallas_call | solution.py:209
  188.0 1.6 collective-permute-start.17
  189.6 1.7 collective-permute-start.19
  191.5 2.5 collective-permute-start.14
  194.0 28.4 %collective-permute-done.17.refs_2_ = bf16[64,2,16,128]{3,2,1,0:T(8,128)(2,1)S(1)} collective-permute-done((bf16[64,2,16,128]{3,2,1,0:T(8,128)(2,1)}, bf16[64,2,16,128]{3,2,1,0:T(8,128)(2,1)S(1)}, u32[]{:S(2)}, u32[]{:S(2)}) %collective-permute-start.17) | collective-permute-done | bytes 524320 | tf_op jit(solution)/shard_map/ppermute | solution.py:377
  222.6 9.6 %finish.3 = (bf16[2048,1024]{1,0:T(8,128)(2,1)}, bf16[2048,1024]{1,0:T(8,128)(2,1)}, bf16[2048,1024]{1,0:T(8,128)(2,1)}, bf16[2048,1024]{1,0:T(8,128)(2,1)}) custom-call(s32[1]{0:T(128)} %bitcast.me_ref, f32[1,1024]{1,0:T(1,128)} %bitcast.22, bf16[2048,1024]{1,0:T(8,128)(2,1)} %key_ref.9, bf16[2048,1024]{1,0:T(8,128)(2,1)} %value_ref.9, ...), custom_call_target="tpu_custom_call" | custom-call | bytes 1048576 | tf_op jit(solution)/shard_map/finish/pallas_call | solution.py:345
  233.7 8.8 %finish.4 = (bf16[2048,1024]{1,0:T(8,128)(2,1)}, bf16[2048,1024]{1,0:T(8,128)(2,1)}, bf16[2048,1024]{1,0:T(8,128)(2,1)}, bf16[2048,1024]{1,0:T(8,128)(2,1)}) custom-call(s32[1]{0:T(128)} %bitcast.me_ref, f32[1,1024]{1,0:T(1,128)} %bitcast.23, ...), custom_call_target="tpu_custom_call", output_to_operand_aliasing={{0}: (12, {}), {1}: (13, {}), {2}: (14, {}), {3}: (15, {})} | custom-call | bytes 1048576 | tf_op jit(solution)/shard_map/finish/pallas_call | solution.py:345
  242.5 3.3 %collective-permute-done.14.refs_0_ = bf16[64,2,16,128]{3,2,1,0:T(8,128)(2,1)S(1)} collective-permute-done((bf16[64,2,16,128]{3,2,1,0:T(8,128)(2,1)}, bf16[64,2,16,128]{3,2,1,0:T(8,128)(2,1)S(1)}, u32[]{:S(2)}, u32[]{:S(2)}) %collective-permute-start.14) | collective-permute-done | bytes 524320 | tf_op jit(solution)/shard_map/ppermute | solution.py:377
  245.8 10.3 %collective-permute-done.15.refs_1_ = bf16[64,2,16,128]{3,2,1,0:T(8,128)(2,1)S(1)} collective-permute-done((bf16[64,2,16,128]{3,2,1,0:T(8,128)(2,1)}, bf16[64,2,16,128]{3,2,1,0:T(8,128)(2,1)S(1)}, u32[]{:S(2)}, u32[]{:S(2)}) %collective-permute-start.15) | collective-permute-done | bytes 524320 | tf_op jit(solution)/shard_map/ppermute | solution.py:377
  256.9 4.1 %finish.5 = (bf16[2048,1024]{1,0:T(8,128)(2,1)}, bf16[2048,1024]{1,0:T(8,128)(2,1)}, bf16[2048,1024]{1,0:T(8,128)(2,1)}, bf16[2048,1024]{1,0:T(8,128)(2,1)}) custom-call(s32[1]{0:T(128)} %bitcast.me_ref, f32[1,1024]{1,0:T(1,128)} %bitcast.24, bf16[2048,1024]{1,0:T(8,128)(2,1)} %key_ref.9, ...), custom_call_target="tpu_custom_call", output_to_operand_aliasing={{0}: (8, {}), {1}: (9, {}), {2}: (10, {}), {3}: (11, {})} | custom-call | bytes 1048576 | tf_op jit(solution)/shard_map/finish/pallas_call | solution.py:345
  (77 shorter events, 9.4 us)
Async XLA Ops:
  3.8 79.4 %all-to-all-start = ((bf16[32,64,512]{2,1,0:T(8,128)(2,1)}), bf16[32,64,512]{2,1,0:T(8,128)(2,1)S(1)}, u32[]{:S(2)}, u32[]{:S(2)}) async-start(bf16[32,64,512]{2,1,0:T(8,128)(2,1)} %bitcast.8), calls=%async_computation | async-start | bytes 4194304 | tf_op jit(solution)/shard_map/all_to_all | solution.py:366
  19.3 3.7 %collective-permute-start = (bf16[64,2,16,128]{3,2,1,0:T(8,128)(2,1)}, bf16[64,2,16,128]{3,2,1,0:T(8,128)(2,1)S(1)}, u32[]{:S(2)}, u32[]{:S(2)}) collective-permute-start(bf16[64,2,16,128]{3,2,1,0:T(8,128)(2,1)} %get-tuple-element.52), channel_id=1, source_target_pairs={{0,4},{4,0},{8,12},{12,8},{16,20},{20,16},{24,28},{28,24},{1,5},{5... | collective-permute-start | bytes 1572872 | tf_op jit(solution)/shard_map/ppermute | solution.py:377
  19.6 25.6 %collective-permute-start.1 = (bf16[64,2,16,128]{3,2,1,0:T(8,128)(2,1)}, bf16[64,2,16,128]{3,2,1,0:T(8,128)(2,1)S(1)}, u32[]{:S(2)}, u32[]{:S(2)}) collective-permute-start(bf16[64,2,16,128]{3,2,1,0:T(8,128)(2,1)} %get-tuple-element.53), channel_id=1, source_target_pairs={{0,8},{4,12},{8,0},{12,4},{16,24},{20,28},{24,16},{28,20},{1,9},{5... | collective-permute-start | bytes 1572872 | tf_op jit(solution)/shard_map/ppermute | solution.py:377
  21.3 37.8 %collective-permute-start.2 = (bf16[64,2,16,128]{3,2,1,0:T(8,128)(2,1)}, bf16[64,2,16,128]{3,2,1,0:T(8,128)(2,1)S(1)}, u32[]{:S(2)}, u32[]{:S(2)}) collective-permute-start(bf16[64,2,16,128]{3,2,1,0:T(8,128)(2,1)} %get-tuple-element.54), channel_id=1, source_target_pairs={{0,12},{4,8},{8,4},{12,0},{16,28},{20,24},{24,20},{28,16},{1,13},{... | collective-permute-start | bytes 1572872 | tf_op jit(solution)/shard_map/ppermute | solution.py:377
  21.3 37.8 %collective-permute-start.3 = (bf16[64,2,16,128]{3,2,1,0:T(8,128)(2,1)}, bf16[64,2,16,128]{3,2,1,0:T(8,128)(2,1)}, u32[]{:S(2)}, u32[]{:S(2)}) collective-permute-start(bf16[64,2,16,128]{3,2,1,0:T(8,128)(2,1)} %get-tuple-element.55), channel_id=1, source_target_pairs={{0,16},{4,20},{8,24},{12,28},{16,0},{20,4},{24,8},{28,12},{1,17},{... | collective-permute-start | bytes 1572872 | tf_op jit(solution)/shard_map/ppermute | solution.py:377
  23.0 60.1 %collective-permute-start.4 = (bf16[64,2,16,128]{3,2,1,0:T(8,128)(2,1)}, bf16[64,2,16,128]{3,2,1,0:T(8,128)(2,1)}, u32[]{:S(2)}, u32[]{:S(2)}) collective-permute-start(bf16[64,2,16,128]{3,2,1,0:T(8,128)(2,1)} %get-tuple-element.56), channel_id=1, source_target_pairs={{0,20},{4,16},{8,28},{12,24},{16,4},{20,0},{24,12},{28,8},{1,21},{... | collective-permute-start | bytes 1572872 | tf_op jit(solution)/shard_map/ppermute | solution.py:377
  23.1 31.2 %copy-start.9 = (bf16[64,2,16,128]{3,2,1,0:T(8,128)(2,1)}, bf16[64,2,16,128]{3,2,1,0:T(8,128)(2,1)S(1)}, u32[]{:S(2)}) copy-start(bf16[64,2,16,128]{3,2,1,0:T(8,128)(2,1)S(1)} %collective-permute-done.refs_1_) | copy-start | bytes 1572868
  23.1 60.0 %collective-permute-start.5 = (bf16[64,2,16,128]{3,2,1,0:T(8,128)(2,1)}, bf16[64,2,16,128]{3,2,1,0:T(8,128)(2,1)}, u32[]{:S(2)}, u32[]{:S(2)}) collective-permute-start(bf16[64,2,16,128]{3,2,1,0:T(8,128)(2,1)} %get-tuple-element.57), channel_id=1, source_target_pairs={{0,24},{4,28},{8,16},{12,20},{16,8},{20,12},{24,0},{28,4},{1,25},{... | collective-permute-start | bytes 1572872 | tf_op jit(solution)/shard_map/ppermute | solution.py:377
  45.2 37.9 %collective-permute-start.6 = (bf16[64,2,16,128]{3,2,1,0:T(8,128)(2,1)}, bf16[64,2,16,128]{3,2,1,0:T(8,128)(2,1)}, u32[]{:S(2)}, u32[]{:S(2)}) collective-permute-start(bf16[64,2,16,128]{3,2,1,0:T(8,128)(2,1)} %get-tuple-element.58), channel_id=1, source_target_pairs={{0,28},{4,24},{8,20},{12,16},{16,12},{20,8},{24,4},{28,0},{1,29},{... | collective-permute-start | bytes 1572872 | tf_op jit(solution)/shard_map/ppermute | solution.py:377
  54.8 33.8 %copy-start.16 = (bf16[2,8,16,256]{3,2,1,0:T(8,128)(2,1)S(1)}, bf16[2,8,16,256]{3,2,1,0:T(8,128)(2,1)}, u32[]{:S(2)}) copy-start(bf16[2,8,16,256]{3,2,1,0:T(8,128)(2,1)} %constant.53) | copy-start | bytes 393220
  54.8 34.3 %copy-start.1 = (bf16[256,2,8,16]{0,3,2,1:T(8,128)(2,1)S(1)}, bf16[256,2,8,16]{0,3,2,1:T(8,128)(2,1)}, u32[]{:S(2)}) copy-start(bf16[256,2,8,16]{0,3,2,1:T(8,128)(2,1)} %constant.52) | copy-start | bytes 393220
  59.1 24.0 %copy-start.11 = (bf16[64,2,16,128]{3,2,1,0:T(8,128)(2,1)}, bf16[64,2,16,128]{3,2,1,0:T(8,128)(2,1)S(1)}, u32[]{:S(2)}) copy-start(bf16[64,2,16,128]{3,2,1,0:T(8,128)(2,1)S(1)} %collective-permute-done.2.refs_3_) | copy-start | bytes 1572868
  83.1 52.9 %all-to-all-start.1 = ((bf16[32,64,512]{2,1,0:T(8,128)(2,1)}), bf16[32,64,512]{2,1,0:T(8,128)(2,1)}, u32[]{:S(2)}, u32[]{:S(2)}) async-start(bf16[32,64,512]{2,1,0:T(8,128)(2,1)} %bitcast.10), calls=%async_computation.1 | async-start | bytes 4194304 | tf_op jit(solution)/shard_map/all_to_all | solution.py:366
  86.9 42.2 %collective-permute-start.8 = (bf16[64,2,16,128]{3,2,1,0:T(8,128)(2,1)}, bf16[64,2,16,128]{3,2,1,0:T(8,128)(2,1)S(1)}, u32[]{:S(2)}, u32[]{:S(2)}) collective-permute-start(bf16[64,2,16,128]{3,2,1,0:T(8,128)(2,1)} %get-tuple-element.73), channel_id=1, source_target_pairs={{0,8},{4,12},{8,0},{12,4},{16,24},{20,28},{24,16},{28,20},{1,9},{5... | collective-permute-start | bytes 1572872 | tf_op jit(solution)/shard_map/ppermute | solution.py:377
  88.4 45.4 %collective-permute-start.9 = (bf16[64,2,16,128]{3,2,1,0:T(8,128)(2,1)}, bf16[64,2,16,128]{3,2,1,0:T(8,128)(2,1)S(1)}, u32[]{:S(2)}, u32[]{:S(2)}) collective-permute-start(bf16[64,2,16,128]{3,2,1,0:T(8,128)(2,1)} %get-tuple-element.74), channel_id=1, source_target_pairs={{0,12},{4,8},{8,4},{12,0},{16,28},{20,24},{24,20},{28,16},{1,13},{... | collective-permute-start | bytes 1572872 | tf_op jit(solution)/shard_map/ppermute | solution.py:377
  90.6 54.5 %collective-permute-start.10 = (bf16[64,2,16,128]{3,2,1,0:T(8,128)(2,1)}, bf16[64,2,16,128]{3,2,1,0:T(8,128)(2,1)}, u32[]{:S(2)}, u32[]{:S(2)}) collective-permute-start(bf16[64,2,16,128]{3,2,1,0:T(8,128)(2,1)} %get-tuple-element.75), channel_id=1, source_target_pairs={{0,16},{4,20},{8,24},{12,28},{16,0},{20,4},{24,8},{28,12},{1,17},{... | collective-permute-start | bytes 1572872 | tf_op jit(solution)/shard_map/ppermute | solution.py:377
  92.1 53.0 %collective-permute-start.11 = (bf16[64,2,16,128]{3,2,1,0:T(8,128)(2,1)}, bf16[64,2,16,128]{3,2,1,0:T(8,128)(2,1)}, u32[]{:S(2)}, u32[]{:S(2)}) collective-permute-start(bf16[64,2,16,128]{3,2,1,0:T(8,128)(2,1)} %get-tuple-element.76), channel_id=1, source_target_pairs={{0,20},{4,16},{8,28},{12,24},{16,4},{20,0},{24,12},{28,8},{1,21},{... | collective-permute-start | bytes 1572872 | tf_op jit(solution)/shard_map/ppermute | solution.py:377
  92.7 54.3 %collective-permute-start.12 = (bf16[64,2,16,128]{3,2,1,0:T(8,128)(2,1)}, bf16[64,2,16,128]{3,2,1,0:T(8,128)(2,1)}, u32[]{:S(2)}, u32[]{:S(2)}) collective-permute-start(bf16[64,2,16,128]{3,2,1,0:T(8,128)(2,1)} %get-tuple-element.77), channel_id=1, source_target_pairs={{0,24},{4,28},{8,16},{12,20},{16,8},{20,12},{24,0},{28,4},{1,25},{... | collective-permute-start | bytes 1572872 | tf_op jit(solution)/shard_map/ppermute | solution.py:377
  104.1 25.0 %copy-start.18 = (bf16[64,2,16,128]{3,2,1,0:T(8,128)(2,1)S(1)}, bf16[64,2,16,128]{3,2,1,0:T(8,128)(2,1)}, u32[]{:S(2)}) copy-start(bf16[64,2,16,128]{3,2,1,0:T(8,128)(2,1)} %get-tuple-element.72) | copy-start | bytes 1572868
  104.1 29.7 %copy-start.17 = (bf16[64,2,16,128]{3,2,1,0:T(8,128)(2,1)S(1)}, bf16[64,2,16,128]{3,2,1,0:T(8,128)(2,1)}, u32[]{:S(2)}) copy-start(bf16[64,2,16,128]{3,2,1,0:T(8,128)(2,1)} %get-tuple-element.79) | copy-start | bytes 1572868
  129.1 16.0 %copy-start.12 = (bf16[64,2,16,128]{3,2,1,0:T(8,128)(2,1)}, bf16[64,2,16,128]{3,2,1,0:T(8,128)(2,1)S(1)}, u32[]{:S(2)}) copy-start(bf16[64,2,16,128]{3,2,1,0:T(8,128)(2,1)S(1)} %collective-permute-done.8.refs_2_) | copy-start | bytes 1572868
  129.1 17.9 %collective-permute-start.7 = (bf16[64,2,16,128]{3,2,1,0:T(8,128)(2,1)S(1)}, bf16[64,2,16,128]{3,2,1,0:T(8,128)(2,1)S(1)}, u32[]{:S(2)}, u32[]{:S(2)}) collective-permute-start(bf16[64,2,16,128]{3,2,1,0:T(8,128)(2,1)S(1)} %copy-done.18), channel_id=1, source_target_pairs={{0,4},{4,0},{8,12},{12,8},{16,20},{20,16},{24,28},{28,24},{1,5},{5... | collective-permute-start | bytes 1572872 | tf_op jit(solution)/shard_map/ppermute | solution.py:377
  133.8 23.4 %collective-permute-start.13 = (bf16[64,2,16,128]{3,2,1,0:T(8,128)(2,1)S(1)}, bf16[64,2,16,128]{3,2,1,0:T(8,128)(2,1)S(1)}, u32[]{:S(2)}, u32[]{:S(2)}) collective-permute-start(bf16[64,2,16,128]{3,2,1,0:T(8,128)(2,1)S(1)} %copy-done.17), channel_id=1, source_target_pairs={{0,28},{4,24},{8,20},{12,16},{16,12},{20,8},{24,4},{28,0},{1,29},{... | collective-permute-start | bytes 1572872 | tf_op jit(solution)/shard_map/ppermute | solution.py:377
  158.0 64.7 %all-to-all-start.2 = ((bf16[8,64,2,16,128]{4,3,2,1,0:T(8,128)(2,1)}), bf16[8,64,2,16,128]{4,3,2,1,0:T(8,128)(2,1)}, u32[]{:S(2)}, u32[]{:S(2)}) async-start(bf16[8,64,2,16,128]{4,3,2,1,0:T(8,128)(2,1)} %convolve.2), calls=%async_computation.2 | async-start | bytes 8388608 | tf_op jit(solution)/shard_map/all_to_all | solution.py:366
  187.7 3.8 %collective-permute-start.16 = (bf16[64,2,16,128]{3,2,1,0:T(8,128)(2,1)}, bf16[64,2,16,128]{3,2,1,0:T(8,128)(2,1)S(1)}, u32[]{:S(2)}, u32[]{:S(2)}) collective-permute-start(bf16[64,2,16,128]{3,2,1,0:T(8,128)(2,1)} %get-tuple-element.83), channel_id=1, source_target_pairs={{0,4},{4,0},{8,12},{12,8},{16,20},{20,16},{24,28},{28,24},{1,5},{5... | collective-permute-start | bytes 1572872 | tf_op jit(solution)/shard_map/ppermute | solution.py:377
  188.0 34.4 %collective-permute-start.17 = (bf16[64,2,16,128]{3,2,1,0:T(8,128)(2,1)}, bf16[64,2,16,128]{3,2,1,0:T(8,128)(2,1)S(1)}, u32[]{:S(2)}, u32[]{:S(2)}) collective-permute-start(bf16[64,2,16,128]{3,2,1,0:T(8,128)(2,1)} %get-tuple-element.84), channel_id=1, source_target_pairs={{0,8},{4,12},{8,0},{12,4},{16,24},{20,28},{24,16},{28,20},{1,9},{5... | collective-permute-start | bytes 1572872 | tf_op jit(solution)/shard_map/ppermute | solution.py:377
  189.6 43.1 %collective-permute-start.18 = (bf16[64,2,16,128]{3,2,1,0:T(8,128)(2,1)}, bf16[64,2,16,128]{3,2,1,0:T(8,128)(2,1)S(1)}, u32[]{:S(2)}, u32[]{:S(2)}) collective-permute-start(bf16[64,2,16,128]{3,2,1,0:T(8,128)(2,1)} %get-tuple-element.85), channel_id=1, source_target_pairs={{0,12},{4,8},{8,4},{12,0},{16,28},{20,24},{24,20},{28,16},{1,13},{... | collective-permute-start | bytes 1572872 | tf_op jit(solution)/shard_map/ppermute | solution.py:377
  189.6 43.1 %collective-permute-start.19 = (bf16[64,2,16,128]{3,2,1,0:T(8,128)(2,1)}, bf16[64,2,16,128]{3,2,1,0:T(8,128)(2,1)S(1)}, u32[]{:S(2)}, u32[]{:S(2)}) collective-permute-start(bf16[64,2,16,128]{3,2,1,0:T(8,128)(2,1)} %get-tuple-element.86), channel_id=1, source_target_pairs={{0,16},{4,20},{8,24},{12,28},{16,0},{20,4},{24,8},{28,12},{1,17},{... | collective-permute-start | bytes 1572872 | tf_op jit(solution)/shard_map/ppermute | solution.py:377
  191.3 41.4 %collective-permute-start.20 = (bf16[64,2,16,128]{3,2,1,0:T(8,128)(2,1)}, bf16[64,2,16,128]{3,2,1,0:T(8,128)(2,1)}, u32[]{:S(2)}, u32[]{:S(2)}) collective-permute-start(bf16[64,2,16,128]{3,2,1,0:T(8,128)(2,1)} %get-tuple-element.87), channel_id=1, source_target_pairs={{0,20},{4,16},{8,28},{12,24},{16,4},{20,0},{24,12},{28,8},{1,21},{... | collective-permute-start | bytes 1572872 | tf_op jit(solution)/shard_map/ppermute | solution.py:377
  191.5 40.8 %copy-start.3 = (bf16[64,2,16,128]{3,2,1,0:T(8,128)(2,1)}, bf16[64,2,16,128]{3,2,1,0:T(8,128)(2,1)S(1)}, u32[]{:S(2)}) copy-start(bf16[64,2,16,128]{3,2,1,0:T(8,128)(2,1)S(1)} %collective-permute-done.16.refs_1_) | copy-start | bytes 1572868
  191.5 54.3 %collective-permute-start.14 = (bf16[64,2,16,128]{3,2,1,0:T(8,128)(2,1)}, bf16[64,2,16,128]{3,2,1,0:T(8,128)(2,1)S(1)}, u32[]{:S(2)}, u32[]{:S(2)}) collective-permute-start(bf16[64,2,16,128]{3,2,1,0:T(8,128)(2,1)} %get-tuple-element.80), channel_id=1, source_target_pairs={{0,24},{4,28},{8,16},{12,20},{16,8},{20,12},{24,0},{28,4},{1,25},{... | collective-permute-start | bytes 1572872 | tf_op jit(solution)/shard_map/ppermute | solution.py:377
  222.4 33.7 %collective-permute-start.15 = (bf16[64,2,16,128]{3,2,1,0:T(8,128)(2,1)}, bf16[64,2,16,128]{3,2,1,0:T(8,128)(2,1)S(1)}, u32[]{:S(2)}, u32[]{:S(2)}) collective-permute-start(bf16[64,2,16,128]{3,2,1,0:T(8,128)(2,1)} %get-tuple-element.81), channel_id=1, source_target_pairs={{0,28},{4,24},{8,20},{12,16},{16,12},{20,8},{24,4},{28,0},{1,29},{... | collective-permute-start | bytes 1572872 | tf_op jit(solution)/shard_map/ppermute | solution.py:377
  (11 other events, 75.0 us)

commit v5 on v4

--- a/solution.py
+++ b/solution.py
@@ -286,22 +286,27 @@
 def finish_kernel(pieces_count, me_ref, skip_ref, key_ref, value_ref, query_ref, grad_ref, *refs):
     pieces = refs[:pieces_count]
     out_ref, query_out, key_out, value_out, scratch = refs[-5:]
-    tokens, width = key_ref.shape
-    local = tokens // LANES
+    share, width = key_ref.shape
+    local = pieces[0].shape[-2]
     pitch = local + 1
+    half = pl.program_id(1)
     inner = pieces[0].shape[-4]
     dests = width // inner
     mine = lax.rem(me_ref[0], dests)
     skip = skip_ref[...]
     if pieces_count == 1:
-        for slot in range(dests):
-            for side in range(2):
-                for index in range(inner):
-                    row = (slot * inner + index) * pitch
-                    scratch[side, row : row + local, :] = pieces[0][slot, index, side].astype(f32)
+
+        @pl.when(half == 0)
+        def _():
+            for slot in range(dests):
+                for side in range(2):
+                    for index in range(inner):
+                        row = (slot * inner + index) * pitch
+                        scratch[side, row : row + local, :] = pieces[0][slot, index, side].astype(f32)
+
     for block in range(pieces_count // dests):
 
-        @pl.when(pl.program_id(0) == block)
+        @pl.when(jnp.logical_and(pl.program_id(0) == block, half == 0))
         def _():
             for slot in range(dests):
                 base = (mine ^ slot) * (inner * pitch)
@@ -311,12 +316,13 @@
                             block * dests + slot
                         ][index, side].astype(f32)
 
-    for row in range(local):
+    first = half * (share // LANES)
+    for row in range(share // LANES):
         place = slice(row * LANES, (row + 1) * LANES)
         key, value = key_ref[place, :].astype(f32), value_ref[place, :].astype(f32)
         query, grad = query_ref[place, :].astype(f32), grad_ref[place, :].astype(f32)
-        convolved = scratch[0, pl.ds(row, width, stride=pitch), :].T
-        reflected = scratch[1, pl.ds(row, width, stride=pitch), :].T
+        convolved = scratch[0, pl.ds(first + row, width, stride=pitch), :].T
+        reflected = scratch[1, pl.ds(first + row, width, stride=pitch), :].T
         summed = convolved + skip * (key * value).astype(bf16).astype(f32)
         grad_sum = reflected + skip * (grad * query).astype(bf16).astype(f32)
         out_ref[place, :] = (query * summed).astype(bf16)
@@ -334,21 +340,21 @@
     if not whole:
         pieces = pieces[spots[0] * dests : (spots[-1] + 1) * dests]
 
-    def place(step, me):
-        return 0, part * blocks + (step if whole else (me[0] // dests) ^ (spots[0] + step))
-
-    column = pl.BlockSpec((tokens, LANES), place)
+    def place(step, half, me):
+        return half, part * blocks + (step if whole else (me[0] // dests) ^ (spots[0] + step))
+
+    column = pl.BlockSpec((tokens // 2, LANES), place)
     if whole:
-        piece = pl.BlockSpec((dests, inner, 2, local, LANES), lambda step, me: (step, 0, 0, 0, 0))
+        piece = pl.BlockSpec((dests, inner, 2, local, LANES), lambda step, half, me: (step, 0, 0, 0, 0))
     else:
-        piece = pl.BlockSpec(pieces[0].shape, lambda step, me: (0, 0, 0, 0))
+        piece = pl.BlockSpec(pieces[0].shape, lambda step, half, me: (0, 0, 0, 0))
     return pl.pallas_call(
         functools.partial(finish_kernel, len(pieces)),
         out_shape=[jax.ShapeDtypeStruct(key_proj.shape, bf16)] * 4,
         grid_spec=pltpu.PrefetchScalarGridSpec(
             num_scalar_prefetch=1,
-            grid=(len(spots),),
-            in_specs=[pl.BlockSpec((1, LANES), place)]
+            grid=(len(spots), 2),
+            in_specs=[pl.BlockSpec((1, LANES), lambda step, half, me: (0, place(step, half, me)[1]))]
             + [column] * 4
             + [piece] * len(pieces)
             + [pl.BlockSpec(memory_space=pl.ANY)] * len(previous),

time: 262 us -> 262 us (level)
  Pallas kernels: 107 us -> 110 us
  waiting for transfers between devices: 105 us -> 102 us
    ppermute x21, waiting for transfers between devices: 105 us -> 102 us  [exchange(): lax.ppermute(pieces[step], axis, [(i, i ^ step) for i in range(count)])]
    pallas_call x3, Pallas kernels: 22.5 us -> 25.5 us  [finish(): pl.pallas_call(functools.partial(finish_kernel, len(pieces)), out_shape=[...]
  transfers between devices with their start and end apart: 24 -> 24, of which waited for: 10 -> 9; matrix products, arithmetic and copies ran while one was open for 2% -> 2% of each run, Pallas kernels for 40% -> 41%
where the time goes in v5:
time: 262 us; the launch traced here: 261 us
  Pallas kernels  110 us (42%)
  waiting for transfers between devices  102 us (39%)
  starting transfers between devices  37.3 us (14%)
  local copies, waits for them, and re-layouts  9.18 us (4%)
    ppermute x21, waiting for transfers between devices, exchange(): lax.ppermute(pieces[step], axis, [(i, i ^ step) for i in range(count)])  102 us
    pallas_call x2, Pallas kernels, convolve(): pl.pallas_call(functools.partial(convolve_kernel, group, sources), out_sh...  49.8 us
    pallas_call x3, Pallas kernels, finish(): pl.pallas_call(functools.partial(finish_kernel, len(pieces)), out_shape=[...  25.5 us
    ppermute x21, starting transfers between devices, exchange(): lax.ppermute(pieces[step], axis, [(i, i ^ step) for i in range(count)])  21.5 us
    pallas_call x2, Pallas kernels, filter_spectrum(): pl.pallas_call(functools.partial(spectrum_kernel, len(pieces), group), ou...  18.2 us
    pallas_call x2, Pallas kernels, gate(): pl.pallas_call(gate_kernel, out_shape=[jax.ShapeDtypeStruct(piece, bf16)]...  16.9 us
    all_to_all x3, starting transfers between devices, swap(): return lax.all_to_all(value, axis, split_axis=0, concat_axis=0, tiled=True)  15.8 us
  transfers between devices with their start and end apart: 24, of which 9 were waited for; matrix products, arithmetic and copies ran while one was open for 2% of the time, Pallas kernels for 41%

profile of v5, /device:TPU:0, one launch (start us, length us, event | category | flops | bytes accessed | tf_op | source)
XLA Modules:
  0.0 260.7 jit_solution(11343776534350055353)
XLA Ops:
  0.6 3.1 %slice.12 = bf16[4,1,8,64,512]{4,3,2,1,0:T(8,128)(2,1)} slice(bf16[4,2,8,64,512]{4,3,2,1,0:T(8,128)(2,1)} %bitcast.17), slice={[0:4], [0:1], [0:8], [0:64], [0:512]} | slice | bytes 4194304 | tf_op jit(solution)/shard_map/slice | solution.py:415
  3.8 7.3 %all-to-all-start = ((bf16[32,64,512]{2,1,0:T(8,128)(2,1)}), bf16[32,64,512]{2,1,0:T(8,128)(2,1)S(1)}, u32[]{:S(2)}, u32[]{:S(2)}) async-start(bf16[32,64,512]{2,1,0:T(8,128)(2,1)} %bitcast.8), calls=%async_computation | async-start | bytes 4194304 | tf_op jit(solution)/shard_map/all_to_all | solution.py:372
  11.1 8.3 %gate.2 = (bf16[64,2,16,128]{3,2,1,0:T(8,128)(2,1)}, bf16[64,2,16,128]{3,2,1,0:T(8,128)(2,1)}, bf16[64,2,16,128]{3,2,1,0:T(8,128)(2,1)}, bf16[64,2,16,128]{3,2,1...) custom-call(s32[1]{0:T(128)} %bitcast.me_ref, ...), custom_call_target="tpu_custom_call" | custom-call | bytes 1048576 | tf_op jit(solution)/shard_map/gate/pallas_call | solution.py:270
  19.6 1.7 collective-permute-start.1
  21.3 1.7 collective-permute-start.3
  23.1 2.6 collective-permute-start.5
  25.7 19.6 %collective-permute-done.1.refs_2_ = bf16[64,2,16,128]{3,2,1,0:T(8,128)(2,1)S(1)} collective-permute-done((bf16[64,2,16,128]{3,2,1,0:T(8,128)(2,1)}, bf16[64,2,16,128]{3,2,1,0:T(8,128)(2,1)S(1)}, u32[]{:S(2)}, u32[]{:S(2)}) %collective-permute-start.1) | collective-permute-done | bytes 524320 | tf_op jit(solution)/shard_map/ppermute | solution.py:383
  45.6 8.7 %gate.3 = (bf16[64,2,16,128]{3,2,1,0:T(8,128)(2,1)}, bf16[64,2,16,128]{3,2,1,0:T(8,128)(2,1)}, bf16[64,2,16,128]{3,2,1,0:T(8,128)(2,1)}, bf16[64,2,16,128]{3,2,1...) custom-call(s32[1]{0:T(128)} %bitcast.me_ref, ...), custom_call_target="tpu_custom_call" | custom-call | bytes 1048576 | tf_op jit(solution)/shard_map/gate/pallas_call | solution.py:270
  54.8 1.5 slice.13
  56.4 2.7 %collective-permute-done.2.refs_3_ = bf16[64,2,16,128]{3,2,1,0:T(8,128)(2,1)S(1)} collective-permute-done((bf16[64,2,16,128]{3,2,1,0:T(8,128)(2,1)}, bf16[64,2,16,128]{3,2,1,0:T(8,128)(2,1)S(1)}, u32[]{:S(2)}, u32[]{:S(2)}) %collective-permute-start.2) | collective-permute-done | bytes 524320 | tf_op jit(solution)/shard_map/ppermute | solution.py:383
  59.1 24.0 %collective-permute-done.4.refs_5_ = bf16[64,2,16,128]{3,2,1,0:T(8,128)(2,1)} collective-permute-done((bf16[64,2,16,128]{3,2,1,0:T(8,128)(2,1)}, bf16[64,2,16,128]{3,2,1,0:T(8,128)(2,1)}, u32[]{:S(2)}, u32[]{:S(2)}) %collective-permute-start.4) | collective-permute-done | bytes 524320 | tf_op jit(solution)/shard_map/ppermute | solution.py:383
  83.1 3.7 %all-to-all-start.1 = ((bf16[32,64,512]{2,1,0:T(8,128)(2,1)}), bf16[32,64,512]{2,1,0:T(8,128)(2,1)}, u32[]{:S(2)}, u32[]{:S(2)}) async-start(bf16[32,64,512]{2,1,0:T(8,128)(2,1)} %bitcast.10), calls=%async_computation.1 | async-start | bytes 4194304 | tf_op jit(solution)/shard_map/all_to_all | solution.py:372
  86.9 1.5 collective-permute-start.8
  90.6 1.5 collective-permute-start.10
  92.7 2.3 collective-permute-start.12
  95.0 9.1 %filter_spectrum.2.filter_ref = f32[64,128,256]{2,1,0:T(8,128)} custom-call(bf16[256,256]{1,0:T(8,128)(2,1)} %constant.46.clone.lead_ref, bf16[768,256]{1,0:T(8,128)(2,1)} %constant.49.clone.trail_ref, f32[2,128,128]{2,1,0:T(8,128)} %constant.51.clone.twist_ref, bf16[32,1,64,512]{3,2,1,0:T(8,128)(2,1)} %bitcast.19), custom_call_target="tpu_custom_call" | custom-call | flops 64000000 | bytes 1048576 | tf_op jit(solution)/shard_map/filter_spectrum/pallas_call | solution.py:116
  104.1 25.0 %convolve.2 = bf16[8,64,2,16,128]{4,3,2,1,0:T(8,128)(2,1)} custom-call(bf16[256,256]{1,0:T(8,128)(2,1)} %get-tuple-element.99.lead_ref, bf16[256,256]{1,0:T(8,128)(2,1)} %constant.48.clone.inv_ref, bf16[768,256]{1,0:T(8,128)(2,1)} %constant.49.clone.trail_ref, bf16[768,256]{1,0:T(8,128)(2,1)} %constant.50.clone.back_ref, ...), custom_call_target="tpu_custom_call" | custom-call | flops 64000000 | bytes 1048576 | tf_op jit(solution)/shard_map/convolve/pallas_call | solution.py:209
  129.2 4.6 %collective-permute-done.9.refs_3_ = bf16[64,2,16,128]{3,2,1,0:T(8,128)(2,1)S(1)} collective-permute-done((bf16[64,2,16,128]{3,2,1,0:T(8,128)(2,1)}, bf16[64,2,16,128]{3,2,1,0:T(8,128)(2,1)S(1)}, u32[]{:S(2)}, u32[]{:S(2)}) %collective-permute-start.9) | collective-permute-done | bytes 524320 | tf_op jit(solution)/shard_map/ppermute | solution.py:383
  133.8 2.2 collective-permute-start.13
  136.0 9.1 %filter_spectrum.3.filter_ref = f32[64,128,256]{2,1,0:T(8,128)} custom-call(bf16[256,256]{1,0:T(8,128)(2,1)} %constant.46.clone.lead_ref, bf16[768,256]{1,0:T(8,128)(2,1)} %constant.49.clone.trail_ref, f32[2,128,128]{2,1,0:T(8,128)} %constant.51.clone.twist_ref, bf16[32,1,64,512]{3,2,1,0:T(8,128)(2,1)} %bitcast.11.refs_0_), custom_call_target="tpu_custom_call" | custom-call | flops 64000000 | bytes 1048576 | tf_op jit(solution)/shard_map/filter_spectrum/pallas_call | solution.py:116
  145.2 1.8 collective-permute-done.12.refs_6_
  147.0 10.2 %collective-permute-done.13.refs_7_ = bf16[64,2,16,128]{3,2,1,0:T(8,128)(2,1)S(1)} collective-permute-done((bf16[64,2,16,128]{3,2,1,0:T(8,128)(2,1)S(1)}, bf16[64,2,16,128]{3,2,1,0:T(8,128)(2,1)S(1)}, u32[]{:S(2)}, u32[]{:S(2)}) %collective-permute-start.13) | collective-permute-done | bytes 524320 | tf_op jit(solution)/shard_map/ppermute | solution.py:383
  158.0 4.8 %all-to-all-start.2 = ((bf16[8,64,2,16,128]{4,3,2,1,0:T(8,128)(2,1)}), bf16[8,64,2,16,128]{4,3,2,1,0:T(8,128)(2,1)}, u32[]{:S(2)}, u32[]{:S(2)}) async-start(bf16[8,64,2,16,128]{4,3,2,1,0:T(8,128)(2,1)} %convolve.2), calls=%async_computation.2 | async-start | bytes 8388608 | tf_op jit(solution)/shard_map/all_to_all | solution.py:372
  162.8 24.9 %convolve.3 = (bf16[64,2,16,128]{3,2,1,0:T(8,128)(2,1)}, bf16[64,2,16,128]{3,2,1,0:T(8,128)(2,1)}, bf16[64,2,16,128]{3,2,1,0:T(8,128)(2,1)}, bf16[64,2,16,128]{3...) custom-call(bf16[256,256]{1,0:T(8,128)(2,1)} %get-tuple-element.99.l, ...), custom_call_target="tpu_custom_call" | custom-call | flops 64000000 | bytes 1048576 | tf_op jit(solution)/shard_map/convolve/pallas_call | solution.py:209
  188.0 1.6 collective-permute-start.17
  189.6 1.7 collective-permute-start.19
  191.5 2.5 collective-permute-start.14
  194.0 28.4 %collective-permute-done.17.refs_2_ = bf16[64,2,16,128]{3,2,1,0:T(8,128)(2,1)S(1)} collective-permute-done((bf16[64,2,16,128]{3,2,1,0:T(8,128)(2,1)}, bf16[64,2,16,128]{3,2,1,0:T(8,128)(2,1)S(1)}, u32[]{:S(2)}, u32[]{:S(2)}) %collective-permute-start.17) | collective-permute-done | bytes 524320 | tf_op jit(solution)/shard_map/ppermute | solution.py:383
  222.6 12.3 %finish.3 = (bf16[2048,1024]{1,0:T(8,128)(2,1)}, bf16[2048,1024]{1,0:T(8,128)(2,1)}, bf16[2048,1024]{1,0:T(8,128)(2,1)}, bf16[2048,1024]{1,0:T(8,128)(2,1)}) custom-call(s32[1]{0:T(128)} %bitcast.me_ref, f32[1,1024]{1,0:T(1,128)} %bitcast.22, bf16[2048,1024]{1,0:T(8,128)(2,1)} %key_ref.9, bf16[2048,1024]{1,0:T(8,128)(2,1)} %value_ref.9, ...), custom_call_target="tpu_custom_call" | custom-call | bytes 1048576 | tf_op jit(solution)/shard_map/finish/pallas_call | solution.py:351
  236.0 9.4 %finish.4 = (bf16[2048,1024]{1,0:T(8,128)(2,1)}, bf16[2048,1024]{1,0:T(8,128)(2,1)}, bf16[2048,1024]{1,0:T(8,128)(2,1)}, bf16[2048,1024]{1,0:T(8,128)(2,1)}) custom-call(s32[1]{0:T(128)} %bitcast.me_ref, f32[1,1024]{1,0:T(1,128)} %bitcast.23, ...), custom_call_target="tpu_custom_call", output_to_operand_aliasing={{0}: (12, {}), {1}: (13, {}), {2}: (14, {}), {3}: (15, {})} | custom-call | bytes 1048576 | tf_op jit(solution)/shard_map/finish/pallas_call | solution.py:351
  245.8 10.3 %collective-permute-done.15.refs_1_ = bf16[64,2,16,128]{3,2,1,0:T(8,128)(2,1)S(1)} collective-permute-done((bf16[64,2,16,128]{3,2,1,0:T(8,128)(2,1)}, bf16[64,2,16,128]{3,2,1,0:T(8,128)(2,1)S(1)}, u32[]{:S(2)}, u32[]{:S(2)}) %collective-permute-start.15) | collective-permute-done | bytes 524320 | tf_op jit(solution)/shard_map/ppermute | solution.py:383
  256.9 3.8 %finish.5 = (bf16[2048,1024]{1,0:T(8,128)(2,1)}, bf16[2048,1024]{1,0:T(8,128)(2,1)}, bf16[2048,1024]{1,0:T(8,128)(2,1)}, bf16[2048,1024]{1,0:T(8,128)(2,1)}) custom-call(s32[1]{0:T(128)} %bitcast.me_ref, f32[1,1024]{1,0:T(1,128)} %bitcast.24, bf16[2048,1024]{1,0:T(8,128)(2,1)} %key_ref.9, ...), custom_call_target="tpu_custom_call", output_to_operand_aliasing={{0}: (8, {}), {1}: (9, {}), {2}: (10, {}), {3}: (11, {})} | custom-call | bytes 1048576 | tf_op jit(solution)/shard_map/finish/pallas_call | solution.py:351
  (77 shorter events, 7.9 us)
Async XLA Ops:
  3.8 79.4 %all-to-all-start = ((bf16[32,64,512]{2,1,0:T(8,128)(2,1)}), bf16[32,64,512]{2,1,0:T(8,128)(2,1)S(1)}, u32[]{:S(2)}, u32[]{:S(2)}) async-start(bf16[32,64,512]{2,1,0:T(8,128)(2,1)} %bitcast.8), calls=%async_computation | async-start | bytes 4194304 | tf_op jit(solution)/shard_map/all_to_all | solution.py:372
  19.3 3.7 %collective-permute-start = (bf16[64,2,16,128]{3,2,1,0:T(8,128)(2,1)}, bf16[64,2,16,128]{3,2,1,0:T(8,128)(2,1)S(1)}, u32[]{:S(2)}, u32[]{:S(2)}) collective-permute-start(bf16[64,2,16,128]{3,2,1,0:T(8,128)(2,1)} %get-tuple-element.52), channel_id=1, source_target_pairs={{0,4},{4,0},{8,12},{12,8},{16,20},{20,16},{24,28},{28,24},{1,5},{5... | collective-permute-start | bytes 1572872 | tf_op jit(solution)/shard_map/ppermute | solution.py:383
  19.6 25.6 %collective-permute-start.1 = (bf16[64,2,16,128]{3,2,1,0:T(8,128)(2,1)}, bf16[64,2,16,128]{3,2,1,0:T(8,128)(2,1)S(1)}, u32[]{:S(2)}, u32[]{:S(2)}) collective-permute-start(bf16[64,2,16,128]{3,2,1,0:T(8,128)(2,1)} %get-tuple-element.53), channel_id=1, source_target_pairs={{0,8},{4,12},{8,0},{12,4},{16,24},{20,28},{24,16},{28,20},{1,9},{5... | collective-permute-start | bytes 1572872 | tf_op jit(solution)/shard_map/ppermute | solution.py:383
  21.3 37.8 %collective-permute-start.2 = (bf16[64,2,16,128]{3,2,1,0:T(8,128)(2,1)}, bf16[64,2,16,128]{3,2,1,0:T(8,128)(2,1)S(1)}, u32[]{:S(2)}, u32[]{:S(2)}) collective-permute-start(bf16[64,2,16,128]{3,2,1,0:T(8,128)(2,1)} %get-tuple-element.54), channel_id=1, source_target_pairs={{0,12},{4,8},{8,4},{12,0},{16,28},{20,24},{24,20},{28,16},{1,13},{... | collective-permute-start | bytes 1572872 | tf_op jit(solution)/shard_map/ppermute | solution.py:383
  21.3 37.8 %collective-permute-start.3 = (bf16[64,2,16,128]{3,2,1,0:T(8,128)(2,1)}, bf16[64,2,16,128]{3,2,1,0:T(8,128)(2,1)}, u32[]{:S(2)}, u32[]{:S(2)}) collective-permute-start(bf16[64,2,16,128]{3,2,1,0:T(8,128)(2,1)} %get-tuple-element.55), channel_id=1, source_target_pairs={{0,16},{4,20},{8,24},{12,28},{16,0},{20,4},{24,8},{28,12},{1,17},{... | collective-permute-start | bytes 1572872 | tf_op jit(solution)/shard_map/ppermute | solution.py:383
  23.0 60.1 %collective-permute-start.4 = (bf16[64,2,16,128]{3,2,1,0:T(8,128)(2,1)}, bf16[64,2,16,128]{3,2,1,0:T(8,128)(2,1)}, u32[]{:S(2)}, u32[]{:S(2)}) collective-permute-start(bf16[64,2,16,128]{3,2,1,0:T(8,128)(2,1)} %get-tuple-element.56), channel_id=1, source_target_pairs={{0,20},{4,16},{8,28},{12,24},{16,4},{20,0},{24,12},{28,8},{1,21},{... | collective-permute-start | bytes 1572872 | tf_op jit(solution)/shard_map/ppermute | solution.py:383
  23.1 31.2 %copy-start.9 = (bf16[64,2,16,128]{3,2,1,0:T(8,128)(2,1)}, bf16[64,2,16,128]{3,2,1,0:T(8,128)(2,1)S(1)}, u32[]{:S(2)}) copy-start(bf16[64,2,16,128]{3,2,1,0:T(8,128)(2,1)S(1)} %collective-permute-done.refs_1_) | copy-start | bytes 1572868
  23.1 60.0 %collective-permute-start.5 = (bf16[64,2,16,128]{3,2,1,0:T(8,128)(2,1)}, bf16[64,2,16,128]{3,2,1,0:T(8,128)(2,1)}, u32[]{:S(2)}, u32[]{:S(2)}) collective-permute-start(bf16[64,2,16,128]{3,2,1,0:T(8,128)(2,1)} %get-tuple-element.57), channel_id=1, source_target_pairs={{0,24},{4,28},{8,16},{12,20},{16,8},{20,12},{24,0},{28,4},{1,25},{... | collective-permute-start | bytes 1572872 | tf_op jit(solution)/shard_map/ppermute | solution.py:383
  45.2 37.9 %collective-permute-start.6 = (bf16[64,2,16,128]{3,2,1,0:T(8,128)(2,1)}, bf16[64,2,16,128]{3,2,1,0:T(8,128)(2,1)}, u32[]{:S(2)}, u32[]{:S(2)}) collective-permute-start(bf16[64,2,16,128]{3,2,1,0:T(8,128)(2,1)} %get-tuple-element.58), channel_id=1, source_target_pairs={{0,28},{4,24},{8,20},{12,16},{16,12},{20,8},{24,4},{28,0},{1,29},{... | collective-permute-start | bytes 1572872 | tf_op jit(solution)/shard_map/ppermute | solution.py:383
  54.8 33.8 %copy-start.16 = (bf16[2,8,16,256]{3,2,1,0:T(8,128)(2,1)S(1)}, bf16[2,8,16,256]{3,2,1,0:T(8,128)(2,1)}, u32[]{:S(2)}) copy-start(bf16[2,8,16,256]{3,2,1,0:T(8,128)(2,1)} %constant.53) | copy-start | bytes 393220
  54.8 34.3 %copy-start.1 = (bf16[256,2,8,16]{0,3,2,1:T(8,128)(2,1)S(1)}, bf16[256,2,8,16]{0,3,2,1:T(8,128)(2,1)}, u32[]{:S(2)}) copy-start(bf16[256,2,8,16]{0,3,2,1:T(8,128)(2,1)} %constant.52) | copy-start | bytes 393220
  59.1 24.0 %copy-start.11 = (bf16[64,2,16,128]{3,2,1,0:T(8,128)(2,1)}, bf16[64,2,16,128]{3,2,1,0:T(8,128)(2,1)S(1)}, u32[]{:S(2)}) copy-start(bf16[64,2,16,128]{3,2,1,0:T(8,128)(2,1)S(1)} %collective-permute-done.2.refs_3_) | copy-start | bytes 1572868
  83.1 52.9 %all-to-all-start.1 = ((bf16[32,64,512]{2,1,0:T(8,128)(2,1)}), bf16[32,64,512]{2,1,0:T(8,128)(2,1)}, u32[]{:S(2)}, u32[]{:S(2)}) async-start(bf16[32,64,512]{2,1,0:T(8,128)(2,1)} %bitcast.10), calls=%async_computation.1 | async-start | bytes 4194304 | tf_op jit(solution)/shard_map/all_to_all | solution.py:372
  86.9 42.2 %collective-permute-start.8 = (bf16[64,2,16,128]{3,2,1,0:T(8,128)(2,1)}, bf16[64,2,16,128]{3,2,1,0:T(8,128)(2,1)S(1)}, u32[]{:S(2)}, u32[]{:S(2)}) collective-permute-start(bf16[64,2,16,128]{3,2,1,0:T(8,128)(2,1)} %get-tuple-element.73), channel_id=1, source_target_pairs={{0,8},{4,12},{8,0},{12,4},{16,24},{20,28},{24,16},{28,20},{1,9},{5... | collective-permute-start | bytes 1572872 | tf_op jit(solution)/shard_map/ppermute | solution.py:383
  88.4 45.4 %collective-permute-start.9 = (bf16[64,2,16,128]{3,2,1,0:T(8,128)(2,1)}, bf16[64,2,16,128]{3,2,1,0:T(8,128)(2,1)S(1)}, u32[]{:S(2)}, u32[]{:S(2)}) collective-permute-start(bf16[64,2,16,128]{3,2,1,0:T(8,128)(2,1)} %get-tuple-element.74), channel_id=1, source_target_pairs={{0,12},{4,8},{8,4},{12,0},{16,28},{20,24},{24,20},{28,16},{1,13},{... | collective-permute-start | bytes 1572872 | tf_op jit(solution)/shard_map/ppermute | solution.py:383
  90.6 54.5 %collective-permute-start.10 = (bf16[64,2,16,128]{3,2,1,0:T(8,128)(2,1)}, bf16[64,2,16,128]{3,2,1,0:T(8,128)(2,1)}, u32[]{:S(2)}, u32[]{:S(2)}) collective-permute-start(bf16[64,2,16,128]{3,2,1,0:T(8,128)(2,1)} %get-tuple-element.75), channel_id=1, source_target_pairs={{0,16},{4,20},{8,24},{12,28},{16,0},{20,4},{24,8},{28,12},{1,17},{... | collective-permute-start | bytes 1572872 | tf_op jit(solution)/shard_map/ppermute | solution.py:383
  92.1 53.0 %collective-permute-start.11 = (bf16[64,2,16,128]{3,2,1,0:T(8,128)(2,1)}, bf16[64,2,16,128]{3,2,1,0:T(8,128)(2,1)}, u32[]{:S(2)}, u32[]{:S(2)}) collective-permute-start(bf16[64,2,16,128]{3,2,1,0:T(8,128)(2,1)} %get-tuple-element.76), channel_id=1, source_target_pairs={{0,20},{4,16},{8,28},{12,24},{16,4},{20,0},{24,12},{28,8},{1,21},{... | collective-permute-start | bytes 1572872 | tf_op jit(solution)/shard_map/ppermute | solution.py:383
  92.7 54.3 %collective-permute-start.12 = (bf16[64,2,16,128]{3,2,1,0:T(8,128)(2,1)}, bf16[64,2,16,128]{3,2,1,0:T(8,128)(2,1)}, u32[]{:S(2)}, u32[]{:S(2)}) collective-permute-start(bf16[64,2,16,128]{3,2,1,0:T(8,128)(2,1)} %get-tuple-element.77), channel_id=1, source_target_pairs={{0,24},{4,28},{8,16},{12,20},{16,8},{20,12},{24,0},{28,4},{1,25},{... | collective-permute-start | bytes 1572872 | tf_op jit(solution)/shard_map/ppermute | solution.py:383
  104.1 25.0 %copy-start.18 = (bf16[64,2,16,128]{3,2,1,0:T(8,128)(2,1)S(1)}, bf16[64,2,16,128]{3,2,1,0:T(8,128)(2,1)}, u32[]{:S(2)}) copy-start(bf16[64,2,16,128]{3,2,1,0:T(8,128)(2,1)} %get-tuple-element.72) | copy-start | bytes 1572868
  104.1 29.7 %copy-start.17 = (bf16[64,2,16,128]{3,2,1,0:T(8,128)(2,1)S(1)}, bf16[64,2,16,128]{3,2,1,0:T(8,128)(2,1)}, u32[]{:S(2)}) copy-start(bf16[64,2,16,128]{3,2,1,0:T(8,128)(2,1)} %get-tuple-element.79) | copy-start | bytes 1572868
  129.1 16.0 %copy-start.12 = (bf16[64,2,16,128]{3,2,1,0:T(8,128)(2,1)}, bf16[64,2,16,128]{3,2,1,0:T(8,128)(2,1)S(1)}, u32[]{:S(2)}) copy-start(bf16[64,2,16,128]{3,2,1,0:T(8,128)(2,1)S(1)} %collective-permute-done.8.refs_2_) | copy-start | bytes 1572868
  129.1 17.9 %collective-permute-start.7 = (bf16[64,2,16,128]{3,2,1,0:T(8,128)(2,1)S(1)}, bf16[64,2,16,128]{3,2,1,0:T(8,128)(2,1)S(1)}, u32[]{:S(2)}, u32[]{:S(2)}) collective-permute-start(bf16[64,2,16,128]{3,2,1,0:T(8,128)(2,1)S(1)} %copy-done.18), channel_id=1, source_target_pairs={{0,4},{4,0},{8,12},{12,8},{16,20},{20,16},{24,28},{28,24},{1,5},{5... | collective-permute-start | bytes 1572872 | tf_op jit(solution)/shard_map/ppermute | solution.py:383
  133.8 23.4 %collective-permute-start.13 = (bf16[64,2,16,128]{3,2,1,0:T(8,128)(2,1)S(1)}, bf16[64,2,16,128]{3,2,1,0:T(8,128)(2,1)S(1)}, u32[]{:S(2)}, u32[]{:S(2)}) collective-permute-start(bf16[64,2,16,128]{3,2,1,0:T(8,128)(2,1)S(1)} %copy-done.17), channel_id=1, source_target_pairs={{0,28},{4,24},{8,20},{12,16},{16,12},{20,8},{24,4},{28,0},{1,29},{... | collective-permute-start | bytes 1572872 | tf_op jit(solution)/shard_map/ppermute | solution.py:383
  158.0 64.7 %all-to-all-start.2 = ((bf16[8,64,2,16,128]{4,3,2,1,0:T(8,128)(2,1)}), bf16[8,64,2,16,128]{4,3,2,1,0:T(8,128)(2,1)}, u32[]{:S(2)}, u32[]{:S(2)}) async-start(bf16[8,64,2,16,128]{4,3,2,1,0:T(8,128)(2,1)} %convolve.2), calls=%async_computation.2 | async-start | bytes 8388608 | tf_op jit(solution)/shard_map/all_to_all | solution.py:372
  187.7 3.8 %collective-permute-start.16 = (bf16[64,2,16,128]{3,2,1,0:T(8,128)(2,1)}, bf16[64,2,16,128]{3,2,1,0:T(8,128)(2,1)S(1)}, u32[]{:S(2)}, u32[]{:S(2)}) collective-permute-start(bf16[64,2,16,128]{3,2,1,0:T(8,128)(2,1)} %get-tuple-element.83), channel_id=1, source_target_pairs={{0,4},{4,0},{8,12},{12,8},{16,20},{20,16},{24,28},{28,24},{1,5},{5... | collective-permute-start | bytes 1572872 | tf_op jit(solution)/shard_map/ppermute | solution.py:383
  188.0 34.4 %collective-permute-start.17 = (bf16[64,2,16,128]{3,2,1,0:T(8,128)(2,1)}, bf16[64,2,16,128]{3,2,1,0:T(8,128)(2,1)S(1)}, u32[]{:S(2)}, u32[]{:S(2)}) collective-permute-start(bf16[64,2,16,128]{3,2,1,0:T(8,128)(2,1)} %get-tuple-element.84), channel_id=1, source_target_pairs={{0,8},{4,12},{8,0},{12,4},{16,24},{20,28},{24,16},{28,20},{1,9},{5... | collective-permute-start | bytes 1572872 | tf_op jit(solution)/shard_map/ppermute | solution.py:383
  189.6 45.4 %collective-permute-start.18 = (bf16[64,2,16,128]{3,2,1,0:T(8,128)(2,1)}, bf16[64,2,16,128]{3,2,1,0:T(8,128)(2,1)S(1)}, u32[]{:S(2)}, u32[]{:S(2)}) collective-permute-start(bf16[64,2,16,128]{3,2,1,0:T(8,128)(2,1)} %get-tuple-element.85), channel_id=1, source_target_pairs={{0,12},{4,8},{8,4},{12,0},{16,28},{20,24},{24,20},{28,16},{1,13},{... | collective-permute-start | bytes 1572872 | tf_op jit(solution)/shard_map/ppermute | solution.py:383
  189.6 45.4 %collective-permute-start.19 = (bf16[64,2,16,128]{3,2,1,0:T(8,128)(2,1)}, bf16[64,2,16,128]{3,2,1,0:T(8,128)(2,1)S(1)}, u32[]{:S(2)}, u32[]{:S(2)}) collective-permute-start(bf16[64,2,16,128]{3,2,1,0:T(8,128)(2,1)} %get-tuple-element.86), channel_id=1, source_target_pairs={{0,16},{4,20},{8,24},{12,28},{16,0},{20,4},{24,8},{28,12},{1,17},{... | collective-permute-start | bytes 1572872 | tf_op jit(solution)/shard_map/ppermute | solution.py:383
  191.3 43.8 %collective-permute-start.20 = (bf16[64,2,16,128]{3,2,1,0:T(8,128)(2,1)}, bf16[64,2,16,128]{3,2,1,0:T(8,128)(2,1)}, u32[]{:S(2)}, u32[]{:S(2)}) collective-permute-start(bf16[64,2,16,128]{3,2,1,0:T(8,128)(2,1)} %get-tuple-element.87), channel_id=1, source_target_pairs={{0,20},{4,16},{8,28},{12,24},{16,4},{20,0},{24,12},{28,8},{1,21},{... | collective-permute-start | bytes 1572872 | tf_op jit(solution)/shard_map/ppermute | solution.py:383
  191.5 43.5 %copy-start.3 = (bf16[64,2,16,128]{3,2,1,0:T(8,128)(2,1)}, bf16[64,2,16,128]{3,2,1,0:T(8,128)(2,1)S(1)}, u32[]{:S(2)}) copy-start(bf16[64,2,16,128]{3,2,1,0:T(8,128)(2,1)S(1)} %collective-permute-done.16.refs_1_) | copy-start | bytes 1572868
  191.5 54.3 %collective-permute-start.14 = (bf16[64,2,16,128]{3,2,1,0:T(8,128)(2,1)}, bf16[64,2,16,128]{3,2,1,0:T(8,128)(2,1)S(1)}, u32[]{:S(2)}, u32[]{:S(2)}) collective-permute-start(bf16[64,2,16,128]{3,2,1,0:T(8,128)(2,1)} %get-tuple-element.80), channel_id=1, source_target_pairs={{0,24},{4,28},{8,16},{12,20},{16,8},{20,12},{24,0},{28,4},{1,25},{... | collective-permute-start | bytes 1572872 | tf_op jit(solution)/shard_map/ppermute | solution.py:383
  222.4 33.7 %collective-permute-start.15 = (bf16[64,2,16,128]{3,2,1,0:T(8,128)(2,1)}, bf16[64,2,16,128]{3,2,1,0:T(8,128)(2,1)S(1)}, u32[]{:S(2)}, u32[]{:S(2)}) collective-permute-start(bf16[64,2,16,128]{3,2,1,0:T(8,128)(2,1)} %get-tuple-element.81), channel_id=1, source_target_pairs={{0,28},{4,24},{8,20},{12,16},{16,12},{20,8},{24,4},{28,0},{1,29},{... | collective-permute-start | bytes 1572872 | tf_op jit(solution)/shard_map/ppermute | solution.py:383
  (11 other events, 77.8 us)
